TPU v7x, 32 devices: a whole 2x2x4 slice. The times are simulated.
32 devices in a mesh: groups: 2 (over y), tm: 4 (over z), row: 2 (over core), col: 2 (over x).
Axes of the slice: x: 2, y: 2, z: 4, core: 2. Of those that a mesh axis runs over, the one named last changes fastest.
Arguments:
- raw_traces: bfloat16 [64, 144, 10240], P('tm', None, ('groups', 'row', 'col')), parts along dimension 2, may hold values from -6 to 6
- window_offsets: int32 [128], P(('groups', 'tm')), parts along dimension 0, may hold values from 0 to 16, as said below
- dead_channels: int32 [256], P('groups'), parts along dimension 0, may hold values from 0 to 5119, as said below
Outputs:
- cross_spectra: bfloat16 [2, 4, 10240, 5120], P(None, None, ('groups', 'tm', 'row'), 'col'), parts along dimension 2
There are 2 independent parts, one for each index of `groups`. A program takes and returns all parts, laid end to end along the dimension named above; each array names one. Nothing has to cross between parts.
Inputs may be any that keep to these rules, and one draw needn't show every extreme that they name: `window_offsets`: some window starts at 0 and some at 16. `dead_channels`: distinct channel numbers; channels 0 and 5119 are always dead.
All inputs are finite; a program needn't handle non-finite values.
Results may differ from a plain program's by a relative error of at most 0.0071.
Values may be sent and summed in bfloat16 or wider, within the bound.
No kernel may reach another device: no remote copies, remote signals or barrier semaphores. Data moves between devices by JAX's collectives and lax.ppermute only.
A program may use at most 192 MiB of HBM per device.

v0:
```python
import math

import jax
import jax.numpy as jnp
from jax import lax
from jax.sharding import PartitionSpec as P

L = 128
F = 4


def make_table(length):
    sample = jnp.arange(length, dtype=jnp.int32)
    bins = (jnp.arange(F, dtype=jnp.int32) + 1) * (length // 16)
    phase = sample[:, None] * bins[None, :] % length
    angle = 2.0 * math.pi * phase.astype(jnp.float32) / length
    taper = 0.5 - 0.5 * jnp.cos(2.0 * math.pi * sample.astype(jnp.float32) / length)
    weight = taper / math.sqrt(length)
    real_part = weight[:, None] * jnp.cos(angle)
    imag_part = -weight[:, None] * jnp.sin(angle)
    return jnp.concatenate([real_part, imag_part], axis=1).astype(jnp.bfloat16)


def contract(left_part, right_part):
    windows_here = left_part.shape[1]
    left_split = left_part.reshape(2, F, windows_here, left_part.shape[2])
    right_split = right_part.reshape(2, F, windows_here, right_part.shape[2])
    real_out = jnp.einsum(
        "cfwi,cfwj->fij", left_split, right_split, preferred_element_type=jnp.float32
    )
    crossed = jnp.stack([right_split[1], -right_split[0]], axis=0)
    imag_out = jnp.einsum("cfwi,cfwj->fij", left_split, crossed, preferred_element_type=jnp.float32)
    return jnp.stack([real_out, imag_out], axis=0)


def body(raw_traces, window_offsets, dead_channels):
    local_windows, record_len, block_chans = raw_traces.shape
    table = make_table(L).astype(jnp.float32)
    sample_index = jnp.arange(record_len, dtype=jnp.int32)
    shifted = sample_index[None, :] - window_offsets[:, None]
    selector = (shifted[:, :, None] == jnp.arange(L, dtype=jnp.int32)[None, None, :]).astype(
        jnp.float32
    )
    tables = jnp.einsum("wmn,nk->wmk", selector, table, precision=lax.Precision.HIGHEST).astype(
        jnp.bfloat16
    )
    spectrum = jnp.einsum("wmc,wmk->kwc", raw_traces, tables, preferred_element_type=jnp.float32)
    power = jnp.mean(spectrum[:F] ** 2 + spectrum[F:] ** 2, axis=0)
    block_index = lax.axis_index("row") * lax.axis_size("col") + lax.axis_index("col")
    channel_ids = block_index * block_chans + jnp.arange(block_chans, dtype=jnp.int32)
    alive = 1.0 - jnp.any(dead_channels[:, None] == channel_ids[None, :], axis=0).astype(
        jnp.float32
    )
    factor = lax.rsqrt(jnp.maximum(power, 0.25)) * alive[None, :]
    whitened = (spectrum * factor[None, :, :]).astype(jnp.bfloat16)
    every_chan = lax.all_gather(whitened, ("row", "col"), axis=2, tiled=True)
    row_pair = lax.all_to_all(every_chan, "tm", split_axis=2, concat_axis=1, tiled=True)
    total_windows = row_pair.shape[1]
    inverse = 1.0 / total_windows
    col_width = every_chan.shape[2] // lax.axis_size("col")
    col_block = lax.dynamic_slice_in_dim(
        every_chan, lax.axis_index("col") * col_width, col_width, 2
    )
    pair_rows = row_pair.shape[2]
    half_rows = pair_rows // lax.axis_size("row")
    row_block = lax.dynamic_slice_in_dim(row_pair, lax.axis_index("row") * half_rows, half_rows, 2)
    total = contract(row_block, lax.all_gather(col_block, "tm", axis=1, tiled=True))
    return (total * inverse).astype(jnp.bfloat16)


def solution(mesh):
    in_specs = (P("tm", None, ("groups", "row", "col")), P(("groups", "tm")), P("groups"))
    out_specs = P(None, None, ("groups", "tm", "row"), "col")
    return jax.shard_map(body, mesh=mesh, in_specs=in_specs, out_specs=out_specs, check_vma=False)
```

profile of v0, /device:TPU:0, one launch (start us, length us, event | category | flops | bytes accessed | tf_op | source)
XLA Modules:
  0.0 196.3 jit_solution(5912474868628622765)
XLA Ops:
  6.5 0.0 all-gather.3.cloned.1.call-start
  6.6 0.8 compare_reduce_fusion
  7.4 0.7 iota_subtract_fusion
  8.2 0.1 multiply_convert_fusion.2
  8.3 0.7 fusion.6
  9.0 3.5 %convolution_bitcast_fusion.2 = f32[8,16,1280]{2,0,1:T(8,128)S(1)} fusion(bf16[16,144,8]{1,2,0:T(8,128)(2,1)S(1)} %fusion.6, bf16[16,144,1280]{2,1,0:T(8,128)(2,1)} %param.3), kind=kOutput, calls=%fused_computation.7 | convolution fusion | flops 47185920 | bytes 6590464 | tf_op jit(solution)/shard_map/wmc,wmk->kwc/dot_general | solution.py:47
  12.5 0.3 fusion.9
  12.9 0.8 multiply_convert_fusion
  13.7 0.0 all-gather.3.cloned.1.call-update
  13.7 0.0 all-gather.5.cloned.1.call-start
  13.7 21.0 %all-gather.3.cloned.1.call-done = bf16[8,16,5120]{2,0,1:T(8,128)(2,1)} async-done(((bf16[8,16,1280]{2,0,1:T(8,128)(2,1)}), bf16[8,16,5120]{2,0,1:T(8,128)(2,1)}) %all-gather.3.cloned.1.call-update) | async-done | bytes 1310736 | tf_op jit(solution)/shard_map/all_gather | solution.py:56
  34.7 0.0 copy-start
  34.7 2.1 %constant_dynamic-slice_fusion = bf16[8,16,2560]{2,0,1:T(8,128)(2,1)} fusion(bf16[8,16,5120]{2,0,1:T(8,128)(2,1)} %all-gather.3.cloned.1.call-done, s32[]{:T(128)S(6)} %select_n.17), kind=kLoop, calls=%fused_computation.36 | loop fusion | bytes 1310724 | tf_op jit(solution)/shard_map/dynamic_slice | solution.py:61
  36.8 0.0 all-gather.5.cloned.1.call-update
  36.8 0.0 copy-done
  36.8 8.3 %copy.27 = bf16[8,16,5120]{1,0,2:T(8,128)(2,1)} copy(bf16[8,16,5120]{2,0,1:T(8,128)(2,1)S(1)} %copy-done) | data formatting | bytes 2621440 | tf_op jit(solution)/shard_map/all_gather | solution.py:56
  45.1 13.5 %reshape.84 = bf16[4,2,81920]{2,1,0:T(2,128)(2,1)} reshape(bf16[5120,8,16]{2,1,0:T(8,128)(2,1)} %bitcast.27) | data formatting | bytes 2621440
  58.6 4.6 %all-to-all-start = ((bf16[4,2,81920]{2,1,0:T(2,128)(2,1)}), bf16[4,2,81920]{2,1,0:T(2,128)(2,1)S(1)}, u32[]{:S(2)}, u32[]{:S(2)}) async-start(bf16[4,2,81920]{2,1,0:T(2,128)(2,1)} %reshape.84), calls=%async_computation | async-start | bytes 2621440 | tf_op jit(solution)/shard_map/all_to_all | solution.py:57
  63.1 56.2 %all-to-all-done = bf16[4,2,81920]{2,1,0:T(2,128)(2,1)S(1)} async-done(((bf16[4,2,81920]{2,1,0:T(2,128)(2,1)}), bf16[4,2,81920]{2,1,0:T(2,128)(2,1)S(1)}, u32[]{:S(2)}, u32[]{:S(2)}) %all-to-all-start) | async-done | bytes 1310752 | tf_op jit(solution)/shard_map/all_to_all | solution.py:57
  119.3 9.2 %reshape.85 = bf16[5120,8,16]{2,1,0:T(8,128)(2,1)} reshape(bf16[4,2,81920]{2,1,0:T(2,128)(2,1)S(1)} %all-to-all-done) | data formatting | bytes 2621440
  128.5 11.1 %copy.33 = bf16[8,16,4,1280]{3,2,1,0:T(4,128)(2,1)S(1)} copy(bf16[8,16,4,1280]{1,0,3,2:T(8,128)(2,1)} %bitcast.28) | data formatting | bytes 2621440 | tf_op jit(solution)/shard_map/all_to_all | solution.py:57
  139.6 0.2 copy.29
  139.8 0.1 constant_dynamic-slice_fusion.1
  139.8 0.0 all-gather.5.cloned.1.call-done
  139.9 2.5 %copy.30 = bf16[8,64,2560]{2,1,0:T(8,128)(2,1)S(1)} copy(bf16[8,64,2560]{2,0,1:T(8,128)(2,1)} %all-gather.5.cloned.1.call-done) | data formatting | bytes 5242880 | tf_op jit(solution)/shard_map/all_gather | solution.py:67
  142.4 0.2 slice_bitcast_fusion
  142.6 10.6 %convolution_bitcast_fusion.1 = f32[1,4,640,2560]{3,2,1,0:T(8,128)} fusion(bf16[2,4,64,640]{3,2,1,0:T(8,128)(2,1)S(1)} %bitcast.30, bf16[2,4,64,2560]{3,2,1,0:T(8,128)(2,1)S(1)} %bitcast.29), kind=kOutput, calls=%fused_computation.3 | convolution fusion | flops 1677721600 | bytes 29491200 | tf_op jit(solution)/shard_map/cfwi,cfwj->fij/dot_general | solution.py:28
  153.1 10.5 %convolution_bitcast_fusion = f32[1,4,640,2560]{3,2,1,0:T(8,128)} fusion(bf16[2,4,64,640]{3,2,1,0:T(8,128)(2,1)S(1)} %bitcast.31, bf16[1,4,64,2560]{3,2,1,0:T(8,128)(2,1)S(1)} %get-tuple-element.6, bf16[1,4,64,2560]{3,2,1,0:T(8,128)(2,1)S(1)} %get-tuple-element.5), kind=kOutput, calls=%fused_computation.2 | convolution fusion | flops 1679032320 | bytes 29491200 | tf_op jit(solution)/shard_map/cfwi,cfwj->fij/dot_general | solution.py:32
  163.7 25.8 %fusion = bf16[2,4,640,2560]{3,2,1,0:T(8,128)(2,1)} fusion(f32[1,4,640,2560]{3,2,1,0:T(8,128)} %convolution_bitcast_fusion, f32[1,4,640,2560]{3,2,1,0:T(8,128)} %convolution_bitcast_fusion.1), kind=kLoop, calls=%fused_computation.1 | loop fusion | flops 39321600 | bytes 78643200 | tf_op jit(solution)/shard_map/convert_element_type | solution.py:68
  (5 shorter events, 0.1 us)
Async XLA Ops:
  6.5 28.2 %all-gather.3.cloned.1.call-start = ((), (), s32[]{:S(2)}) async-start(), calls=%async_computation.1 | async-start | bytes 1638400 | tf_op jit(solution)/shard_map/all_gather | solution.py:56
  13.7 126.2 %all-gather.5.cloned.1.call-start = ((), (), s32[]{:S(2)}) async-start(), calls=%async_computation.2 | async-start | bytes 3276800 | tf_op jit(solution)/shard_map/all_gather | solution.py:67
  34.7 2.1 %copy-start = (bf16[8,16,5120]{2,0,1:T(8,128)(2,1)S(1)}, bf16[8,16,5120]{2,0,1:T(8,128)(2,1)}, u32[]{:S(2)}) copy-start(bf16[8,16,5120]{2,0,1:T(8,128)(2,1)} %all-gather.3.cloned.1.call-done) | copy-start | bytes 3932164
  58.6 60.7 %all-to-all-start = ((bf16[4,2,81920]{2,1,0:T(2,128)(2,1)}), bf16[4,2,81920]{2,1,0:T(2,128)(2,1)S(1)}, u32[]{:S(2)}, u32[]{:S(2)}) async-start(bf16[4,2,81920]{2,1,0:T(2,128)(2,1)} %reshape.84), calls=%async_computation | async-start | bytes 2621440 | tf_op jit(solution)/shard_map/all_to_all | solution.py:57
Sparse Core Ops, SparseCore 0:
  13.8 20.8 all-gather.2
  37.0 80.8 all-gather.4
where the time goes:
time: 197 us; the launch traced here: 196 us
  waiting for transfers between devices  77.2 us (39%)
  local copies, waits for them, and re-layouts  46.8 us (24%)
  other arithmetic  28.8 us (15%)
  matrix products  25.3 us (13%)
  between operations  13.5 us (7%)
  starting transfers between devices  4.6 us (2%)
    all_to_all x1, waiting for transfers between devices, body(): lax.all_to_all(every_chan, 'tm', split_axis=2, concat_axis=1, tiled=True)  56.2 us
    convert_element_type x1, other arithmetic, body(): return (total * inverse).astype(jnp.bfloat16)  25.8 us
    unnamed x4, local copies, waits for them, and re-layouts  22.7 us
    all_gather x1, waiting for transfers between devices, body(): every_chan = lax.all_gather(whitened, ('row', 'col'), axis=2, tiled=True)  21 us
    all_to_all x2, local copies, waits for them, and re-layouts, body(): lax.all_to_all(every_chan, 'tm', split_axis=2, concat_axis=1, tiled=True)  11.2 us
    dot_general x1, matrix products, contract(): jnp.einsum('cfwi,cfwj->fij', left_split, right_split, preferred_element_t...  10.6 us
    dot_general x1, matrix products, contract(): jnp.einsum('cfwi,cfwj->fij', left_split, crossed, preferred_element_type=...  10.5 us
    all_gather x1, local copies, waits for them, and re-layouts, body(): every_chan = lax.all_gather(whitened, ('row', 'col'), axis=2, tiled=True)  8.25 us
  transfers between devices with their start and end apart: 3, of which 2 were waited for; matrix products, arithmetic and copies ran while one was open for 22% of the time, Pallas kernels for 0%

commit v1 on v0

v1 whole, which is shorter than its diff:
```python
import functools
import math

import jax
import jax.numpy as jnp
import numpy as np
from jax import lax
from jax.experimental import pallas as pl
from jax.experimental.pallas import tpu as pltpu
from jax.sharding import PartitionSpec as P

L = 128
F = 4
GROUPS = 4
VMEM_LIMIT = 48 * 1024 * 1024


def make_table(length):
    sample = np.arange(length)
    bins = (np.arange(F) + 1) * (length // 16)
    angle = 2.0 * math.pi * (sample[:, None] * bins[None, :] % length) / length
    taper = 0.5 - 0.5 * np.cos(2.0 * math.pi * sample / length)
    weight = taper / math.sqrt(length)
    real_part = weight[:, None] * np.cos(angle)
    imag_part = -weight[:, None] * np.sin(angle)
    table = np.concatenate([real_part, imag_part], axis=1).astype(np.float32)
    return table.astype(jnp.bfloat16)


def spectra_kernel(offsets, table_ref, dead_ref, raw_ref, *rest):
    outs, (shifted, dead_rows, spectrum) = rest[:-3], rest[-3:]
    windows, record_len, width = raw_ref.shape
    step = pl.program_id(0)

    @pl.when(step == 0)
    def _():
        for w in range(windows):
            shifted[w] = pltpu.roll(table_ref[...], offsets[w], 1)
        listed = jnp.broadcast_to(dead_ref[...], (128, dead_ref.shape[1]))
        dead_rows[...] = listed.T

    for w in range(windows):
        lhs = shifted[w][:, :record_len].astype(jnp.bfloat16)
        found = jnp.dot(lhs, raw_ref[w], preferred_element_type=jnp.float32)
        spectrum[:, w, :] = found[: 2 * F]

    power = spectrum[0] * spectrum[0] + spectrum[F] * spectrum[F]
    for f in range(1, F):
        power += spectrum[f] * spectrum[f] + spectrum[F + f] * spectrum[F + f]
    power *= 1.0 / F
    block = lax.axis_index("row") * lax.axis_size("col") + lax.axis_index("col")
    first = (block * pl.num_programs(0) + step) * width
    alive = []
    for part in range(width // 128):
        ids = first + part * 128 + lax.broadcasted_iota(jnp.int32, (1, 128), 1)
        hit = (dead_rows[...] == ids).astype(jnp.float32)
        alive.append(1.0 - jnp.max(hit, axis=0, keepdims=True))
    factor = lax.rsqrt(jnp.maximum(power, 0.25)) * jnp.concatenate(alive, axis=1)
    per = F // len(outs)
    for f in range(F):
        out = outs[f // per]
        for part in range(2):
            white = (spectrum[part * F + f] * factor).astype(jnp.bfloat16)
            out[f % per, part * windows : (part + 1) * windows, :] = white


def spectra(raw_traces, window_offsets, dead_channels, groups):
    windows, record_len, chans = raw_traces.shape
    width = 256 if chans % 256 == 0 else 128
    table = np.zeros((16, 256), np.float32)
    table[: 2 * F, :L] = make_table(L).astype(np.float32).T
    dead = dead_channels.reshape(1, -1)
    per = F // groups
    shape = jax.ShapeDtypeStruct((per, 2 * windows, chans), jnp.bfloat16)
    return pl.pallas_call(
        spectra_kernel,
        grid_spec=pltpu.PrefetchScalarGridSpec(
            num_scalar_prefetch=1,
            grid=(chans // width,),
            in_specs=[
                pl.BlockSpec((16, 256), lambda j, o: (0, 0)),
                pl.BlockSpec(dead.shape, lambda j, o: (0, 0)),
                pl.BlockSpec((windows, record_len, width), lambda j, o: (0, 0, j)),
            ],
            out_specs=[
                pl.BlockSpec((per, 2 * windows, width), lambda j, o: (0, 0, j))
            ]
            * groups,
            scratch_shapes=[
                pltpu.VMEM((windows, 16, 256), jnp.float32),
                pltpu.VMEM((dead.shape[1], 128), jnp.int32),
                pltpu.VMEM((2 * F, windows, width), jnp.float32),
            ],
        ),
        out_shape=[shape] * groups,
        compiler_params=pltpu.CompilerParams(vmem_limit_bytes=VMEM_LIMIT),
        cost_estimate=pl.CostEstimate(
            flops=2 * 16 * windows * record_len * chans,
            bytes_accessed=2 * windows * record_len * chans,
            transcendentals=0,
        ),
        name="spectra",
    )(window_offsets, jnp.asarray(table), dead, raw_traces)


def products_kernel(scale, pieces, spots, *rest):
    mine, (theirs, sent_rows) = rest[:pieces], rest[pieces : pieces + 2]
    out, left = rest[-2:]
    half, tile = pl.program_id(1), pl.program_id(2)
    depth, rows = sent_rows.shape[1:]
    piece = depth // pieces
    width = out.shape[3]

    @pl.when((half == 0) & (tile == 0))
    def _():
        for p in range(pieces):
            real = sent_rows[0, p * piece : p * piece + piece // 2, :].astype(jnp.float32)
            imag = sent_rows[0, p * piece + piece // 2 : (p + 1) * piece, :].astype(jnp.float32)
            at = slice(p * piece, (p + 1) * piece)
            same = jnp.concatenate([real, imag], axis=0)
            crossed = jnp.concatenate([-imag, real], axis=0)
            left[:rows, at] = same.T.astype(jnp.bfloat16)
            left[rows:, at] = crossed.T.astype(jnp.bfloat16)

    columns = pl.ds(pl.multiple_of(tile * width, 128), width)

    def multiply(right):
        found = jnp.dot(left[...], right, preferred_element_type=jnp.float32) * scale
        out[0, 0] = found[:rows].astype(jnp.bfloat16)
        out[1, 0] = found[rows:].astype(jnp.bfloat16)

    @pl.when(half == 0)
    def _():
        multiply(jnp.concatenate([ref[0, :, columns] for ref in mine], axis=0))

    @pl.when(half == 1)
    def _():
        multiply(theirs[0, :, columns])


def products(spots, mine, theirs, rows_in, start, total, target, scale):
    per, depth, chans = theirs.shape
    rows = rows_in.shape[2]
    width = 256
    tiles = chans // width
    piece = mine[0].shape[1]

    def out_map(f, h, j, s):
        return (0, start + f, 0, (h + s[0] - 2 * h * s[0]) * tiles + j)

    in_specs = [pl.BlockSpec((1, piece, chans), lambda f, h, j, s: (f, 0, 0))] * len(mine)
    in_specs += [
        pl.BlockSpec((1, depth, chans), lambda f, h, j, s: (f, 0, 0)),
        pl.BlockSpec((1, depth, rows), lambda f, h, j, s: (f, 0, 0)),
    ]
    args = [spots, *mine, theirs, rows_in]
    aliases = {}
    if target is not None:
        in_specs.append(pl.BlockSpec(memory_space=pl.ANY))
        aliases = {len(args): 0}
        args.append(target)
    return pl.pallas_call(
        functools.partial(products_kernel, scale, len(mine)),
        grid_spec=pltpu.PrefetchScalarGridSpec(
            num_scalar_prefetch=1,
            grid=(per, 2, tiles),
            in_specs=in_specs,
            out_specs=pl.BlockSpec((2, 1, rows, width), out_map),
            scratch_shapes=[pltpu.VMEM((2 * rows, depth), jnp.bfloat16)],
        ),
        out_shape=jax.ShapeDtypeStruct((2, total, rows, 2 * chans), jnp.bfloat16),
        input_output_aliases=aliases,
        compiler_params=pltpu.CompilerParams(vmem_limit_bytes=VMEM_LIMIT),
        cost_estimate=pl.CostEstimate(
            flops=8 * per * rows * depth * chans,
            bytes_accessed=8 * per * rows * chans,
            transcendentals=0,
        ),
        name="products",
    )(*args)


def swap_body(raw_traces, window_offsets, dead_channels):
    nz = lax.axis_size("tm")
    windows = raw_traces.shape[0]
    t, r, c = lax.axis_index("tm"), lax.axis_index("row"), lax.axis_index("col")
    groups = spectra(raw_traces, window_offsets, dead_channels, GROUPS)
    scale = 1.0 / (nz * windows)

    def place(z, row, col):
        return (z * 2 + row) * 2 + col

    def across(apart):
        every = [(z, a, b) for z in range(nz) for a in range(2) for b in range(2)]
        return [(place(z, a, b), place(z ^ apart, b, a)) for z, a, b in every]

    spots = r.reshape(1).astype(jnp.int32)
    half = raw_traces.shape[2] // 2
    result = None
    for g, block in enumerate(groups):
        mine = [lax.ppermute(block, ("tm", "row", "col"), across(d)) for d in range(nz)]
        whole = jnp.concatenate(mine, axis=1)
        theirs = lax.ppermute(whole, "row", [(0, 1), (1, 0)])
        wanted = jnp.where(r == t % 2, whole, theirs)
        held = lax.dynamic_slice_in_dim(wanted, r * half, half, 2)
        passed = lax.ppermute(held, "col", [(0, 1), (1, 0)])
        rows_in = jnp.where(c == t // 2, held, passed)
        result = products(
            spots, mine, theirs, rows_in, g * block.shape[0], F, result, scale
        )
    return result


def contract(left_part, right_part):
    windows_here = left_part.shape[1]
    left_split = left_part.reshape(2, F, windows_here, left_part.shape[2])
    right_split = right_part.reshape(2, F, windows_here, right_part.shape[2])
    real_out = jnp.einsum(
        "cfwi,cfwj->fij", left_split, right_split, preferred_element_type=jnp.float32
    )
    crossed = jnp.stack([right_split[1], -right_split[0]], axis=0)
    imag_out = jnp.einsum("cfwi,cfwj->fij", left_split, crossed, preferred_element_type=jnp.float32)
    return jnp.stack([real_out, imag_out], axis=0)


def gather_body(raw_traces, window_offsets, dead_channels):
    windows, _, chans = raw_traces.shape
    (whole,) = spectra(raw_traces, window_offsets, dead_channels, 1)
    whitened = whole.reshape(F, 2, windows, chans).transpose(1, 0, 2, 3)
    whitened = whitened.reshape(2 * F, windows, chans)
    every_chan = lax.all_gather(whitened, ("row", "col"), axis=2, tiled=True)
    row_pair = lax.all_to_all(every_chan, "tm", split_axis=2, concat_axis=1, tiled=True)
    inverse = 1.0 / row_pair.shape[1]
    col_width = every_chan.shape[2] // lax.axis_size("col")
    col_block = lax.dynamic_slice_in_dim(
        every_chan, lax.axis_index("col") * col_width, col_width, 2
    )
    half_rows = row_pair.shape[2] // lax.axis_size("row")
    row_block = lax.dynamic_slice_in_dim(row_pair, lax.axis_index("row") * half_rows, half_rows, 2)
    total = contract(row_block, lax.all_gather(col_block, "tm", axis=1, tiled=True))
    return (total * inverse).astype(jnp.bfloat16)


def solution(mesh):
    sizes = mesh.shape
    square = sizes["tm"] == 4 and sizes["row"] == 2 and sizes["col"] == 2
    in_specs = (P("tm", None, ("groups", "row", "col")), P(("groups", "tm")), P("groups"))
    out_specs = P(None, None, ("groups", "tm", "row"), "col")
    return jax.shard_map(
        swap_body if square else gather_body,
        mesh=mesh,
        in_specs=in_specs,
        out_specs=out_specs,
        check_vma=False,
    )
```

time: 197 us -> 101 us (0.51)
  waiting for transfers between devices: 77.2 us -> 13.3 us
  starting transfers between devices: 4.6 us -> 50.9 us
  local copies, waits for them, and re-layouts: 46.8 us -> 2.13 us
  Pallas kernels: 0 us -> 33.9 us
  other arithmetic: 28.8 us -> 0.26 us
  matrix products: 25.3 us -> 0 us
  between operations: 13.5 us -> 0.24 us
    all_to_all x1 -> x0, waiting for transfers between devices: 56.2 us -> none  [body(): lax.all_to_all(every_chan, 'tm', split_axis=2, concat_axis=1, tiled=True)]
    ppermute x0 -> x24, starting transfers between devices: none -> 50.9 us  [the longest x4 25.2 us: swap_body(): theirs = lax.ppermute(whole, 'row', [(0, 1), (1, 0)])]
    pallas_call x0 -> x5, Pallas kernels: none -> 33.9 us  [the longest x4 28.3 us: products(): pl.pallas_call(functools.partial(products_kernel, scale, len(mine)), grid...]
    convert_element_type x2 -> x0, other arithmetic: 26.6 us -> none  [the longest x1 25.8 us: body(): return (total * inverse).astype(jnp.bfloat16)]
    dot_general x4 -> x0, matrix products: 25.3 us -> none  [the longest x1 10.6 us: contract(): jnp.einsum('cfwi,cfwj->fij', left_split, right_split, preferred_element_t...]
    all_gather x2 -> x0, waiting for transfers between devices: 21 us -> none  [the longest x1 21 us: body(): every_chan = lax.all_gather(whitened, ('row', 'col'), axis=2, tiled=True)]
    unnamed x4 -> x18, local copies, waits for them, and re-layouts: 22.7 us -> 2.11 us
    ppermute x0 -> x24, waiting for transfers between devices: none -> 13.3 us  [the longest x4 12.2 us: swap_body(): passed = lax.ppermute(held, 'col', [(0, 1), (1, 0)])]
  transfers between devices with their start and end apart: 3 -> 24, of which waited for: 2 -> 5; matrix products, arithmetic and copies ran while one was open for 22% -> 0% of each run, Pallas kernels for 0% -> 0%
where the time goes in v1:
time: 101 us
  starting transfers between devices  50.9 us (50%)
  Pallas kernels  33.9 us (34%)
  waiting for transfers between devices  13.3 us (13%)
  local copies, waits for them, and re-layouts  2.13 us (2%)
    pallas_call x4, Pallas kernels, products(): pl.pallas_call(functools.partial(products_kernel, scale, len(mine)), grid...  28.3 us
    ppermute x4, starting transfers between devices, swap_body(): theirs = lax.ppermute(whole, 'row', [(0, 1), (1, 0)])  25.2 us
    ppermute x16, starting transfers between devices, swap_body(): lax.ppermute(block, ('tm', 'row', 'col'), across(d))  21.4 us
    ppermute x4, waiting for transfers between devices, swap_body(): passed = lax.ppermute(held, 'col', [(0, 1), (1, 0)])  12.2 us
    pallas_call x1, Pallas kernels, spectra(): pl.pallas_call(spectra_kernel, grid_spec=pltpu.PrefetchScalarGridSpec(num...  5.58 us
    ppermute x4, starting transfers between devices, swap_body(): passed = lax.ppermute(held, 'col', [(0, 1), (1, 0)])  4.31 us
    unnamed x18, local copies, waits for them, and re-layouts  2.11 us
  transfers between devices with their start and end apart: 24, of which 5 were waited for; matrix products, arithmetic and copies ran while one was open for 0% of the time, Pallas kernels for 0%

profile of v1, /device:TPU:0, one launch (start us, length us, event | category | flops | bytes accessed | tf_op | source)
XLA Modules:
  0.0 100.8 jit_solution(2047276171219353743)
XLA Ops:
  0.0 0.7 copy-done
  0.7 0.7 copy-done.1
  1.4 0.7 copy-done.2
  2.0 5.6 %spectra.1 = (bf16[1,32,1280]{2,1,0:T(8,128)(2,1)S(1)}, bf16[1,32,1280]{2,1,0:T(8,128)(2,1)S(1)}, bf16[1,32,1280]{2,1,0:T(8,128)(2,1)S(1)}, bf16[1,32,1280]{2,1,0:T(8,128)(2,1)S(1)}) custom-call(s32[16]{0:T(128)S(1)} %copy-done.1, f32[16,256]{1,0:T(8,128)S(1)} %copy-done, s32[1,128]{1,0:T(1,128)S(1)} %bitcast.2, bf16[16,144,1280]{2,1,0:T(8,128)(2,1)} %raw_ref.1), custom_call_target="tpu_custom_call" | custom-call | flops 94371840 | bytes 5898240 | tf_op jit(solution)/shard_map/spectra/pallas_call | solution.py:75
  7.6 0.7 collective-permute-start.18
  8.3 3.1 %collective-permute-start.19 = (bf16[1,32,1280]{2,1,0:T(8,128)(2,1)S(1)}, bf16[1,32,1280]{2,1,0:T(8,128)(2,1)S(1)}, u32[]{:S(2)}, u32[]{:S(2)}) collective-permute-start(bf16[1,32,1280]{2,1,0:T(8,128)(2,1)S(1)} %get-tuple-element.12), channel_id=1, source_target_pairs={{0,4},{1,6},{2,5},{3,7},{4,0},{5,2},{6,1},{7,3},{8,12},{9,14},{10,... | collective-permute-start | bytes 245768 | tf_op jit(solution)/shard_map/ppermute | solution.py:201
  11.4 2.6 %collective-permute-start.20 = (bf16[1,32,1280]{2,1,0:T(8,128)(2,1)S(1)}, bf16[1,32,1280]{2,1,0:T(8,128)(2,1)S(1)}, u32[]{:S(2)}, u32[]{:S(2)}) collective-permute-start(bf16[1,32,1280]{2,1,0:T(8,128)(2,1)S(1)} %get-tuple-element.12), channel_id=1, source_target_pairs={{0,8},{1,10},{2,9},{3,11},{4,12},{5,14},{6,13},{7,15},{8,0},{9,2},... | collective-permute-start | bytes 245768 | tf_op jit(solution)/shard_map/ppermute | solution.py:201
  14.0 0.0 collective-permute-start.21
  14.0 0.7 collective-permute-start.12
  14.7 0.0 collective-permute-done.18.rest_0_
  14.7 1.0 collective-permute-start.13
  15.6 0.0 collective-permute-done.12.rest_0_
  15.6 0.7 collective-permute-start.6
  16.3 0.0 collective-permute-done.6.rest_0_
  16.3 0.7 collective-permute-start
  17.0 3.6 %collective-permute-start.14 = (bf16[1,32,1280]{2,1,0:T(8,128)(2,1)S(1)}, bf16[1,32,1280]{2,1,0:T(8,128)(2,1)S(1)}, u32[]{:S(2)}, u32[]{:S(2)}) collective-permute-start(bf16[1,32,1280]{2,1,0:T(8,128)(2,1)S(1)} %get-tuple-element.11), channel_id=1, source_target_pairs={{0,8},{1,10},{2,9},{3,11},{4,12},{5,14},{6,13},{7,15},{8,0},{9,2},... | collective-permute-start | bytes 245768 | tf_op jit(solution)/shard_map/ppermute | solution.py:201
  20.6 0.0 collective-permute-done.19.rest_1_
  20.6 0.1 collective-permute-start.15
  20.7 0.6 collective-permute-start.7
  21.4 3.9 %collective-permute-start.8 = (bf16[1,32,1280]{2,1,0:T(8,128)(2,1)S(1)}, bf16[1,32,1280]{2,1,0:T(8,128)(2,1)S(1)}, u32[]{:S(2)}, u32[]{:S(2)}) collective-permute-start(bf16[1,32,1280]{2,1,0:T(8,128)(2,1)S(1)} %get-tuple-element.10), channel_id=1, source_target_pairs={{0,8},{1,10},{2,9},{3,11},{4,12},{5,14},{6,13},{7,15},{8,0},{9,2},... | collective-permute-start | bytes 245768 | tf_op jit(solution)/shard_map/ppermute | solution.py:201
  25.2 0.0 collective-permute-done.13.rest_1_
  25.2 0.1 collective-permute-start.9
  25.3 0.6 collective-permute-start.1
  26.0 1.1 %collective-permute-done.15.rest_3_ = bf16[1,32,1280]{2,1,0:T(8,128)(2,1)S(1)} collective-permute-done((bf16[1,32,1280]{2,1,0:T(8,128)(2,1)S(1)}, bf16[1,32,1280]{2,1,0:T(8,128)(2,1)S(1)}, u32[]{:S(2)}, u32[]{:S(2)}) %collective-permute-start.15) | collective-permute-done | bytes 81952 | tf_op jit(solution)/shard_map/ppermute | solution.py:201
  27.1 2.8 %collective-permute-start.2 = (bf16[1,32,1280]{2,1,0:T(8,128)(2,1)S(1)}, bf16[1,32,1280]{2,1,0:T(8,128)(2,1)S(1)}, u32[]{:S(2)}, u32[]{:S(2)}) collective-permute-start(bf16[1,32,1280]{2,1,0:T(8,128)(2,1)S(1)} %get-tuple-element.9), channel_id=1, source_target_pairs={{0,8},{1,10},{2,9},{3,11},{4,12},{5,14},{6,13},{7,15},{8,0},{9,2},... | collective-permute-start | bytes 245768 | tf_op jit(solution)/shard_map/ppermute | solution.py:201
  29.9 0.5 collective-permute-start.3
  30.4 0.0 collective-permute-done.8.rest_2_
  30.4 20.0 %collective-permute-start.22 = (bf16[1,128,1280]{2,1,0:T(8,128)(2,1)S(1)}, bf16[1,128,1280]{2,1,0:T(8,128)(2,1)S(1)}, u32[]{:S(2)}, u32[]{:S(2)}) collective-permute-start(bf16[1,128,1280]{2,1,0:T(8,128)(2,1)S(1)} %constant_dynamic-update-slice_fusion.12), channel_id=1, source_target_pairs={{0,2},{2,0},{1,3},{3,1},{4,6},{6,4},{5,7},{7,5},{8,10},{10,8},{9,1... | collective-permute-start | bytes 983048 | tf_op jit(solution)/shard_map/ppermute | solution.py:203
  50.4 0.1 collective-permute-start.16
  50.5 0.0 collective-permute-done.1.rest_1_
  50.5 0.5 collective-permute-start.10
  51.1 0.0 collective-permute-done.2.rest_2_
  51.1 0.0 collective-permute-done.3.rest_3_
  51.1 4.5 %collective-permute-start.4 = (bf16[1,128,1280]{2,1,0:T(8,128)(2,1)S(1)}, bf16[1,128,1280]{2,1,0:T(8,128)(2,1)S(1)}, u32[]{:S(2)}, u32[]{:S(2)}) collective-permute-start(bf16[1,128,1280]{2,1,0:T(8,128)(2,1)S(1)} %constant_dynamic-update-slice_fusion), channel_id=1, source_target_pairs={{0,2},{2,0},{1,3},{3,1},{4,6},{6,4},{5,7},{7,5},{8,10},{10,8},{9,1... | collective-permute-start | bytes 983048 | tf_op jit(solution)/shard_map/ppermute | solution.py:203
  55.6 0.0 collective-permute-done.22.rest_4_
  55.7 0.3 collective-permute-start.23
  56.0 1.9 %collective-permute-start.17 = (bf16[1,128,640]{2,1,0:T(8,128)(2,1)S(1)}, bf16[1,128,640]{2,1,0:T(8,128)(2,1)S(1)}, u32[]{:S(2)}, u32[]{:S(2)}) collective-permute-start(bf16[1,128,640]{2,1,0:T(8,128)(2,1)S(1)} %dynamic-slice_select_fusion.1), channel_id=1, source_target_pairs={{0,1},{1,0},{2,3},{3,2},{4,5},{5,4},{6,7},{7,6},{8,9},{9,8},{10,11... | collective-permute-start | bytes 491528 | tf_op jit(solution)/shard_map/ppermute | solution.py:206
  57.9 0.0 collective-permute-done.10.rest_4_
  58.0 0.3 collective-permute-start.11
  58.3 1.9 %collective-permute-start.5 = (bf16[1,128,640]{2,1,0:T(8,128)(2,1)S(1)}, bf16[1,128,640]{2,1,0:T(8,128)(2,1)S(1)}, u32[]{:S(2)}, u32[]{:S(2)}) collective-permute-start(bf16[1,128,640]{2,1,0:T(8,128)(2,1)S(1)} %dynamic-slice_select_fusion.3), channel_id=1, source_target_pairs={{0,1},{1,0},{2,3},{3,2},{4,5},{5,4},{6,7},{7,6},{8,9},{9,8},{10,11... | collective-permute-start | bytes 491528 | tf_op jit(solution)/shard_map/ppermute | solution.py:206
  60.2 2.7 %collective-permute-done.23 = bf16[1,128,640]{2,1,0:T(8,128)(2,1)S(1)} collective-permute-done((bf16[1,128,640]{2,1,0:T(8,128)(2,1)S(1)}, bf16[1,128,640]{2,1,0:T(8,128)(2,1)S(1)}, u32[]{:S(2)}, u32[]{:S(2)}) %collective-permute-start.23) | collective-permute-done | bytes 163872 | tf_op jit(solution)/shard_map/ppermute | solution.py:206
  62.8 3.5 %collective-permute-done.17 = bf16[1,128,640]{2,1,0:T(8,128)(2,1)S(1)} collective-permute-done((bf16[1,128,640]{2,1,0:T(8,128)(2,1)S(1)}, bf16[1,128,640]{2,1,0:T(8,128)(2,1)S(1)}, u32[]{:S(2)}, u32[]{:S(2)}) %collective-permute-start.17) | collective-permute-done | bytes 163872 | tf_op jit(solution)/shard_map/ppermute | solution.py:206
  66.4 3.5 %collective-permute-done.11 = bf16[1,128,640]{2,1,0:T(8,128)(2,1)S(1)} collective-permute-done((bf16[1,128,640]{2,1,0:T(8,128)(2,1)S(1)}, bf16[1,128,640]{2,1,0:T(8,128)(2,1)S(1)}, u32[]{:S(2)}, u32[]{:S(2)}) %collective-permute-start.11) | collective-permute-done | bytes 163872 | tf_op jit(solution)/shard_map/ppermute | solution.py:206
  69.9 2.6 %collective-permute-done.5 = bf16[1,128,640]{2,1,0:T(8,128)(2,1)S(1)} collective-permute-done((bf16[1,128,640]{2,1,0:T(8,128)(2,1)S(1)}, bf16[1,128,640]{2,1,0:T(8,128)(2,1)S(1)}, u32[]{:S(2)}, u32[]{:S(2)}) %collective-permute-start.5) | collective-permute-done | bytes 163872 | tf_op jit(solution)/shard_map/ppermute | solution.py:206
  72.5 7.1 %products.4.rest_6_ = bf16[2,4,640,2560]{3,2,1,0:T(8,128)(2,1)} custom-call(s32[1]{0:T(128)} %bitcast.spots, bf16[1,32,1280]{2,1,0:T(8,128)(2,1)S(1)} %collective-permute-done.18.rest_0_, bf16[1,32,1280]{2,1,0:T(8,128)(2,1)S(1)} %collective-permute-done.19.rest_1_, bf16[1,32,1280]{2,1,0:T(8,128)(2,1)S(1)} %collective-permute-done.20.rest_2_, ...), custom_call_target="tpu_custom_call" | custom-call | flops 838860800 | bytes 6553600 | tf_op jit(solution)/shard_map/products/pallas_call | solution.py:162
  79.6 7.1 %products.5.rest_6_ = bf16[2,4,640,2560]{3,2,1,0:T(8,128)(2,1)} custom-call(s32[1]{0:T(128)} %bitcast.spots, bf16[1,32,1280]{2,1,0:T(8,128)(2,1)S(1)} %collective-permute-done.12.rest_0_, bf16[1,32,1280]{2,1,0:T(8,128)(2,1)S(1)} %collective-permute-done.13.rest_1_, ...), custom_call_target="tpu_custom_call", output_to_operand_aliasing={{}: (7, {})} | custom-call | flops 838860800 | bytes 6553600 | tf_op jit(solution)/shard_map/products/pallas_call | solution.py:162
  86.6 7.1 %products.6.rest_6_ = bf16[2,4,640,2560]{3,2,1,0:T(8,128)(2,1)} custom-call(s32[1]{0:T(128)} %bitcast.spots, bf16[1,32,1280]{2,1,0:T(8,128)(2,1)S(1)} %collective-permute-done.6.rest_0_, bf16[1,32,1280]{2,1,0:T(8,128)(2,1)S(1)} %collective-permute-done.7.rest_1_, ...), custom_call_target="tpu_custom_call", output_to_operand_aliasing={{}: (7, {})} | custom-call | flops 838860800 | bytes 6553600 | tf_op jit(solution)/shard_map/products/pallas_call | solution.py:162
  93.7 7.1 %products.7 = bf16[2,4,640,2560]{3,2,1,0:T(8,128)(2,1)} custom-call(s32[1]{0:T(128)} %bitcast.spots, bf16[1,32,1280]{2,1,0:T(8,128)(2,1)S(1)} %collective-permute-done.rest_0_, bf16[1,32,1280]{2,1,0:T(8,128)(2,1)S(1)} %collective-permute-done.1.rest_1_, bf16[1,32,1280]{2,1,0:T(8,128)(2,1)S(1)} %collective-permute-done.2.rest_2_, ...), custom_call_target="tpu_custom_call", output_to_operand_aliasing={{}: (7, {})} | custom-call | flops 838860800 | bytes 6553600 | tf_op jit(solution)/shard_map/products/pallas_call | solution.py:162
  (35 shorter events, 0.4 us)
Async XLA Ops:
  0.0 0.7 copy-start
  0.7 0.7 copy-start.1
  1.4 0.7 copy-start.2
  7.6 7.0 %collective-permute-start.18 = (bf16[1,32,1280]{2,1,0:T(8,128)(2,1)S(1)}, bf16[1,32,1280]{2,1,0:T(8,128)(2,1)S(1)}, u32[]{:S(2)}, u32[]{:S(2)}) collective-permute-start(bf16[1,32,1280]{2,1,0:T(8,128)(2,1)S(1)} %get-tuple-element.12), channel_id=1, source_target_pairs={{0,0},{1,2},{2,1},{3,3},{4,4},{5,6},{6,5},{7,7},{8,8},{9,10},{10,9... | collective-permute-start | bytes 245768 | tf_op jit(solution)/shard_map/ppermute | solution.py:201
  8.3 12.3 %collective-permute-start.19 = (bf16[1,32,1280]{2,1,0:T(8,128)(2,1)S(1)}, bf16[1,32,1280]{2,1,0:T(8,128)(2,1)S(1)}, u32[]{:S(2)}, u32[]{:S(2)}) collective-permute-start(bf16[1,32,1280]{2,1,0:T(8,128)(2,1)S(1)} %get-tuple-element.12), channel_id=1, source_target_pairs={{0,4},{1,6},{2,5},{3,7},{4,0},{5,2},{6,1},{7,3},{8,12},{9,14},{10,... | collective-permute-start | bytes 245768 | tf_op jit(solution)/shard_map/ppermute | solution.py:201
  11.4 9.3 %collective-permute-start.20 = (bf16[1,32,1280]{2,1,0:T(8,128)(2,1)S(1)}, bf16[1,32,1280]{2,1,0:T(8,128)(2,1)S(1)}, u32[]{:S(2)}, u32[]{:S(2)}) collective-permute-start(bf16[1,32,1280]{2,1,0:T(8,128)(2,1)S(1)} %get-tuple-element.12), channel_id=1, source_target_pairs={{0,8},{1,10},{2,9},{3,11},{4,12},{5,14},{6,13},{7,15},{8,0},{9,2},... | collective-permute-start | bytes 245768 | tf_op jit(solution)/shard_map/ppermute | solution.py:201
  14.0 7.4 %collective-permute-start.21 = (bf16[1,32,1280]{2,1,0:T(8,128)(2,1)S(1)}, bf16[1,32,1280]{2,1,0:T(8,128)(2,1)S(1)}, u32[]{:S(2)}, u32[]{:S(2)}) collective-permute-start(bf16[1,32,1280]{2,1,0:T(8,128)(2,1)S(1)} %get-tuple-element.12), channel_id=1, source_target_pairs={{0,12},{1,14},{2,13},{3,15},{4,8},{5,10},{6,9},{7,11},{8,4},{9,6},... | collective-permute-start | bytes 245768 | tf_op jit(solution)/shard_map/ppermute | solution.py:201
  14.0 1.7 %collective-permute-start.12 = (bf16[1,32,1280]{2,1,0:T(8,128)(2,1)S(1)}, bf16[1,32,1280]{2,1,0:T(8,128)(2,1)S(1)}, u32[]{:S(2)}, u32[]{:S(2)}) collective-permute-start(bf16[1,32,1280]{2,1,0:T(8,128)(2,1)S(1)} %get-tuple-element.11), channel_id=1, source_target_pairs={{0,0},{1,2},{2,1},{3,3},{4,4},{5,6},{6,5},{7,7},{8,8},{9,10},{10,9... | collective-permute-start | bytes 245768 | tf_op jit(solution)/shard_map/ppermute | solution.py:201
  14.7 10.6 %collective-permute-start.13 = (bf16[1,32,1280]{2,1,0:T(8,128)(2,1)S(1)}, bf16[1,32,1280]{2,1,0:T(8,128)(2,1)S(1)}, u32[]{:S(2)}, u32[]{:S(2)}) collective-permute-start(bf16[1,32,1280]{2,1,0:T(8,128)(2,1)S(1)} %get-tuple-element.11), channel_id=1, source_target_pairs={{0,4},{1,6},{2,5},{3,7},{4,0},{5,2},{6,1},{7,3},{8,12},{9,14},{10,... | collective-permute-start | bytes 245768 | tf_op jit(solution)/shard_map/ppermute | solution.py:201
  15.6 0.7 collective-permute-start.6
  16.3 0.7 collective-permute-start
  17.0 8.3 %collective-permute-start.14 = (bf16[1,32,1280]{2,1,0:T(8,128)(2,1)S(1)}, bf16[1,32,1280]{2,1,0:T(8,128)(2,1)S(1)}, u32[]{:S(2)}, u32[]{:S(2)}) collective-permute-start(bf16[1,32,1280]{2,1,0:T(8,128)(2,1)S(1)} %get-tuple-element.11), channel_id=1, source_target_pairs={{0,8},{1,10},{2,9},{3,11},{4,12},{5,14},{6,13},{7,15},{8,0},{9,2},... | collective-permute-start | bytes 245768 | tf_op jit(solution)/shard_map/ppermute | solution.py:201
  20.6 6.5 %collective-permute-start.15 = (bf16[1,32,1280]{2,1,0:T(8,128)(2,1)S(1)}, bf16[1,32,1280]{2,1,0:T(8,128)(2,1)S(1)}, u32[]{:S(2)}, u32[]{:S(2)}) collective-permute-start(bf16[1,32,1280]{2,1,0:T(8,128)(2,1)S(1)} %get-tuple-element.11), channel_id=1, source_target_pairs={{0,12},{1,14},{2,13},{3,15},{4,8},{5,10},{6,9},{7,11},{8,4},{9,6},... | collective-permute-start | bytes 245768 | tf_op jit(solution)/shard_map/ppermute | solution.py:201
  20.7 9.1 %collective-permute-start.7 = (bf16[1,32,1280]{2,1,0:T(8,128)(2,1)S(1)}, bf16[1,32,1280]{2,1,0:T(8,128)(2,1)S(1)}, u32[]{:S(2)}, u32[]{:S(2)}) collective-permute-start(bf16[1,32,1280]{2,1,0:T(8,128)(2,1)S(1)} %get-tuple-element.10), channel_id=1, source_target_pairs={{0,4},{1,6},{2,5},{3,7},{4,0},{5,2},{6,1},{7,3},{8,12},{9,14},{10,... | collective-permute-start | bytes 245768 | tf_op jit(solution)/shard_map/ppermute | solution.py:201
  21.4 9.0 %collective-permute-start.8 = (bf16[1,32,1280]{2,1,0:T(8,128)(2,1)S(1)}, bf16[1,32,1280]{2,1,0:T(8,128)(2,1)S(1)}, u32[]{:S(2)}, u32[]{:S(2)}) collective-permute-start(bf16[1,32,1280]{2,1,0:T(8,128)(2,1)S(1)} %get-tuple-element.10), channel_id=1, source_target_pairs={{0,8},{1,10},{2,9},{3,11},{4,12},{5,14},{6,13},{7,15},{8,0},{9,2},... | collective-permute-start | bytes 245768 | tf_op jit(solution)/shard_map/ppermute | solution.py:201
  25.2 25.2 %collective-permute-start.9 = (bf16[1,32,1280]{2,1,0:T(8,128)(2,1)S(1)}, bf16[1,32,1280]{2,1,0:T(8,128)(2,1)S(1)}, u32[]{:S(2)}, u32[]{:S(2)}) collective-permute-start(bf16[1,32,1280]{2,1,0:T(8,128)(2,1)S(1)} %get-tuple-element.10), channel_id=1, source_target_pairs={{0,12},{1,14},{2,13},{3,15},{4,8},{5,10},{6,9},{7,11},{8,4},{9,6},... | collective-permute-start | bytes 245768 | tf_op jit(solution)/shard_map/ppermute | solution.py:201
  25.3 25.2 %collective-permute-start.1 = (bf16[1,32,1280]{2,1,0:T(8,128)(2,1)S(1)}, bf16[1,32,1280]{2,1,0:T(8,128)(2,1)S(1)}, u32[]{:S(2)}, u32[]{:S(2)}) collective-permute-start(bf16[1,32,1280]{2,1,0:T(8,128)(2,1)S(1)} %get-tuple-element.9), channel_id=1, source_target_pairs={{0,4},{1,6},{2,5},{3,7},{4,0},{5,2},{6,1},{7,3},{8,12},{9,14},{10,... | collective-permute-start | bytes 245768 | tf_op jit(solution)/shard_map/ppermute | solution.py:201
  27.1 24.0 %collective-permute-start.2 = (bf16[1,32,1280]{2,1,0:T(8,128)(2,1)S(1)}, bf16[1,32,1280]{2,1,0:T(8,128)(2,1)S(1)}, u32[]{:S(2)}, u32[]{:S(2)}) collective-permute-start(bf16[1,32,1280]{2,1,0:T(8,128)(2,1)S(1)} %get-tuple-element.9), channel_id=1, source_target_pairs={{0,8},{1,10},{2,9},{3,11},{4,12},{5,14},{6,13},{7,15},{8,0},{9,2},... | collective-permute-start | bytes 245768 | tf_op jit(solution)/shard_map/ppermute | solution.py:201
  29.9 21.2 %collective-permute-start.3 = (bf16[1,32,1280]{2,1,0:T(8,128)(2,1)S(1)}, bf16[1,32,1280]{2,1,0:T(8,128)(2,1)S(1)}, u32[]{:S(2)}, u32[]{:S(2)}) collective-permute-start(bf16[1,32,1280]{2,1,0:T(8,128)(2,1)S(1)} %get-tuple-element.9), channel_id=1, source_target_pairs={{0,12},{1,14},{2,13},{3,15},{4,8},{5,10},{6,9},{7,11},{8,4},{9,6},... | collective-permute-start | bytes 245768 | tf_op jit(solution)/shard_map/ppermute | solution.py:201
  30.4 25.3 %collective-permute-start.22 = (bf16[1,128,1280]{2,1,0:T(8,128)(2,1)S(1)}, bf16[1,128,1280]{2,1,0:T(8,128)(2,1)S(1)}, u32[]{:S(2)}, u32[]{:S(2)}) collective-permute-start(bf16[1,128,1280]{2,1,0:T(8,128)(2,1)S(1)} %constant_dynamic-update-slice_fusion.12), channel_id=1, source_target_pairs={{0,2},{2,0},{1,3},{3,1},{4,6},{6,4},{5,7},{7,5},{8,10},{10,8},{9,1... | collective-permute-start | bytes 983048 | tf_op jit(solution)/shard_map/ppermute | solution.py:203
  50.4 5.6 %collective-permute-start.16 = (bf16[1,128,1280]{2,1,0:T(8,128)(2,1)S(1)}, bf16[1,128,1280]{2,1,0:T(8,128)(2,1)S(1)}, u32[]{:S(2)}, u32[]{:S(2)}) collective-permute-start(bf16[1,128,1280]{2,1,0:T(8,128)(2,1)S(1)} %constant_dynamic-update-slice_fusion.8), channel_id=1, source_target_pairs={{0,2},{2,0},{1,3},{3,1},{4,6},{6,4},{5,7},{7,5},{8,10},{10,8},{9,1... | collective-permute-start | bytes 983048 | tf_op jit(solution)/shard_map/ppermute | solution.py:203
  50.5 7.4 %collective-permute-start.10 = (bf16[1,128,1280]{2,1,0:T(8,128)(2,1)S(1)}, bf16[1,128,1280]{2,1,0:T(8,128)(2,1)S(1)}, u32[]{:S(2)}, u32[]{:S(2)}) collective-permute-start(bf16[1,128,1280]{2,1,0:T(8,128)(2,1)S(1)} %constant_dynamic-update-slice_fusion.4), channel_id=1, source_target_pairs={{0,2},{2,0},{1,3},{3,1},{4,6},{6,4},{5,7},{7,5},{8,10},{10,8},{9,1... | collective-permute-start | bytes 983048 | tf_op jit(solution)/shard_map/ppermute | solution.py:203
  51.1 7.1 %collective-permute-start.4 = (bf16[1,128,1280]{2,1,0:T(8,128)(2,1)S(1)}, bf16[1,128,1280]{2,1,0:T(8,128)(2,1)S(1)}, u32[]{:S(2)}, u32[]{:S(2)}) collective-permute-start(bf16[1,128,1280]{2,1,0:T(8,128)(2,1)S(1)} %constant_dynamic-update-slice_fusion), channel_id=1, source_target_pairs={{0,2},{2,0},{1,3},{3,1},{4,6},{6,4},{5,7},{7,5},{8,10},{10,8},{9,1... | collective-permute-start | bytes 983048 | tf_op jit(solution)/shard_map/ppermute | solution.py:203
  55.7 7.1 %collective-permute-start.23 = (bf16[1,128,640]{2,1,0:T(8,128)(2,1)S(1)}, bf16[1,128,640]{2,1,0:T(8,128)(2,1)S(1)}, u32[]{:S(2)}, u32[]{:S(2)}) collective-permute-start(bf16[1,128,640]{2,1,0:T(8,128)(2,1)S(1)} %dynamic-slice_select_fusion), channel_id=1, source_target_pairs={{0,1},{1,0},{2,3},{3,2},{4,5},{5,4},{6,7},{7,6},{8,9},{9,8},{10,11... | collective-permute-start | bytes 491528 | tf_op jit(solution)/shard_map/ppermute | solution.py:206
  56.0 10.3 %collective-permute-start.17 = (bf16[1,128,640]{2,1,0:T(8,128)(2,1)S(1)}, bf16[1,128,640]{2,1,0:T(8,128)(2,1)S(1)}, u32[]{:S(2)}, u32[]{:S(2)}) collective-permute-start(bf16[1,128,640]{2,1,0:T(8,128)(2,1)S(1)} %dynamic-slice_select_fusion.1), channel_id=1, source_target_pairs={{0,1},{1,0},{2,3},{3,2},{4,5},{5,4},{6,7},{7,6},{8,9},{9,8},{10,11... | collective-permute-start | bytes 491528 | tf_op jit(solution)/shard_map/ppermute | solution.py:206
  58.0 11.9 %collective-permute-start.11 = (bf16[1,128,640]{2,1,0:T(8,128)(2,1)S(1)}, bf16[1,128,640]{2,1,0:T(8,128)(2,1)S(1)}, u32[]{:S(2)}, u32[]{:S(2)}) collective-permute-start(bf16[1,128,640]{2,1,0:T(8,128)(2,1)S(1)} %dynamic-slice_select_fusion.2), channel_id=1, source_target_pairs={{0,1},{1,0},{2,3},{3,2},{4,5},{5,4},{6,7},{7,6},{8,9},{9,8},{10,11... | collective-permute-start | bytes 491528 | tf_op jit(solution)/shard_map/ppermute | solution.py:206
  58.3 14.1 %collective-permute-start.5 = (bf16[1,128,640]{2,1,0:T(8,128)(2,1)S(1)}, bf16[1,128,640]{2,1,0:T(8,128)(2,1)S(1)}, u32[]{:S(2)}, u32[]{:S(2)}) collective-permute-start(bf16[1,128,640]{2,1,0:T(8,128)(2,1)S(1)} %dynamic-slice_select_fusion.3), channel_id=1, source_target_pairs={{0,1},{1,0},{2,3},{3,2},{4,5},{5,4},{6,7},{7,6},{8,9},{9,8},{10,11... | collective-permute-start | bytes 491528 | tf_op jit(solution)/shard_map/ppermute | solution.py:206

commit v2 on v1

v2 whole, which is shorter than its diff:
```python
import functools
import math

import jax
import jax.numpy as jnp
import numpy as np
from jax import lax
from jax.experimental import pallas as pl
from jax.experimental.pallas import tpu as pltpu
from jax.sharding import PartitionSpec as P

L = 128
F = 4
SHARES = 4
SIZES = (2, 2)
VMEM_LIMIT = 48 * 1024 * 1024


def make_table(length):
    sample = np.arange(length)
    bins = (np.arange(F) + 1) * (length // 16)
    angle = 2.0 * math.pi * (sample[:, None] * bins[None, :] % length) / length
    taper = 0.5 - 0.5 * np.cos(2.0 * math.pi * sample / length)
    weight = taper / math.sqrt(length)
    real_part = weight[:, None] * np.cos(angle)
    imag_part = -weight[:, None] * np.sin(angle)
    table = np.concatenate([real_part, imag_part], axis=1).astype(np.float32)
    return table.astype(jnp.bfloat16)


def spectra_kernel(offsets, table_ref, dead_ref, raw_ref, *rest):
    outs, (shifted, dead_rows, spectrum) = rest[:-3], rest[-3:]
    windows, record_len, width = raw_ref.shape
    step = pl.program_id(0)

    @pl.when(step == 0)
    def _():
        for w in range(windows):
            shifted[w] = pltpu.roll(table_ref[...], offsets[w], 1)
        listed = jnp.broadcast_to(dead_ref[...], (128, dead_ref.shape[1]))
        dead_rows[...] = listed.T

    for w in range(windows):
        lhs = shifted[w][:, :record_len].astype(jnp.bfloat16)
        found = jnp.dot(lhs, raw_ref[w], preferred_element_type=jnp.float32)
        spectrum[:, w, :] = found[: 2 * F]

    power = spectrum[0] * spectrum[0] + spectrum[F] * spectrum[F]
    for f in range(1, F):
        power += spectrum[f] * spectrum[f] + spectrum[F + f] * spectrum[F + f]
    power *= 1.0 / F
    block = lax.axis_index("row") * lax.axis_size("col") + lax.axis_index("col")
    first = (block * pl.num_programs(0) + step) * width
    alive = []
    for part in range(width // 128):
        ids = first + part * 128 + lax.broadcasted_iota(jnp.int32, (1, 128), 1)
        hit = (dead_rows[...] == ids).astype(jnp.float32)
        alive.append(1.0 - jnp.max(hit, axis=0, keepdims=True))
    factor = lax.rsqrt(jnp.maximum(power, 0.25)) * jnp.concatenate(alive, axis=1)
    places = [(out, k) for out in outs for k in range(out.shape[0])]
    for f, (out, k) in enumerate(places):
        for part in range(2):
            white = (spectrum[part * F + f] * factor).astype(jnp.bfloat16)
            out[k, part * windows : (part + 1) * windows, :] = white


def spectra(raw_traces, window_offsets, dead_channels, sizes):
    windows, record_len, chans = raw_traces.shape
    width = 256 if chans % 256 == 0 else 128
    table = np.zeros((16, 256), np.float32)
    table[: 2 * F, :L] = make_table(L).astype(np.float32).T
    dead = dead_channels.reshape(1, -1)
    return pl.pallas_call(
        spectra_kernel,
        grid_spec=pltpu.PrefetchScalarGridSpec(
            num_scalar_prefetch=1,
            grid=(chans // width,),
            in_specs=[
                pl.BlockSpec((16, 256), lambda j, o: (0, 0)),
                pl.BlockSpec(dead.shape, lambda j, o: (0, 0)),
                pl.BlockSpec((windows, record_len, width), lambda j, o: (0, 0, j)),
            ],
            out_specs=[
                pl.BlockSpec((per, 2 * windows, width), lambda j, o: (0, 0, j)) for per in sizes
            ],
            scratch_shapes=[
                pltpu.VMEM((windows, 16, 256), jnp.float32),
                pltpu.VMEM((dead.shape[1], 128), jnp.int32),
                pltpu.VMEM((2 * F, windows, width), jnp.float32),
            ],
        ),
        out_shape=[
            jax.ShapeDtypeStruct((per, 2 * windows, chans), jnp.bfloat16) for per in sizes
        ],
        compiler_params=pltpu.CompilerParams(vmem_limit_bytes=VMEM_LIMIT),
        cost_estimate=pl.CostEstimate(
            flops=2 * 16 * windows * record_len * chans,
            bytes_accessed=2 * windows * record_len * chans,
            transcendentals=0,
        ),
        name="spectra",
    )(window_offsets, jnp.asarray(table), dead, raw_traces)


def products_kernel(scale, start, spots, whole, theirs, near, far, *rest):
    out, picked, left, ready, sems = rest[-5:]
    per, depth, chans = whole.shape
    rows = near.shape[2]
    width = ready.shape[3]
    tiles = chans // width
    slots = ready.shape[0]
    f, step = pl.program_id(0), pl.program_id(1)
    count = f * pl.num_programs(1) + step
    own, source = spots[0], spots[1]

    @pl.when(step == 0)
    def _():
        lanes = pl.ds(pl.multiple_of(own * rows, 128), rows)
        for case, take in enumerate(
            (
                lambda: whole[f, :, lanes],
                lambda: theirs[f, :, lanes],
                lambda: near[f],
                lambda: far[f],
            )
        ):

            @pl.when(source == case)
            def _():
                picked[...] = take()

        piece = depth // SHARES
        for p in range(SHARES):
            at = slice(p * piece, (p + 1) * piece)
            real = picked[p * piece : p * piece + piece // 2, :].astype(jnp.float32)
            imag = picked[p * piece + piece // 2 : (p + 1) * piece, :].astype(jnp.float32)
            left[0, :, at] = jnp.concatenate([real, imag], axis=0).T.astype(jnp.bfloat16)
            left[1, :, at] = jnp.concatenate([-imag, real], axis=0).T.astype(jnp.bfloat16)

    second = step // tiles
    tile = step - second * tiles
    slot = lax.rem(count, slots)
    side = own + second - 2 * own * second
    columns = pl.ds(pl.multiple_of(tile * width, 128), width)
    places = pl.ds(pl.multiple_of(side * chans + tile * width, 128), width)

    def store(at):
        return pltpu.make_async_copy(
            ready.at[at], out.at[:, start + f, :, places], sems.at[at]
        )

    @pl.when(count >= slots)
    def _():
        store(slot).wait()

    def multiply(right):
        for part in range(2):
            found = jnp.dot(left[part], right, preferred_element_type=jnp.float32)
            ready[slot, part] = (found * scale).astype(jnp.bfloat16)

    @pl.when(second == 0)
    def _():
        multiply(whole[f, :, columns])

    @pl.when(second == 1)
    def _():
        multiply(theirs[f, :, columns])

    store(slot).start()

    @pl.when(count == per * pl.num_programs(1) - 1)
    def _():
        for at in range(min(slots, per * 2 * tiles)):
            store(at).wait()


def products(spots, whole, theirs, near, far, start, total, target, scale):
    per, depth, chans = whole.shape
    rows = near.shape[2]
    width = chans // 2
    slots = 4
    operands = [whole, theirs, near, far]
    in_specs = [pl.BlockSpec(memory_space=pltpu.VMEM)] * 4
    args = [spots, *operands]
    aliases = {}
    if target is not None:
        in_specs.append(pl.BlockSpec(memory_space=pl.ANY))
        aliases = {len(args): 0}
        args.append(target)
    return pl.pallas_call(
        functools.partial(products_kernel, scale, start),
        grid_spec=pltpu.PrefetchScalarGridSpec(
            num_scalar_prefetch=1,
            grid=(per, 2 * (chans // width)),
            in_specs=in_specs,
            out_specs=pl.BlockSpec(memory_space=pl.ANY),
            scratch_shapes=[
                pltpu.VMEM((depth, rows), jnp.bfloat16),
                pltpu.VMEM((2, rows, depth), jnp.bfloat16),
                pltpu.VMEM((slots, 2, rows, width), jnp.bfloat16),
                pltpu.SemaphoreType.DMA((slots,)),
            ],
        ),
        out_shape=jax.ShapeDtypeStruct((2, total, rows, 2 * chans), jnp.bfloat16),
        input_output_aliases=aliases,
        compiler_params=pltpu.CompilerParams(vmem_limit_bytes=VMEM_LIMIT),
        cost_estimate=pl.CostEstimate(
            flops=8 * per * rows * depth * chans,
            bytes_accessed=8 * per * rows * chans,
            transcendentals=0,
        ),
        name="products",
    )(*args)


def square_body(raw_traces, window_offsets, dead_channels):
    windows, _, chans = raw_traces.shape
    t, r, c = lax.axis_index("tm"), lax.axis_index("row"), lax.axis_index("col")
    scale = 1.0 / (SHARES * windows)
    half = chans // 2
    axes = ("tm", "row", "col")
    corners = [(a, b) for a in range(2) for b in range(2)]

    def place(z, row, col):
        return (z * 2 + row) * 2 + col

    def along(pairs, turned):
        moves = []
        for z, to in pairs:
            for a, b in corners:
                moves.append((place(z, a, b), place(to, b, a) if turned else place(to, a, b)))
        return moves

    def apart(d):
        return [(z, z ^ d) for z in range(SHARES)]

    across, slanted = [], []
    for z in range(SHARES):
        for b in range(2):
            across.append((place(z, z % 2, b), place(z, z % 2, 1 - b)))
            slanted.append((place(z, z % 2, b), place(z, 1 - z % 2, 1 - b)))

    home = (c == t // 2).astype(jnp.int32)
    holder = (r == t % 2).astype(jnp.int32)
    spots = jnp.stack([r, (1 - home) * 2 + 1 - holder]).astype(jnp.int32)
    inner = (t == 1) | (t == 2)

    blocks = spectra(raw_traces, window_offsets, dead_channels, SIZES)
    result, start = None, 0
    for block in blocks:
        here = lax.ppermute(block, axes, along(apart(0), True))
        second = lax.ppermute(block, axes, along(apart(2), True))
        first = lax.ppermute(block, axes, along(apart(1), True))
        middle = lax.ppermute(block, axes, along([(1, 2), (2, 1)], True))
        passed = lax.ppermute(second, axes, along([(2, 3), (1, 0)], False))
        third = jnp.where(inner, middle, passed)
        whole = jnp.concatenate([here, first, second, third], axis=1)
        same = lax.dynamic_slice_in_dim(whole, r * half, half, 2)
        other = lax.dynamic_slice_in_dim(whole, (1 - r) * half, half, 2)
        near = lax.ppermute(same, axes, across)
        far = lax.ppermute(other, axes, slanted)
        theirs = lax.ppermute(whole, "row", [(0, 1), (1, 0)])
        result = products(spots, whole, theirs, near, far, start, F, result, scale)
        start += block.shape[0]
    return result


def contract(left_part, right_part):
    windows_here = left_part.shape[1]
    left_split = left_part.reshape(2, F, windows_here, left_part.shape[2])
    right_split = right_part.reshape(2, F, windows_here, right_part.shape[2])
    real_out = jnp.einsum(
        "cfwi,cfwj->fij", left_split, right_split, preferred_element_type=jnp.float32
    )
    crossed = jnp.stack([right_split[1], -right_split[0]], axis=0)
    imag_out = jnp.einsum("cfwi,cfwj->fij", left_split, crossed, preferred_element_type=jnp.float32)
    return jnp.stack([real_out, imag_out], axis=0)


def gather_body(raw_traces, window_offsets, dead_channels):
    windows, _, chans = raw_traces.shape
    (whole,) = spectra(raw_traces, window_offsets, dead_channels, (F,))
    whitened = whole.reshape(F, 2, windows, chans).transpose(1, 0, 2, 3)
    whitened = whitened.reshape(2 * F, windows, chans)
    every_chan = lax.all_gather(whitened, ("row", "col"), axis=2, tiled=True)
    row_pair = lax.all_to_all(every_chan, "tm", split_axis=2, concat_axis=1, tiled=True)
    inverse = 1.0 / row_pair.shape[1]
    col_width = every_chan.shape[2] // lax.axis_size("col")
    col_block = lax.dynamic_slice_in_dim(
        every_chan, lax.axis_index("col") * col_width, col_width, 2
    )
    half_rows = row_pair.shape[2] // lax.axis_size("row")
    row_block = lax.dynamic_slice_in_dim(row_pair, lax.axis_index("row") * half_rows, half_rows, 2)
    total = contract(row_block, lax.all_gather(col_block, "tm", axis=1, tiled=True))
    return (total * inverse).astype(jnp.bfloat16)


def solution(mesh):
    sizes = mesh.shape
    square = sizes["tm"] == SHARES and sizes["row"] == 2 and sizes["col"] == 2
    in_specs = (P("tm", None, ("groups", "row", "col")), P(("groups", "tm")), P("groups"))
    out_specs = P(None, None, ("groups", "tm", "row"), "col")
    return jax.shard_map(
        square_body if square else gather_body,
        mesh=mesh,
        in_specs=in_specs,
        out_specs=out_specs,
        check_vma=False,
    )
```

time: 101 us -> 79.9 us (0.79)
  starting transfers between devices: 50.9 us -> 30.7 us
  Pallas kernels: 33.9 us -> 23.8 us
  waiting for transfers between devices: 13.3 us -> 19 us
  local copies, waits for them, and re-layouts: 2.13 us -> 5.49 us
    ppermute x24 -> x16, starting transfers between devices: 50.9 us -> 30.7 us  [the longest x2 11 us: square_body(): second = lax.ppermute(block, axes, along(apart(2), True))]
    pallas_call x4 -> x2, Pallas kernels: 28.3 us -> 18.2 us  [products(): pl.pallas_call(functools.partial(products_kernel, scale, start), grid_spe...]
    ppermute x24 -> x16, waiting for transfers between devices: 13.3 us -> 19 us  [the longest x2 16.5 us: square_body(): second = lax.ppermute(block, axes, along(apart(2), True))]
    dynamic_slice x0 -> x2, local copies, waits for them, and re-layouts: none -> 1.76 us  [square_body(): other = lax.dynamic_slice_in_dim(whole, (1 - r) * half, half, 2)]
    unnamed x18 -> x10, local copies, waits for them, and re-layouts: 2.11 us -> 3.72 us
  transfers between devices with their start and end apart: 24 -> 16, of which waited for: 5 -> 5; matrix products, arithmetic and copies ran while one was open for 0% -> 2% of each run, Pallas kernels for 0% -> 12%
where the time goes in v2:
time: 79.9 us; the launch traced here: 79.4 us
  starting transfers between devices  30.7 us (38%)
  Pallas kernels  23.8 us (30%)
  waiting for transfers between devices  19 us (24%)
  local copies, waits for them, and re-layouts  5.49 us (7%)
    pallas_call x2, Pallas kernels, products(): pl.pallas_call(functools.partial(products_kernel, scale, start), grid_spe...  18.2 us
    ppermute x2, waiting for transfers between devices, square_body(): second = lax.ppermute(block, axes, along(apart(2), True))  16.5 us
    ppermute x2, starting transfers between devices, square_body(): second = lax.ppermute(block, axes, along(apart(2), True))  11 us
    ppermute x2, starting transfers between devices, square_body(): near = lax.ppermute(same, axes, across)  5.65 us
    pallas_call x1, Pallas kernels, spectra(): pl.pallas_call(spectra_kernel, grid_spec=pltpu.PrefetchScalarGridSpec(num...  5.57 us
    unnamed x10, local copies, waits for them, and re-layouts  3.72 us
    ppermute x2, starting transfers between devices, square_body(): far = lax.ppermute(other, axes, slanted)  3.45 us
    ppermute x2, starting transfers between devices, square_body(): theirs = lax.ppermute(whole, 'row', [(0, 1), (1, 0)])  3.3 us
  transfers between devices with their start and end apart: 16, of which 5 were waited for; matrix products, arithmetic and copies ran while one was open for 2% of the time, Pallas kernels for 12%

profile of v2, /device:TPU:0, one launch (start us, length us, event | category | flops | bytes accessed | tf_op | source)
XLA Modules:
  0.0 79.4 jit_solution(3084767058094968733)
XLA Ops:
  0.0 0.0 copy-start.2
  0.0 0.7 copy-done.2
  0.7 0.0 copy-start.3
  0.7 0.7 copy-done.3
  1.4 0.0 copy-start.4
  1.4 0.7 copy-done.4
  2.0 5.6 %spectra.1 = (bf16[2,32,1280]{2,1,0:T(8,128)(2,1)S(1)}, bf16[2,32,1280]{2,1,0:T(8,128)(2,1)S(1)}) custom-call(s32[16]{0:T(128)S(1)} %copy-done.3, f32[16,256]{1,0:T(8,128)S(1)} %copy-done.2, s32[1,128]{1,0:T(1,128)S(1)} %bitcast.3, bf16[16,144,1280]{2,1,0:T(8,128)(2,1)} %raw_ref.1), custom_call_target="tpu_custom_call" | custom-call | flops 94371840 | bytes 5898240 | tf_op jit(solution)/shard_map/spectra/pallas_call | solution.py:73
  7.6 4.1 %collective-permute-start.10 = (bf16[2,32,1280]{2,1,0:T(8,128)(2,1)S(1)}, bf16[2,32,1280]{2,1,0:T(8,128)(2,1)S(1)}, u32[]{:S(2)}, u32[]{:S(2)}) collective-permute-start(bf16[2,32,1280]{2,1,0:T(8,128)(2,1)S(1)} %get-tuple-element.8), channel_id=1, source_target_pairs={{0,8},{1,10},{2,9},{3,11},{4,12},{5,14},{6,13},{7,15},{8,0},{9,2},... | collective-permute-start | bytes 491528 | tf_op jit(solution)/shard_map/ppermute | solution.py:252
  11.7 0.7 collective-permute-start.11
  12.4 7.3 %collective-permute-done.10 = bf16[2,32,1280]{2,1,0:T(8,128)(2,1)S(1)} collective-permute-done((bf16[2,32,1280]{2,1,0:T(8,128)(2,1)S(1)}, bf16[2,32,1280]{2,1,0:T(8,128)(2,1)S(1)}, u32[]{:S(2)}, u32[]{:S(2)}) %collective-permute-start.10) | collective-permute-done | bytes 163872 | tf_op jit(solution)/shard_map/ppermute | solution.py:252
  19.6 1.3 %collective-permute-start.12 = (bf16[2,32,1280]{2,1,0:T(8,128)(2,1)S(1)}, bf16[2,32,1280]{2,1,0:T(8,128)(2,1)S(1)}, u32[]{:S(2)}, u32[]{:S(2)}) collective-permute-start(bf16[2,32,1280]{2,1,0:T(8,128)(2,1)S(1)} %collective-permute-done.10), channel_id=1, source_target_pairs={{8,12},{9,13},{10,14},{11,15},{4,0},{5,1},{6,2},{7,3},{24,28},{25,... | collective-permute-start | bytes 491528 | tf_op jit(solution)/shard_map/ppermute | solution.py:255
  20.9 0.7 collective-permute-start.3
  21.6 6.9 %collective-permute-start.2 = (bf16[2,32,1280]{2,1,0:T(8,128)(2,1)S(1)}, bf16[2,32,1280]{2,1,0:T(8,128)(2,1)S(1)}, u32[]{:S(2)}, u32[]{:S(2)}) collective-permute-start(bf16[2,32,1280]{2,1,0:T(8,128)(2,1)S(1)} %get-tuple-element.7), channel_id=1, source_target_pairs={{0,8},{1,10},{2,9},{3,11},{4,12},{5,14},{6,13},{7,15},{8,0},{9,2},... | collective-permute-start | bytes 491528 | tf_op jit(solution)/shard_map/ppermute | solution.py:252
  28.5 0.6 collective-permute-start.1
  29.2 0.0 collective-permute-done.11
  29.2 1.4 %collective-permute-start.9 = (bf16[2,32,1280]{2,1,0:T(8,128)(2,1)S(1)}, bf16[2,32,1280]{2,1,0:T(8,128)(2,1)S(1)}, u32[]{:S(2)}, u32[]{:S(2)}) collective-permute-start(bf16[2,32,1280]{2,1,0:T(8,128)(2,1)S(1)} %get-tuple-element.8), channel_id=1, source_target_pairs={{0,4},{1,6},{2,5},{3,7},{4,0},{5,2},{6,1},{7,3},{8,12},{9,14},{10,... | collective-permute-start | bytes 491528 | tf_op jit(solution)/shard_map/ppermute | solution.py:253
  30.6 0.0 collective-permute-done.12
  30.6 0.7 collective-permute-start.8
  31.3 9.3 %collective-permute-done.2 = bf16[2,32,1280]{2,1,0:T(8,128)(2,1)S(1)} collective-permute-done((bf16[2,32,1280]{2,1,0:T(8,128)(2,1)S(1)}, bf16[2,32,1280]{2,1,0:T(8,128)(2,1)S(1)}, u32[]{:S(2)}, u32[]{:S(2)}) %collective-permute-start.2) | collective-permute-done | bytes 163872 | tf_op jit(solution)/shard_map/ppermute | solution.py:252
  40.5 0.7 collective-permute-start
  41.2 0.8 collective-permute-done.9
  42.0 1.3 %collective-permute-start.4 = (bf16[2,32,1280]{2,1,0:T(8,128)(2,1)S(1)}, bf16[2,32,1280]{2,1,0:T(8,128)(2,1)S(1)}, u32[]{:S(2)}, u32[]{:S(2)}) collective-permute-start(bf16[2,32,1280]{2,1,0:T(8,128)(2,1)S(1)} %collective-permute-done.2), channel_id=1, source_target_pairs={{8,12},{9,13},{10,14},{11,15},{4,0},{5,1},{6,2},{7,3},{24,28},{25,... | collective-permute-start | bytes 491528 | tf_op jit(solution)/shard_map/ppermute | solution.py:255
  43.3 0.0 collective-permute-done.8
  43.3 2.2 %collective-permute-start.13 = (bf16[2,128,1280]{2,1,0:T(8,128)(2,1)S(1)}, bf16[2,128,1280]{2,1,0:T(8,128)(2,1)S(1)}, u32[]{:S(2)}, u32[]{:S(2)}) collective-permute-start(bf16[2,128,1280]{2,1,0:T(8,128)(2,1)S(1)} %pad_maximum_fusion.1.whole), channel_id=1, source_target_pairs={{0,2},{2,0},{1,3},{3,1},{4,6},{6,4},{5,7},{7,5},{8,10},{10,8},{9,1... | collective-permute-start | bytes 1966088 | tf_op jit(solution)/shard_map/ppermute | solution.py:262
  45.5 0.8 %constant_dynamic-slice_fusion = (bf16[2,128,640]{2,1,0:T(8,128)(2,1)S(1)}, bf16[2,128,640]{2,1,0:T(8,128)(2,1)}) fusion(bf16[2,128,1280]{2,1,0:T(8,128)(2,1)S(1)} %pad_maximum_fusion.1.whole, s32[]{:T(128)S(6)} %select_n.36, s32[]{:T(128)S(6)} %select_n.35), kind=kLoop, calls=%fused_computation.4 | loop fusion | bytes 1310728 | tf_op jit(solution)/shard_map/dynamic_slice | solution.py:259
  46.3 0.0 collective-permute-done.3
  46.3 2.0 %collective-permute-start.15 = (bf16[2,128,640]{2,1,0:T(8,128)(2,1)S(1)}, bf16[2,128,640]{2,1,0:T(8,128)(2,1)S(1)}, u32[]{:S(2)}, u32[]{:S(2)}) collective-permute-start(bf16[2,128,640]{2,1,0:T(8,128)(2,1)S(1)} %get-tuple-element.9), channel_id=1, source_target_pairs={{0,3},{1,2},{6,5},{7,4},{8,11},{9,10},{14,13},{15,12},{16,19},{17,... | collective-permute-start | bytes 983048 | tf_op jit(solution)/shard_map/ppermute | solution.py:261
  48.3 1.4 %collective-permute-done.4 = bf16[2,32,1280]{2,1,0:T(8,128)(2,1)S(1)} collective-permute-done((bf16[2,32,1280]{2,1,0:T(8,128)(2,1)S(1)}, bf16[2,32,1280]{2,1,0:T(8,128)(2,1)S(1)}, u32[]{:S(2)}, u32[]{:S(2)}) %collective-permute-start.4) | collective-permute-done | bytes 163872 | tf_op jit(solution)/shard_map/ppermute | solution.py:255
  49.7 0.0 collective-permute-done.1
  49.8 0.0 collective-permute-done
  49.8 1.1 %collective-permute-start.5 = (bf16[2,128,1280]{2,1,0:T(8,128)(2,1)S(1)}, bf16[2,128,1280]{2,1,0:T(8,128)(2,1)S(1)}, u32[]{:S(2)}, u32[]{:S(2)}) collective-permute-start(bf16[2,128,1280]{2,1,0:T(8,128)(2,1)S(1)} %pad_maximum_fusion.whole), channel_id=1, source_target_pairs={{0,2},{2,0},{1,3},{3,1},{4,6},{6,4},{5,7},{7,5},{8,10},{10,8},{9,1... | collective-permute-start | bytes 1966088 | tf_op jit(solution)/shard_map/ppermute | solution.py:262
  50.9 2.5 %collective-permute-start.14 = (bf16[2,128,640]{2,1,0:T(8,128)(2,1)}, bf16[2,128,640]{2,1,0:T(8,128)(2,1)}, u32[]{:S(2)}, u32[]{:S(2)}) collective-permute-start(bf16[2,128,640]{2,1,0:T(8,128)(2,1)} %get-tuple-element.10), channel_id=1, source_target_pairs={{0,1},{1,0},{6,7},{7,6},{8,9},{9,8},{14,15},{15,14},{16,17},{17,16... | collective-permute-start | bytes 983048 | tf_op jit(solution)/shard_map/ppermute | solution.py:260
  53.4 1.0 %constant_dynamic-slice_fusion.2 = (bf16[2,128,640]{2,1,0:T(8,128)(2,1)}, bf16[2,128,640]{2,1,0:T(8,128)(2,1)}) fusion(bf16[2,128,1280]{2,1,0:T(8,128)(2,1)S(1)} %pad_maximum_fusion.whole, s32[]{:T(128)S(6)} %select_n.36, s32[]{:T(128)S(6)} %select_n.35), kind=kLoop, calls=%fused_computation.6 | loop fusion | bytes 1310728 | tf_op jit(solution)/shard_map/dynamic_slice | solution.py:259
  54.3 1.5 %collective-permute-start.7 = (bf16[2,128,640]{2,1,0:T(8,128)(2,1)}, bf16[2,128,640]{2,1,0:T(8,128)(2,1)S(1)}, u32[]{:S(2)}, u32[]{:S(2)}) collective-permute-start(bf16[2,128,640]{2,1,0:T(8,128)(2,1)} %get-tuple-element.11), channel_id=1, source_target_pairs={{0,3},{1,2},{6,5},{7,4},{8,11},{9,10},{14,13},{15,12},{16,19},{17,... | collective-permute-start | bytes 983048 | tf_op jit(solution)/shard_map/ppermute | solution.py:261
  55.8 0.0 collective-permute-done.15.far
  55.8 0.0 copy-start
  55.8 0.7 copy-done
  56.6 3.2 %collective-permute-start.6 = (bf16[2,128,640]{2,1,0:T(8,128)(2,1)}, bf16[2,128,640]{2,1,0:T(8,128)(2,1)S(1)}, u32[]{:S(2)}, u32[]{:S(2)}) collective-permute-start(bf16[2,128,640]{2,1,0:T(8,128)(2,1)} %get-tuple-element.12), channel_id=1, source_target_pairs={{0,1},{1,0},{6,7},{7,6},{8,9},{9,8},{14,15},{15,14},{16,17},{17,16... | collective-permute-start | bytes 983048 | tf_op jit(solution)/shard_map/ppermute | solution.py:260
  59.8 0.1 pad_add_fusion.spots
  59.9 0.3 collective-permute-done.14.near
  60.2 0.0 collective-permute-done.13.theirs
  60.2 0.0 copy-start.1
  60.2 1.0 %copy-done.1 = bf16[2,128,640]{2,1,0:T(8,128)(2,1)S(1)} copy-done((bf16[2,128,640]{2,1,0:T(8,128)(2,1)S(1)}, bf16[2,128,640]{2,1,0:T(8,128)(2,1)}, u32[]{:S(2)}) %copy-start.1) | copy-done | bytes 327704
  61.2 9.6 %products.2.rest_0_ = bf16[2,4,640,2560]{3,2,1,0:T(8,128)(2,1)} custom-call(s32[2]{0:T(128)S(1)} %pad_add_fusion.spots, bf16[2,128,1280]{2,1,0:T(8,128)(2,1)S(1)} %pad_maximum_fusion.1.whole, bf16[2,128,1280]{2,1,0:T(8,128)(2,1)S(1)} %collective-permute-done.13.theirs, bf16[2,128,640]{2,1,0:T(8,128)(2,1)} %collective-permute-done.14.near, ...), custom_call_target="tpu_custom_call" | custom-call | flops 1677721600 | bytes 13107200 | tf_op jit(solution)/shard_map/products/pallas_call | solution.py:190
  70.7 0.0 collective-permute-done.7.far
  70.8 0.0 collective-permute-done.6.near
  70.8 0.0 collective-permute-done.5.theirs
  70.8 8.6 %products.3 = bf16[2,4,640,2560]{3,2,1,0:T(8,128)(2,1)} custom-call(s32[2]{0:T(128)S(1)} %pad_add_fusion.spots, bf16[2,128,1280]{2,1,0:T(8,128)(2,1)S(1)} %pad_maximum_fusion.whole, bf16[2,128,1280]{2,1,0:T(8,128)(2,1)S(1)} %collective-permute-done.5.theirs, bf16[2,128,640]{2,1,0:T(8,128)(2,1)S(1)} %collective-permute-done.6.near, ...), custom_call_target="tpu_custom_call", output_to_operand_aliasing={{}: (5, {})} | custom-call | flops 1677721600 | bytes 13107200 | tf_op jit(solution)/shard_map/products/pallas_call | solution.py:190
  (4 shorter events, 0.1 us)
Async XLA Ops:
  0.0 0.7 copy-start.2
  0.7 0.7 copy-start.3
  1.4 0.7 copy-start.4
  7.6 12.0 %collective-permute-start.10 = (bf16[2,32,1280]{2,1,0:T(8,128)(2,1)S(1)}, bf16[2,32,1280]{2,1,0:T(8,128)(2,1)S(1)}, u32[]{:S(2)}, u32[]{:S(2)}) collective-permute-start(bf16[2,32,1280]{2,1,0:T(8,128)(2,1)S(1)} %get-tuple-element.8), channel_id=1, source_target_pairs={{0,8},{1,10},{2,9},{3,11},{4,12},{5,14},{6,13},{7,15},{8,0},{9,2},... | collective-permute-start | bytes 491528 | tf_op jit(solution)/shard_map/ppermute | solution.py:252
  11.7 17.5 %collective-permute-start.11 = (bf16[2,32,1280]{2,1,0:T(8,128)(2,1)S(1)}, bf16[2,32,1280]{2,1,0:T(8,128)(2,1)S(1)}, u32[]{:S(2)}, u32[]{:S(2)}) collective-permute-start(bf16[2,32,1280]{2,1,0:T(8,128)(2,1)S(1)} %get-tuple-element.8), channel_id=1, source_target_pairs={{4,8},{5,10},{6,9},{7,11},{8,4},{9,6},{10,5},{11,7},{20,24},{21,26... | collective-permute-start | bytes 491528 | tf_op jit(solution)/shard_map/ppermute | solution.py:254
  19.6 10.9 %collective-permute-start.12 = (bf16[2,32,1280]{2,1,0:T(8,128)(2,1)S(1)}, bf16[2,32,1280]{2,1,0:T(8,128)(2,1)S(1)}, u32[]{:S(2)}, u32[]{:S(2)}) collective-permute-start(bf16[2,32,1280]{2,1,0:T(8,128)(2,1)S(1)} %collective-permute-done.10), channel_id=1, source_target_pairs={{8,12},{9,13},{10,14},{11,15},{4,0},{5,1},{6,2},{7,3},{24,28},{25,... | collective-permute-start | bytes 491528 | tf_op jit(solution)/shard_map/ppermute | solution.py:255
  20.9 25.4 %collective-permute-start.3 = (bf16[2,32,1280]{2,1,0:T(8,128)(2,1)S(1)}, bf16[2,32,1280]{2,1,0:T(8,128)(2,1)S(1)}, u32[]{:S(2)}, u32[]{:S(2)}) collective-permute-start(bf16[2,32,1280]{2,1,0:T(8,128)(2,1)S(1)} %get-tuple-element.7), channel_id=1, source_target_pairs={{4,8},{5,10},{6,9},{7,11},{8,4},{9,6},{10,5},{11,7},{20,24},{21,26... | collective-permute-start | bytes 491528 | tf_op jit(solution)/shard_map/ppermute | solution.py:254
  21.6 18.9 %collective-permute-start.2 = (bf16[2,32,1280]{2,1,0:T(8,128)(2,1)S(1)}, bf16[2,32,1280]{2,1,0:T(8,128)(2,1)S(1)}, u32[]{:S(2)}, u32[]{:S(2)}) collective-permute-start(bf16[2,32,1280]{2,1,0:T(8,128)(2,1)S(1)} %get-tuple-element.7), channel_id=1, source_target_pairs={{0,8},{1,10},{2,9},{3,11},{4,12},{5,14},{6,13},{7,15},{8,0},{9,2},... | collective-permute-start | bytes 491528 | tf_op jit(solution)/shard_map/ppermute | solution.py:252
  28.5 21.2 %collective-permute-start.1 = (bf16[2,32,1280]{2,1,0:T(8,128)(2,1)S(1)}, bf16[2,32,1280]{2,1,0:T(8,128)(2,1)S(1)}, u32[]{:S(2)}, u32[]{:S(2)}) collective-permute-start(bf16[2,32,1280]{2,1,0:T(8,128)(2,1)S(1)} %get-tuple-element.7), channel_id=1, source_target_pairs={{0,4},{1,6},{2,5},{3,7},{4,0},{5,2},{6,1},{7,3},{8,12},{9,14},{10,... | collective-permute-start | bytes 491528 | tf_op jit(solution)/shard_map/ppermute | solution.py:253
  29.2 12.8 %collective-permute-start.9 = (bf16[2,32,1280]{2,1,0:T(8,128)(2,1)S(1)}, bf16[2,32,1280]{2,1,0:T(8,128)(2,1)S(1)}, u32[]{:S(2)}, u32[]{:S(2)}) collective-permute-start(bf16[2,32,1280]{2,1,0:T(8,128)(2,1)S(1)} %get-tuple-element.8), channel_id=1, source_target_pairs={{0,4},{1,6},{2,5},{3,7},{4,0},{5,2},{6,1},{7,3},{8,12},{9,14},{10,... | collective-permute-start | bytes 491528 | tf_op jit(solution)/shard_map/ppermute | solution.py:253
  30.6 12.7 %collective-permute-start.8 = (bf16[2,32,1280]{2,1,0:T(8,128)(2,1)S(1)}, bf16[2,32,1280]{2,1,0:T(8,128)(2,1)S(1)}, u32[]{:S(2)}, u32[]{:S(2)}) collective-permute-start(bf16[2,32,1280]{2,1,0:T(8,128)(2,1)S(1)} %get-tuple-element.8), channel_id=1, source_target_pairs={{0,0},{1,2},{2,1},{3,3},{4,4},{5,6},{6,5},{7,7},{8,8},{9,10},{10,9... | collective-permute-start | bytes 491528 | tf_op jit(solution)/shard_map/ppermute | solution.py:251
  40.5 9.2 %collective-permute-start = (bf16[2,32,1280]{2,1,0:T(8,128)(2,1)S(1)}, bf16[2,32,1280]{2,1,0:T(8,128)(2,1)S(1)}, u32[]{:S(2)}, u32[]{:S(2)}) collective-permute-start(bf16[2,32,1280]{2,1,0:T(8,128)(2,1)S(1)} %get-tuple-element.7), channel_id=1, source_target_pairs={{0,0},{1,2},{2,1},{3,3},{4,4},{5,6},{6,5},{7,7},{8,8},{9,10},{10,9... | collective-permute-start | bytes 491528 | tf_op jit(solution)/shard_map/ppermute | solution.py:251
  42.0 7.8 %collective-permute-start.4 = (bf16[2,32,1280]{2,1,0:T(8,128)(2,1)S(1)}, bf16[2,32,1280]{2,1,0:T(8,128)(2,1)S(1)}, u32[]{:S(2)}, u32[]{:S(2)}) collective-permute-start(bf16[2,32,1280]{2,1,0:T(8,128)(2,1)S(1)} %collective-permute-done.2), channel_id=1, source_target_pairs={{8,12},{9,13},{10,14},{11,15},{4,0},{5,1},{6,2},{7,3},{24,28},{25,... | collective-permute-start | bytes 491528 | tf_op jit(solution)/shard_map/ppermute | solution.py:255
  43.3 16.9 %collective-permute-start.13 = (bf16[2,128,1280]{2,1,0:T(8,128)(2,1)S(1)}, bf16[2,128,1280]{2,1,0:T(8,128)(2,1)S(1)}, u32[]{:S(2)}, u32[]{:S(2)}) collective-permute-start(bf16[2,128,1280]{2,1,0:T(8,128)(2,1)S(1)} %pad_maximum_fusion.1.whole), channel_id=1, source_target_pairs={{0,2},{2,0},{1,3},{3,1},{4,6},{6,4},{5,7},{7,5},{8,10},{10,8},{9,1... | collective-permute-start | bytes 1966088 | tf_op jit(solution)/shard_map/ppermute | solution.py:262
  46.3 9.5 %collective-permute-start.15 = (bf16[2,128,640]{2,1,0:T(8,128)(2,1)S(1)}, bf16[2,128,640]{2,1,0:T(8,128)(2,1)S(1)}, u32[]{:S(2)}, u32[]{:S(2)}) collective-permute-start(bf16[2,128,640]{2,1,0:T(8,128)(2,1)S(1)} %get-tuple-element.9), channel_id=1, source_target_pairs={{0,3},{1,2},{6,5},{7,4},{8,11},{9,10},{14,13},{15,12},{16,19},{17,... | collective-permute-start | bytes 983048 | tf_op jit(solution)/shard_map/ppermute | solution.py:261
  49.8 21.0 %collective-permute-start.5 = (bf16[2,128,1280]{2,1,0:T(8,128)(2,1)S(1)}, bf16[2,128,1280]{2,1,0:T(8,128)(2,1)S(1)}, u32[]{:S(2)}, u32[]{:S(2)}) collective-permute-start(bf16[2,128,1280]{2,1,0:T(8,128)(2,1)S(1)} %pad_maximum_fusion.whole), channel_id=1, source_target_pairs={{0,2},{2,0},{1,3},{3,1},{4,6},{6,4},{5,7},{7,5},{8,10},{10,8},{9,1... | collective-permute-start | bytes 1966088 | tf_op jit(solution)/shard_map/ppermute | solution.py:262
  50.9 9.3 %collective-permute-start.14 = (bf16[2,128,640]{2,1,0:T(8,128)(2,1)}, bf16[2,128,640]{2,1,0:T(8,128)(2,1)}, u32[]{:S(2)}, u32[]{:S(2)}) collective-permute-start(bf16[2,128,640]{2,1,0:T(8,128)(2,1)} %get-tuple-element.10), channel_id=1, source_target_pairs={{0,1},{1,0},{6,7},{7,6},{8,9},{9,8},{14,15},{15,14},{16,17},{17,16... | collective-permute-start | bytes 983048 | tf_op jit(solution)/shard_map/ppermute | solution.py:260
  54.3 16.4 %collective-permute-start.7 = (bf16[2,128,640]{2,1,0:T(8,128)(2,1)}, bf16[2,128,640]{2,1,0:T(8,128)(2,1)S(1)}, u32[]{:S(2)}, u32[]{:S(2)}) collective-permute-start(bf16[2,128,640]{2,1,0:T(8,128)(2,1)} %get-tuple-element.11), channel_id=1, source_target_pairs={{0,3},{1,2},{6,5},{7,4},{8,11},{9,10},{14,13},{15,12},{16,19},{17,... | collective-permute-start | bytes 983048 | tf_op jit(solution)/shard_map/ppermute | solution.py:261
  55.8 0.7 copy-start
  56.6 14.2 %collective-permute-start.6 = (bf16[2,128,640]{2,1,0:T(8,128)(2,1)}, bf16[2,128,640]{2,1,0:T(8,128)(2,1)S(1)}, u32[]{:S(2)}, u32[]{:S(2)}) collective-permute-start(bf16[2,128,640]{2,1,0:T(8,128)(2,1)} %get-tuple-element.12), channel_id=1, source_target_pairs={{0,1},{1,0},{6,7},{7,6},{8,9},{9,8},{14,15},{15,14},{16,17},{17,16... | collective-permute-start | bytes 983048 | tf_op jit(solution)/shard_map/ppermute | solution.py:260
  60.2 1.0 %copy-start.1 = (bf16[2,128,640]{2,1,0:T(8,128)(2,1)S(1)}, bf16[2,128,640]{2,1,0:T(8,128)(2,1)}, u32[]{:S(2)}) copy-start(bf16[2,128,640]{2,1,0:T(8,128)(2,1)} %copy-done) | copy-start | bytes 983044

commit v3 on v2

v3 whole, which is shorter than its diff:
```python
import functools
import math

import jax
import jax.numpy as jnp
import numpy as np
from jax import lax
from jax.experimental import pallas as pl
from jax.experimental.pallas import tpu as pltpu
from jax.sharding import PartitionSpec as P

L = 128
F = 4
SHARES = 4
SIZES = (2, 2)
FORWARD = (True, False)
VMEM_LIMIT = 16 * 1024 * 1024
SPECTRA_VMEM = 60 * 1024 * 1024


def make_table(length):
    sample = np.arange(length)
    bins = (np.arange(F) + 1) * (length // 16)
    angle = 2.0 * math.pi * (sample[:, None] * bins[None, :] % length) / length
    taper = 0.5 - 0.5 * np.cos(2.0 * math.pi * sample / length)
    weight = taper / math.sqrt(length)
    real_part = weight[:, None] * np.cos(angle)
    imag_part = -weight[:, None] * np.sin(angle)
    table = np.concatenate([real_part, imag_part], axis=1).astype(np.float32)
    return table.astype(jnp.bfloat16)


def spectra_kernel(offsets_in, table_in, dead_in, raw_in, *rest):
    outs, scratch = rest[:2], rest[2:]
    raw, table, dead, offsets, shifted, spectrum, raw_sems, small_sems = scratch
    steps, windows, record_len, width = raw.shape

    def fetch(step):
        lanes = pl.ds(step * width, width)
        return pltpu.make_async_copy(raw_in.at[:, :, lanes], raw.at[step], raw_sems.at[step])

    small = [
        pltpu.make_async_copy(source, target, small_sems.at[k])
        for k, (source, target) in enumerate(
            ((offsets_in, offsets), (table_in, table), (dead_in, dead))
        )
    ]
    for copy in small:
        copy.start()
    for step in range(steps):
        fetch(step).start()
    for copy in small:
        copy.wait()
    for w in range(windows):
        shifted[w] = pltpu.roll(table[...], offsets[0, w], 1)
    dead_rows = jnp.broadcast_to(dead[...], (128, dead.shape[1])).T
    block = lax.axis_index("row") * lax.axis_size("col") + lax.axis_index("col")

    for step in range(steps):
        fetch(step).wait()
        for w in range(windows):
            lhs = shifted[w][:, :record_len].astype(jnp.bfloat16)
            found = jnp.dot(lhs, raw[step, w], preferred_element_type=jnp.float32)
            spectrum[:, w, :] = found[: 2 * F]
        power = spectrum[0] * spectrum[0] + spectrum[F] * spectrum[F]
        for f in range(1, F):
            power += spectrum[f] * spectrum[f] + spectrum[F + f] * spectrum[F + f]
        power *= 1.0 / F
        first = (block * steps + step) * width
        alive = []
        for part in range(width // 128):
            ids = first + part * 128 + lax.broadcasted_iota(jnp.int32, (1, 128), 1)
            hit = (dead_rows == ids).astype(jnp.float32)
            alive.append(1.0 - jnp.max(hit, axis=0, keepdims=True))
        factor = lax.rsqrt(jnp.maximum(power, 0.25)) * jnp.concatenate(alive, axis=1)
        run = math.gcd(outs[0].shape[3], width)
        for f in range(F):
            for part in range(2):
                white = (spectrum[part * F + f] * factor).astype(jnp.bfloat16)
                at = slice(part * windows, (part + 1) * windows)
                for out in outs:
                    for low in range(0, width if f < out.shape[1] else 0, run):
                        split, lane = divmod(step * width + low, out.shape[3])
                        out[split, f, at, lane : lane + run] = white[:, low : low + run]


def spectra(raw_traces, window_offsets, dead_channels, leading, splits):
    windows, record_len, chans = raw_traces.shape
    width = 256 if chans % 256 == 0 else 128
    steps = chans // width
    table = np.zeros((16, 256), np.float32)
    table[: 2 * F, :L] = make_table(L).astype(np.float32).T
    dead = dead_channels.reshape(1, -1)
    offsets = window_offsets.reshape(1, -1)
    return pl.pallas_call(
        spectra_kernel,
        in_specs=[pl.BlockSpec(memory_space=pltpu.HBM)] * 4,
        out_specs=[pl.BlockSpec(memory_space=pltpu.VMEM)] * 2,
        scratch_shapes=[
            pltpu.VMEM((steps, windows, record_len, width), jnp.bfloat16),
            pltpu.VMEM((16, 256), jnp.float32),
            pltpu.VMEM(dead.shape, jnp.int32),
            pltpu.SMEM(offsets.shape, jnp.int32),
            pltpu.VMEM((windows, 16, 256), jnp.float32),
            pltpu.VMEM((2 * F, windows, width), jnp.float32),
            pltpu.SemaphoreType.DMA((steps,)),
            pltpu.SemaphoreType.DMA((3,)),
        ],
        out_shape=[
            jax.ShapeDtypeStruct((splits, per, 2 * windows, chans // splits), jnp.bfloat16)
            for per in (leading, F)
        ],
        compiler_params=pltpu.CompilerParams(vmem_limit_bytes=SPECTRA_VMEM),
        cost_estimate=pl.CostEstimate(
            flops=2 * 16 * windows * record_len * chans,
            bytes_accessed=2 * windows * record_len * chans,
            transcendentals=0,
        ),
        name="spectra",
    )(offsets, jnp.asarray(table), dead, raw_traces)


def products_kernel(scale, start, spots, whole, theirs, near, far, *rest):
    out, picked, left, ready, sems, pick_sem = rest[-6:]
    splits, per, depth, width = whole.shape
    slots = ready.shape[0]
    f, step = pl.program_id(0), pl.program_id(1)
    count = f * pl.num_programs(1) + step
    own, source = spots[0], spots[1]

    @pl.when(step == 0)
    def _():
        for case, ref in enumerate((whole.at[own, f], theirs.at[own, f], near.at[f], far.at[f])):

            @pl.when(source == case)
            def _():
                pltpu.make_async_copy(ref, picked, pick_sem).start()

        pltpu.make_async_copy(near.at[f], picked, pick_sem).wait()
        piece = depth // SHARES
        for p in range(SHARES):
            at = slice(p * piece, (p + 1) * piece)
            real = picked[p * piece : p * piece + piece // 2, :].astype(jnp.float32)
            imag = picked[p * piece + piece // 2 : (p + 1) * piece, :].astype(jnp.float32)
            left[0, :, at] = jnp.concatenate([real, imag], axis=0).T.astype(jnp.bfloat16)
            left[1, :, at] = jnp.concatenate([-imag, real], axis=0).T.astype(jnp.bfloat16)

    second = step // splits
    tile = step - second * splits
    slot = lax.rem(count, slots)
    side = own + second - 2 * own * second
    places = pl.ds(pl.multiple_of((side * splits + tile) * width, 128), width)

    def store(at):
        return pltpu.make_async_copy(
            ready.at[at], out.at[:, start + f, :, places], sems.at[at]
        )

    @pl.when(count >= slots)
    def _():
        store(slot).wait()

    def multiply(right):
        for part in range(2):
            found = jnp.dot(left[part], right, preferred_element_type=jnp.float32)
            ready[slot, part] = (found * scale).astype(jnp.bfloat16)

    @pl.when(second == 0)
    def _():
        multiply(whole[tile, f])

    @pl.when(second == 1)
    def _():
        multiply(theirs[tile, f])

    store(slot).start()

    @pl.when(count == per * pl.num_programs(1) - 1)
    def _():
        for at in range(min(slots, per * 2 * splits)):
            store(at).wait()


def products(spots, whole, theirs, near, far, start, total, target, scale):
    splits, per, depth, width = whole.shape
    rows, chans = near.shape[2], splits * width
    slots = 4
    operands = [whole, theirs, near, far]
    in_specs = [pl.BlockSpec(memory_space=pltpu.VMEM)] * 2
    in_specs += [pl.BlockSpec(memory_space=pl.ANY)] * 2
    args = [spots, *operands]
    aliases = {}
    if target is not None:
        in_specs.append(pl.BlockSpec(memory_space=pl.ANY))
        aliases = {len(args): 0}
        args.append(target)
    return pl.pallas_call(
        functools.partial(products_kernel, scale, start),
        grid_spec=pltpu.PrefetchScalarGridSpec(
            num_scalar_prefetch=1,
            grid=(per, 2 * splits),
            in_specs=in_specs,
            out_specs=pl.BlockSpec(memory_space=pl.ANY),
            scratch_shapes=[
                pltpu.VMEM((depth, rows), jnp.bfloat16),
                pltpu.VMEM((2, rows, depth), jnp.bfloat16),
                pltpu.VMEM((slots, 2, rows, width), jnp.bfloat16),
                pltpu.SemaphoreType.DMA((slots,)),
                pltpu.SemaphoreType.DMA,
            ],
        ),
        out_shape=jax.ShapeDtypeStruct((2, total, rows, 2 * chans), jnp.bfloat16),
        input_output_aliases=aliases,
        compiler_params=pltpu.CompilerParams(vmem_limit_bytes=VMEM_LIMIT),
        cost_estimate=pl.CostEstimate(
            flops=8 * per * rows * depth * chans,
            bytes_accessed=8 * per * rows * chans,
            transcendentals=0,
        ),
        name="products",
    )(*args)


def square_body(raw_traces, window_offsets, dead_channels):
    windows = raw_traces.shape[0]
    t, r, c = lax.axis_index("tm"), lax.axis_index("row"), lax.axis_index("col")
    scale = 1.0 / (SHARES * windows)
    axes = ("tm", "row", "col")

    def moves(rule):
        def place(z, a, b):
            return (z * 2 + a) * 2 + b

        every = [(z, a, b) for z in range(SHARES) for a in range(2) for b in range(2)]
        return [(place(*at), place(*rule(*at))) for at in every]

    def turned(d):
        return moves(lambda z, a, b: (z ^ d, b, a))

    def apart(d):
        return moves(lambda z, a, b: (z ^ d, a, b))

    def across(z, a, b):
        return (z, a, 1 - b) if (a == z % 2) == (b == z // 2) else (z, 1 - a, b)

    def slanted(z, a, b):
        return (z, 1 - a, 1 - b) if a == z % 2 else (z, 1 - a, b)

    def between(z, a, b):
        return (3 - z, a, b) if z in (1, 2) else (z, 1 - a, b)

    def between_turned(z, a, b):
        return (3 - z, b, a) if z in (1, 2) else (z, 1 - a, b)

    def partner(z, a, b):
        return z, 1 - a, b

    home = (c == t // 2).astype(jnp.int32)
    holder = (r == t % 2).astype(jnp.int32)
    spots = jnp.stack([r, (1 - home) * 2 + 1 - holder]).astype(jnp.int32)

    inner = (t == 1) | (t == 2)

    def share(block, turn, forward):
        move = turned if turn else apart
        second = lax.ppermute(block, axes, move(2))
        first = lax.ppermute(block, axes, move(1))
        if not forward:
            return first, second, lax.ppermute(block, axes, move(3))
        middle = lax.ppermute(block, axes, moves(between_turned if turn else between))
        passed = lax.ppermute(second, axes, apart(1))
        return first, second, jnp.where(inner, middle, passed)

    leading, every = spectra(raw_traces, window_offsets, dead_channels, SIZES[0], 2)
    here_all = lax.ppermute(every, axes, turned(0))
    result, late, start = None, None, 0
    for size, forward in zip(SIZES, FORWARD):
        here = here_all[:, start : start + size]
        pieces = share(leading if start == 0 else here, start == 0, forward)
        whole = jnp.concatenate([here, *pieces], axis=2)
        near = lax.ppermute(whole[r], axes, moves(across))
        far = lax.ppermute(whole[1 - r], axes, moves(slanted))
        theirs = lax.ppermute(whole, axes, moves(partner))
        if late is not None:
            result = products(*late, F, result, scale)
        late = (spots, whole, theirs, near, far, start)
        start += size
    return products(*late, F, result, scale)


def contract(left_part, right_part):
    windows_here = left_part.shape[1]
    left_split = left_part.reshape(2, F, windows_here, left_part.shape[2])
    right_split = right_part.reshape(2, F, windows_here, right_part.shape[2])
    real_out = jnp.einsum(
        "cfwi,cfwj->fij", left_split, right_split, preferred_element_type=jnp.float32
    )
    crossed = jnp.stack([right_split[1], -right_split[0]], axis=0)
    imag_out = jnp.einsum("cfwi,cfwj->fij", left_split, crossed, preferred_element_type=jnp.float32)
    return jnp.stack([real_out, imag_out], axis=0)


def gather_body(raw_traces, window_offsets, dead_channels):
    windows, _, chans = raw_traces.shape
    _, whole = spectra(raw_traces, window_offsets, dead_channels, 1, 1)
    whitened = whole.reshape(F, 2, windows, chans).transpose(1, 0, 2, 3)
    whitened = whitened.reshape(2 * F, windows, chans)
    every_chan = lax.all_gather(whitened, ("row", "col"), axis=2, tiled=True)
    row_pair = lax.all_to_all(every_chan, "tm", split_axis=2, concat_axis=1, tiled=True)
    inverse = 1.0 / row_pair.shape[1]
    col_width = every_chan.shape[2] // lax.axis_size("col")
    col_block = lax.dynamic_slice_in_dim(
        every_chan, lax.axis_index("col") * col_width, col_width, 2
    )
    half_rows = row_pair.shape[2] // lax.axis_size("row")
    row_block = lax.dynamic_slice_in_dim(row_pair, lax.axis_index("row") * half_rows, half_rows, 2)
    total = contract(row_block, lax.all_gather(col_block, "tm", axis=1, tiled=True))
    return (total * inverse).astype(jnp.bfloat16)


def solution(mesh):
    sizes = mesh.shape
    square = sizes["tm"] == SHARES and sizes["row"] == 2 and sizes["col"] == 2
    in_specs = (P("tm", None, ("groups", "row", "col")), P(("groups", "tm")), P("groups"))
    out_specs = P(None, None, ("groups", "tm", "row"), "col")
    return jax.shard_map(
        square_body if square else gather_body,
        mesh=mesh,
        in_specs=in_specs,
        out_specs=out_specs,
        check_vma=False,
    )
```

time: 79.9 us -> 66.4 us (0.83)
  the two profiles are of different devices: /device:TPU:0 before, /device:TPU:1 now
where the time goes in v3:
time: 66.4 us; the launch traced here: 66.2 us
  waiting for transfers between devices  23.6 us (36%)
  Pallas kernels  22.6 us (34%)
  starting transfers between devices  16.2 us (24%)
  local copies, waits for them, and re-layouts  3.44 us (5%)
    pallas_call x2, Pallas kernels, products(): pl.pallas_call(functools.partial(products_kernel, scale, start), grid_spe...  18 us
    ppermute x2, waiting for transfers between devices, share(): second = lax.ppermute(block, axes, move(2))  12.9 us
    ppermute x1, waiting for transfers between devices, share(): return (first, second, lax.ppermute(block, axes, move(3)))  4.99 us
    pallas_call x1, Pallas kernels, spectra(): pl.pallas_call(spectra_kernel, in_specs=[pl.BlockSpec(memory_space=pltpu....  4.68 us
    ppermute x2, waiting for transfers between devices, square_body(): near = lax.ppermute(whole[r], axes, moves(across))  4.53 us
    ppermute x1, starting transfers between devices, square_body(): here_all = lax.ppermute(every, axes, turned(0))  4.51 us
    ppermute x1, starting transfers between devices, share(): return (first, second, lax.ppermute(block, axes, move(3)))  3.13 us
    ppermute x2, starting transfers between devices, share(): first = lax.ppermute(block, axes, move(1))  2.96 us
  transfers between devices with their start and end apart: 14, of which 5 were waited for; matrix products, arithmetic and copies ran while one was open for 3% of the time, Pallas kernels for 14%

profile of v3, /device:TPU:1, one launch (start us, length us, event | category | flops | bytes accessed | tf_op | source)
XLA Modules:
  0.0 66.2 jit_solution(2625079073712105810)
XLA Ops:
  0.0 4.7 %spectra.1 = (bf16[2,2,32,640]{3,2,1,0:T(8,128)(2,1)}, bf16[2,4,32,640]{3,2,1,0:T(8,128)(2,1)}) custom-call(s32[1,16]{1,0:T(1,128)} %bitcast.12, f32[16,256]{1,0:T(8,128)} %constant.41.clone.table_in, s32[1,128]{1,0:T(1,128)} %bitcast.13, bf16[16,144,1280]{2,1,0:T(8,128)(2,1)} %raw_in.1), custom_call_target="tpu_custom_call" | custom-call | flops 94371840 | bytes 5898240 | tf_op jit(solution)/shard_map/spectra/pallas_call | solution.py:95
  4.7 4.5 %collective-permute-start = (bf16[2,4,32,640]{3,2,1,0:T(8,128)(2,1)}, bf16[2,4,32,640]{3,2,1,0:T(8,128)(2,1)S(1)}, u32[]{:S(2)}, u32[]{:S(2)}) collective-permute-start(bf16[2,4,32,640]{3,2,1,0:T(8,128)(2,1)} %get-tuple-element.7), channel_id=1, source_target_pairs={{0,0},{1,2},{2,1},{3,3},{4,4},{5,6},{6,5},{7,7},{8,8},{9,10},{10,9... | collective-permute-start | bytes 983048 | tf_op jit(solution)/shard_map/ppermute | solution.py:275
  9.2 2.1 %collective-permute-start.8 = (bf16[2,2,32,640]{3,2,1,0:T(8,128)(2,1)}, bf16[2,2,32,640]{3,2,1,0:T(8,128)(2,1)S(1)}, u32[]{:S(2)}, u32[]{:S(2)}) collective-permute-start(bf16[2,2,32,640]{3,2,1,0:T(8,128)(2,1)} %get-tuple-element.8), channel_id=1, source_target_pairs={{0,8},{1,10},{2,9},{3,11},{4,12},{5,14},{6,13},{7,15},{8,0},{9,2},... | collective-permute-start | bytes 491528 | tf_op jit(solution)/shard_map/ppermute | solution.py:266
  11.3 0.0 collective-permute-start.9
  11.3 2.7 %collective-permute-start.7 = (bf16[2,2,32,640]{3,2,1,0:T(8,128)(2,1)}, bf16[2,2,32,640]{3,2,1,0:T(8,128)(2,1)S(1)}, u32[]{:S(2)}, u32[]{:S(2)}) collective-permute-start(bf16[2,2,32,640]{3,2,1,0:T(8,128)(2,1)} %get-tuple-element.8), channel_id=1, source_target_pairs={{0,4},{1,6},{2,5},{3,7},{4,0},{5,2},{6,1},{7,3},{8,12},{9,14},{10,... | collective-permute-start | bytes 491528 | tf_op jit(solution)/shard_map/ppermute | solution.py:267
  14.1 5.7 %collective-permute-done.8 = bf16[2,2,32,640]{3,2,1,0:T(8,128)(2,1)S(1)} collective-permute-done((bf16[2,2,32,640]{3,2,1,0:T(8,128)(2,1)}, bf16[2,2,32,640]{3,2,1,0:T(8,128)(2,1)S(1)}, u32[]{:S(2)}, u32[]{:S(2)}) %collective-permute-start.8) | collective-permute-done | bytes 163872 | tf_op jit(solution)/shard_map/ppermute | solution.py:266
  19.8 0.0 collective-permute-start.10
  19.8 0.0 collective-permute-done
  19.8 3.1 %collective-permute-start.3 = (bf16[2,2,32,640]{3,2,1,0:T(8,128)(2,1)S(1)}, bf16[2,2,32,640]{3,2,1,0:T(8,128)(2,1)S(1)}, u32[]{:S(2)}, u32[]{:S(2)}) collective-permute-start(bf16[2,2,32,640]{3,2,1,0:T(8,128)(2,1)S(1)} %get-tuple-element.14), channel_id=1, source_target_pairs={{0,12},{1,13},{2,14},{3,15},{4,8},{5,9},{6,10},{7,11},{8,4},{9,5},... | collective-permute-start | bytes 491528 | tf_op jit(solution)/shard_map/ppermute | solution.py:269
  23.0 0.4 collective-permute-start.2
  23.3 0.0 collective-permute-done.9
  23.3 0.2 collective-permute-start.1
  23.6 1.1 %collective-permute-done.10 = bf16[2,2,32,640]{3,2,1,0:T(8,128)(2,1)S(1)} collective-permute-done((bf16[2,2,32,640]{3,2,1,0:T(8,128)(2,1)S(1)}, bf16[2,2,32,640]{3,2,1,0:T(8,128)(2,1)S(1)}, u32[]{:S(2)}, u32[]{:S(2)}) %collective-permute-start.10) | collective-permute-done | bytes 163872 | tf_op jit(solution)/shard_map/ppermute | solution.py:271
  24.7 0.0 collective-permute-done.7
  24.7 0.1 pad_maximum_fusion.1.whole
  24.7 0.2 collective-permute-start.11
  25.0 0.8 %dynamic-slice_bitcast_fusion = (bf16[2,128,640]{2,1,0:T(8,128)(2,1)S(1)}, bf16[2,128,640]{2,1,0:T(8,128)(2,1)}) fusion(bf16[2,2,128,640]{3,2,1,0:T(8,128)(2,1)S(1)} %pad_maximum_fusion.1.whole, s32[]{:T(128)S(6)} %select_n.30, s32[]{:T(128)S(6)} %select_n.29), kind=kLoop, calls=%fused_computation.2 | loop fusion | bytes 1310728 | tf_op jit(solution)/shard_map/squeeze | solution.py:282
  25.7 0.4 collective-permute-start.13
  26.1 5.0 %collective-permute-done.3 = bf16[2,2,32,640]{3,2,1,0:T(8,128)(2,1)S(1)} collective-permute-done((bf16[2,2,32,640]{3,2,1,0:T(8,128)(2,1)S(1)}, bf16[2,2,32,640]{3,2,1,0:T(8,128)(2,1)S(1)}, u32[]{:S(2)}, u32[]{:S(2)}) %collective-permute-start.3) | collective-permute-done | bytes 163872 | tf_op jit(solution)/shard_map/ppermute | solution.py:269
  31.1 7.2 %collective-permute-done.2 = bf16[2,2,32,640]{3,2,1,0:T(8,128)(2,1)S(1)} collective-permute-done((bf16[2,2,32,640]{3,2,1,0:T(8,128)(2,1)S(1)}, bf16[2,2,32,640]{3,2,1,0:T(8,128)(2,1)S(1)}, u32[]{:S(2)}, u32[]{:S(2)}) %collective-permute-start.2) | collective-permute-done | bytes 163872 | tf_op jit(solution)/shard_map/ppermute | solution.py:266
  38.3 0.0 collective-permute-done.1
  38.3 0.1 pad_maximum_fusion.whole
  38.3 0.7 %collective-permute-start.4 = (bf16[2,2,128,640]{3,2,1,0:T(8,128)(2,1)S(1)}, bf16[2,2,128,640]{3,2,1,0:T(8,128)(2,1)S(1)}, u32[]{:S(2)}, u32[]{:S(2)}) collective-permute-start(bf16[2,2,128,640]{3,2,1,0:T(8,128)(2,1)S(1)} %pad_maximum_fusion.whole), channel_id=1, source_target_pairs={{0,2},{1,3},{2,0},{3,1},{4,6},{5,7},{6,4},{7,5},{8,10},{9,11},{10,... | collective-permute-start | bytes 1966088 | tf_op jit(solution)/shard_map/ppermute | solution.py:283
  39.1 0.1 collective-permute-start.12
  39.2 0.9 %dynamic-slice_bitcast_fusion.2 = (bf16[2,128,640]{2,1,0:T(8,128)(2,1)}, bf16[2,128,640]{2,1,0:T(8,128)(2,1)}) fusion(bf16[2,2,128,640]{3,2,1,0:T(8,128)(2,1)S(1)} %pad_maximum_fusion.whole, s32[]{:T(128)S(6)} %select_n.30, s32[]{:T(128)S(6)} %select_n.29), kind=kLoop, calls=%fused_computation.4 | loop fusion | bytes 1310728 | tf_op jit(solution)/shard_map/squeeze | solution.py:282
  40.1 0.0 collective-permute-start.6
  40.1 0.0 collective-permute-done.13.far
  40.1 0.0 copy-start
  40.1 0.7 %copy-done = bf16[2,128,640]{2,1,0:T(8,128)(2,1)} copy-done((bf16[2,128,640]{2,1,0:T(8,128)(2,1)}, bf16[2,128,640]{2,1,0:T(8,128)(2,1)S(1)}, u32[]{:S(2)}) %copy-start) | copy-done | bytes 327704
  40.8 1.8 %collective-permute-start.5 = (bf16[2,128,640]{2,1,0:T(8,128)(2,1)}, bf16[2,128,640]{2,1,0:T(8,128)(2,1)S(1)}, u32[]{:S(2)}, u32[]{:S(2)}) collective-permute-start(bf16[2,128,640]{2,1,0:T(8,128)(2,1)} %get-tuple-element.12), channel_id=1, source_target_pairs={{0,1},{1,3},{2,0},{3,2},{4,6},{5,4},{6,7},{7,5},{8,10},{9,8},{10,1... | collective-permute-start | bytes 983048 | tf_op jit(solution)/shard_map/ppermute | solution.py:281
  42.6 0.1 pad_add_fusion.spots
  42.7 4.5 %collective-permute-done.12.near = bf16[2,128,640]{2,1,0:T(8,128)(2,1)} collective-permute-done((bf16[2,128,640]{2,1,0:T(8,128)(2,1)}, bf16[2,128,640]{2,1,0:T(8,128)(2,1)}, u32[]{:S(2)}, u32[]{:S(2)}) %collective-permute-start.12) | collective-permute-done | bytes 327712 | tf_op jit(solution)/shard_map/ppermute | solution.py:281
  47.2 0.0 collective-permute-done.11.theirs
  47.2 0.0 copy-start.1
  47.2 1.0 %copy-done.1 = bf16[2,128,640]{2,1,0:T(8,128)(2,1)S(1)} copy-done((bf16[2,128,640]{2,1,0:T(8,128)(2,1)S(1)}, bf16[2,128,640]{2,1,0:T(8,128)(2,1)}, u32[]{:S(2)}) %copy-start.1) | copy-done | bytes 327704
  48.2 9.0 %products.2.rest_0_ = bf16[2,4,640,2560]{3,2,1,0:T(8,128)(2,1)} custom-call(s32[2]{0:T(128)S(1)} %pad_add_fusion.spots, bf16[2,2,128,640]{3,2,1,0:T(8,128)(2,1)S(1)} %pad_maximum_fusion.1.whole, bf16[2,2,128,640]{3,2,1,0:T(8,128)(2,1)S(1)} %collective-permute-done.11.theirs, bf16[2,128,640]{2,1,0:T(8,128)(2,1)} %collective-permute-done.12.near, ...), custom_call_target="tpu_custom_call" | custom-call | flops 1677721600 | bytes 13107200 | tf_op jit(solution)/shard_map/products/pallas_call | solution.py:197
  57.2 0.0 collective-permute-done.6.far
  57.2 0.0 collective-permute-done.5.near
  57.2 0.0 collective-permute-done.4.theirs
  57.2 9.0 %products.3 = bf16[2,4,640,2560]{3,2,1,0:T(8,128)(2,1)} custom-call(s32[2]{0:T(128)S(1)} %pad_add_fusion.spots, bf16[2,2,128,640]{3,2,1,0:T(8,128)(2,1)S(1)} %pad_maximum_fusion.whole, bf16[2,2,128,640]{3,2,1,0:T(8,128)(2,1)S(1)} %collective-permute-done.4.theirs, ...), custom_call_target="tpu_custom_call", output_to_operand_aliasing={{}: (5, {})} | custom-call | flops 1677721600 | bytes 13107200 | tf_op jit(solution)/shard_map/products/pallas_call | solution.py:197
  (2 shorter events, 0.1 us)
Async XLA Ops:
  4.7 15.1 %collective-permute-start = (bf16[2,4,32,640]{3,2,1,0:T(8,128)(2,1)}, bf16[2,4,32,640]{3,2,1,0:T(8,128)(2,1)S(1)}, u32[]{:S(2)}, u32[]{:S(2)}) collective-permute-start(bf16[2,4,32,640]{3,2,1,0:T(8,128)(2,1)} %get-tuple-element.7), channel_id=1, source_target_pairs={{0,0},{1,2},{2,1},{3,3},{4,4},{5,6},{6,5},{7,7},{8,8},{9,10},{10,9... | collective-permute-start | bytes 983048 | tf_op jit(solution)/shard_map/ppermute | solution.py:275
  9.2 10.6 %collective-permute-start.8 = (bf16[2,2,32,640]{3,2,1,0:T(8,128)(2,1)}, bf16[2,2,32,640]{3,2,1,0:T(8,128)(2,1)S(1)}, u32[]{:S(2)}, u32[]{:S(2)}) collective-permute-start(bf16[2,2,32,640]{3,2,1,0:T(8,128)(2,1)} %get-tuple-element.8), channel_id=1, source_target_pairs={{0,8},{1,10},{2,9},{3,11},{4,12},{5,14},{6,13},{7,15},{8,0},{9,2},... | collective-permute-start | bytes 491528 | tf_op jit(solution)/shard_map/ppermute | solution.py:266
  11.3 12.0 %collective-permute-start.9 = (bf16[2,2,32,640]{3,2,1,0:T(8,128)(2,1)}, bf16[2,2,32,640]{3,2,1,0:T(8,128)(2,1)S(1)}, u32[]{:S(2)}, u32[]{:S(2)}) collective-permute-start(bf16[2,2,32,640]{3,2,1,0:T(8,128)(2,1)} %get-tuple-element.8), channel_id=1, source_target_pairs={{0,2},{1,3},{2,0},{3,1},{4,8},{5,10},{6,9},{7,11},{8,4},{9,6},{10,... | collective-permute-start | bytes 491528 | tf_op jit(solution)/shard_map/ppermute | solution.py:270
  11.3 13.4 %collective-permute-start.7 = (bf16[2,2,32,640]{3,2,1,0:T(8,128)(2,1)}, bf16[2,2,32,640]{3,2,1,0:T(8,128)(2,1)S(1)}, u32[]{:S(2)}, u32[]{:S(2)}) collective-permute-start(bf16[2,2,32,640]{3,2,1,0:T(8,128)(2,1)} %get-tuple-element.8), channel_id=1, source_target_pairs={{0,4},{1,6},{2,5},{3,7},{4,0},{5,2},{6,1},{7,3},{8,12},{9,14},{10,... | collective-permute-start | bytes 491528 | tf_op jit(solution)/shard_map/ppermute | solution.py:267
  19.8 4.8 %collective-permute-start.10 = (bf16[2,2,32,640]{3,2,1,0:T(8,128)(2,1)S(1)}, bf16[2,2,32,640]{3,2,1,0:T(8,128)(2,1)S(1)}, u32[]{:S(2)}, u32[]{:S(2)}) collective-permute-start(bf16[2,2,32,640]{3,2,1,0:T(8,128)(2,1)S(1)} %collective-permute-done.8), channel_id=1, source_target_pairs={{0,4},{1,5},{2,6},{3,7},{4,0},{5,1},{6,2},{7,3},{8,12},{9,13},{10,... | collective-permute-start | bytes 491528 | tf_op jit(solution)/shard_map/ppermute | solution.py:271
  19.8 11.3 %collective-permute-start.3 = (bf16[2,2,32,640]{3,2,1,0:T(8,128)(2,1)S(1)}, bf16[2,2,32,640]{3,2,1,0:T(8,128)(2,1)S(1)}, u32[]{:S(2)}, u32[]{:S(2)}) collective-permute-start(bf16[2,2,32,640]{3,2,1,0:T(8,128)(2,1)S(1)} %get-tuple-element.14), channel_id=1, source_target_pairs={{0,12},{1,13},{2,14},{3,15},{4,8},{5,9},{6,10},{7,11},{8,4},{9,5},... | collective-permute-start | bytes 491528 | tf_op jit(solution)/shard_map/ppermute | solution.py:269
  23.0 15.3 %collective-permute-start.2 = (bf16[2,2,32,640]{3,2,1,0:T(8,128)(2,1)S(1)}, bf16[2,2,32,640]{3,2,1,0:T(8,128)(2,1)S(1)}, u32[]{:S(2)}, u32[]{:S(2)}) collective-permute-start(bf16[2,2,32,640]{3,2,1,0:T(8,128)(2,1)S(1)} %get-tuple-element.14), channel_id=1, source_target_pairs={{0,8},{1,9},{2,10},{3,11},{4,12},{5,13},{6,14},{7,15},{8,0},{9,1},... | collective-permute-start | bytes 491528 | tf_op jit(solution)/shard_map/ppermute | solution.py:266
  23.3 14.9 %collective-permute-start.1 = (bf16[2,2,32,640]{3,2,1,0:T(8,128)(2,1)S(1)}, bf16[2,2,32,640]{3,2,1,0:T(8,128)(2,1)S(1)}, u32[]{:S(2)}, u32[]{:S(2)}) collective-permute-start(bf16[2,2,32,640]{3,2,1,0:T(8,128)(2,1)S(1)} %get-tuple-element.14), channel_id=1, source_target_pairs={{0,4},{1,5},{2,6},{3,7},{4,0},{5,1},{6,2},{7,3},{8,12},{9,13},{10,... | collective-permute-start | bytes 491528 | tf_op jit(solution)/shard_map/ppermute | solution.py:267
  24.7 22.5 %collective-permute-start.11 = (bf16[2,2,128,640]{3,2,1,0:T(8,128)(2,1)S(1)}, bf16[2,2,128,640]{3,2,1,0:T(8,128)(2,1)S(1)}, u32[]{:S(2)}, u32[]{:S(2)}) collective-permute-start(bf16[2,2,128,640]{3,2,1,0:T(8,128)(2,1)S(1)} %pad_maximum_fusion.1.whole), channel_id=1, source_target_pairs={{0,2},{1,3},{2,0},{3,1},{4,6},{5,7},{6,4},{7,5},{8,10},{9,11},{10,... | collective-permute-start | bytes 1966088 | tf_op jit(solution)/shard_map/ppermute | solution.py:283
  25.7 14.4 %collective-permute-start.13 = (bf16[2,128,640]{2,1,0:T(8,128)(2,1)S(1)}, bf16[2,128,640]{2,1,0:T(8,128)(2,1)S(1)}, u32[]{:S(2)}, u32[]{:S(2)}) collective-permute-start(bf16[2,128,640]{2,1,0:T(8,128)(2,1)S(1)} %get-tuple-element.9), channel_id=1, source_target_pairs={{0,3},{1,2},{2,0},{3,1},{4,6},{5,7},{6,5},{7,4},{8,11},{9,10},{10,... | collective-permute-start | bytes 983048 | tf_op jit(solution)/shard_map/ppermute | solution.py:282
  38.3 18.8 %collective-permute-start.4 = (bf16[2,2,128,640]{3,2,1,0:T(8,128)(2,1)S(1)}, bf16[2,2,128,640]{3,2,1,0:T(8,128)(2,1)S(1)}, u32[]{:S(2)}, u32[]{:S(2)}) collective-permute-start(bf16[2,2,128,640]{3,2,1,0:T(8,128)(2,1)S(1)} %pad_maximum_fusion.whole), channel_id=1, source_target_pairs={{0,2},{1,3},{2,0},{3,1},{4,6},{5,7},{6,4},{7,5},{8,10},{9,11},{10,... | collective-permute-start | bytes 1966088 | tf_op jit(solution)/shard_map/ppermute | solution.py:283
  39.1 8.1 %collective-permute-start.12 = (bf16[2,128,640]{2,1,0:T(8,128)(2,1)}, bf16[2,128,640]{2,1,0:T(8,128)(2,1)}, u32[]{:S(2)}, u32[]{:S(2)}) collective-permute-start(bf16[2,128,640]{2,1,0:T(8,128)(2,1)} %get-tuple-element.10), channel_id=1, source_target_pairs={{0,1},{1,3},{2,0},{3,2},{4,6},{5,4},{6,7},{7,5},{8,10},{9,8},{10,1... | collective-permute-start | bytes 983048 | tf_op jit(solution)/shard_map/ppermute | solution.py:281
  40.1 17.1 %collective-permute-start.6 = (bf16[2,128,640]{2,1,0:T(8,128)(2,1)}, bf16[2,128,640]{2,1,0:T(8,128)(2,1)S(1)}, u32[]{:S(2)}, u32[]{:S(2)}) collective-permute-start(bf16[2,128,640]{2,1,0:T(8,128)(2,1)} %get-tuple-element.11), channel_id=1, source_target_pairs={{0,3},{1,2},{2,0},{3,1},{4,6},{5,7},{6,5},{7,4},{8,11},{9,10},{10,... | collective-permute-start | bytes 983048 | tf_op jit(solution)/shard_map/ppermute | solution.py:282
  40.1 0.7 %copy-start = (bf16[2,128,640]{2,1,0:T(8,128)(2,1)}, bf16[2,128,640]{2,1,0:T(8,128)(2,1)S(1)}, u32[]{:S(2)}) copy-start(bf16[2,128,640]{2,1,0:T(8,128)(2,1)S(1)} %collective-permute-done.13.far) | copy-start | bytes 983044
  40.8 16.3 %collective-permute-start.5 = (bf16[2,128,640]{2,1,0:T(8,128)(2,1)}, bf16[2,128,640]{2,1,0:T(8,128)(2,1)S(1)}, u32[]{:S(2)}, u32[]{:S(2)}) collective-permute-start(bf16[2,128,640]{2,1,0:T(8,128)(2,1)} %get-tuple-element.12), channel_id=1, source_target_pairs={{0,1},{1,3},{2,0},{3,2},{4,6},{5,4},{6,7},{7,5},{8,10},{9,8},{10,1... | collective-permute-start | bytes 983048 | tf_op jit(solution)/shard_map/ppermute | solution.py:281
  47.2 1.0 %copy-start.1 = (bf16[2,128,640]{2,1,0:T(8,128)(2,1)S(1)}, bf16[2,128,640]{2,1,0:T(8,128)(2,1)}, u32[]{:S(2)}) copy-start(bf16[2,128,640]{2,1,0:T(8,128)(2,1)} %copy-done) | copy-start | bytes 983044

commit v4 on v3

--- a/solution.py
+++ b/solution.py
@@ -14,7 +14,7 @@
 SHARES = 4
 SIZES = (2, 2)
 FORWARD = (True, False)
-VMEM_LIMIT = 16 * 1024 * 1024
+VMEM_LIMIT = 20 * 1024 * 1024
 SPECTRA_VMEM = 60 * 1024 * 1024
 
 
@@ -121,74 +121,60 @@
 
 
 def products_kernel(scale, start, spots, whole, theirs, near, far, *rest):
-    out, picked, left, ready, sems, pick_sem = rest[-6:]
+    out, picked, left, ready, sems, pick_sems = rest[-6:]
     splits, per, depth, width = whole.shape
-    slots = ready.shape[0]
-    f, step = pl.program_id(0), pl.program_id(1)
-    count = f * pl.num_programs(1) + step
     own, source = spots[0], spots[1]
 
-    @pl.when(step == 0)
-    def _():
-        for case, ref in enumerate((whole.at[own, f], theirs.at[own, f], near.at[f], far.at[f])):
-
-            @pl.when(source == case)
-            def _():
-                pltpu.make_async_copy(ref, picked, pick_sem).start()
-
-        pltpu.make_async_copy(near.at[f], picked, pick_sem).wait()
+    for case, refs in enumerate((whole.at[own], theirs.at[own], near, far)):
+
+        @pl.when(source == case)
+        def _():
+            for f in range(per):
+                pltpu.make_async_copy(refs.at[f], picked.at[f], pick_sems.at[f]).start()
+
+    def turn(f):
+        pltpu.make_async_copy(near.at[f], picked.at[f], pick_sems.at[f]).wait()
         piece = depth // SHARES
         for p in range(SHARES):
             at = slice(p * piece, (p + 1) * piece)
-            real = picked[p * piece : p * piece + piece // 2, :].astype(jnp.float32)
-            imag = picked[p * piece + piece // 2 : (p + 1) * piece, :].astype(jnp.float32)
-            left[0, :, at] = jnp.concatenate([real, imag], axis=0).T.astype(jnp.bfloat16)
-            left[1, :, at] = jnp.concatenate([-imag, real], axis=0).T.astype(jnp.bfloat16)
-
-    second = step // splits
-    tile = step - second * splits
-    slot = lax.rem(count, slots)
-    side = own + second - 2 * own * second
-    places = pl.ds(pl.multiple_of((side * splits + tile) * width, 128), width)
-
-    def store(at):
-        return pltpu.make_async_copy(
-            ready.at[at], out.at[:, start + f, :, places], sems.at[at]
-        )
-
-    @pl.when(count >= slots)
-    def _():
-        store(slot).wait()
-
-    def multiply(right):
-        for part in range(2):
-            found = jnp.dot(left[part], right, preferred_element_type=jnp.float32)
-            ready[slot, part] = (found * scale).astype(jnp.bfloat16)
-
-    @pl.when(second == 0)
-    def _():
-        multiply(whole[tile, f])
-
-    @pl.when(second == 1)
-    def _():
-        multiply(theirs[tile, f])
-
-    store(slot).start()
-
-    @pl.when(count == per * pl.num_programs(1) - 1)
-    def _():
-        for at in range(min(slots, per * 2 * splits)):
-            store(at).wait()
+            middle = p * piece + piece // 2
+            real = picked[f, p * piece : middle, :].astype(jnp.float32)
+            imag = picked[f, middle : (p + 1) * piece, :].astype(jnp.float32)
+            left[f, 0, :, at] = jnp.concatenate([real, imag], axis=0).T.astype(jnp.bfloat16)
+            left[f, 1, :, at] = jnp.concatenate([-imag, real], axis=0).T.astype(jnp.bfloat16)
+
+    copies = []
+    turn(0)
+    for f in range(per):
+        for second, source_ref in enumerate((whole, theirs)):
+            side = own + second - 2 * own * second
+            for tile in range(splits):
+                slot = (f * 2 + second) * splits + tile
+                right = source_ref[tile, f]
+                for part in range(2):
+                    found = jnp.dot(left[f, part], right, preferred_element_type=jnp.float32)
+                    ready[slot, part] = (found * scale).astype(jnp.bfloat16)
+                places = pl.ds(pl.multiple_of((side * splits + tile) * width, 128), width)
+                copies.append(
+                    pltpu.make_async_copy(
+                        ready.at[slot], out.at[:, start + f, :, places], sems.at[slot]
+                    )
+                )
+                copies[-1].start()
+                if slot == f * 2 * splits and f + 1 < per:
+                    turn(f + 1)
+    for copy in copies:
+        copy.wait()
 
 
 def products(spots, whole, theirs, near, far, start, total, target, scale):
     splits, per, depth, width = whole.shape
-    rows, chans = near.shape[2], splits * width
-    slots = 4
-    operands = [whole, theirs, near, far]
-    in_specs = [pl.BlockSpec(memory_space=pltpu.VMEM)] * 2
+    chans = splits * width
+    slots = per * 2 * splits
+    in_specs = [pl.BlockSpec(memory_space=pltpu.SMEM)]
+    in_specs += [pl.BlockSpec(memory_space=pltpu.VMEM)] * 2
     in_specs += [pl.BlockSpec(memory_space=pl.ANY)] * 2
-    args = [spots, *operands]
+    args = [spots, whole, theirs, near, far]
     aliases = {}
     if target is not None:
         in_specs.append(pl.BlockSpec(memory_space=pl.ANY))
@@ -196,25 +182,21 @@
         args.append(target)
     return pl.pallas_call(
         functools.partial(products_kernel, scale, start),
-        grid_spec=pltpu.PrefetchScalarGridSpec(
-            num_scalar_prefetch=1,
-            grid=(per, 2 * splits),
-            in_specs=in_specs,
-            out_specs=pl.BlockSpec(memory_space=pl.ANY),
-            scratch_shapes=[
-                pltpu.VMEM((depth, rows), jnp.bfloat16),
-                pltpu.VMEM((2, rows, depth), jnp.bfloat16),
-                pltpu.VMEM((slots, 2, rows, width), jnp.bfloat16),
-                pltpu.SemaphoreType.DMA((slots,)),
-                pltpu.SemaphoreType.DMA,
-            ],
-        ),
-        out_shape=jax.ShapeDtypeStruct((2, total, rows, 2 * chans), jnp.bfloat16),
+        in_specs=in_specs,
+        out_specs=pl.BlockSpec(memory_space=pl.ANY),
+        scratch_shapes=[
+            pltpu.VMEM((per, depth, width), jnp.bfloat16),
+            pltpu.VMEM((per, 2, width, depth), jnp.bfloat16),
+            pltpu.VMEM((slots, 2, width, width), jnp.bfloat16),
+            pltpu.SemaphoreType.DMA((slots,)),
+            pltpu.SemaphoreType.DMA((per,)),
+        ],
+        out_shape=jax.ShapeDtypeStruct((2, total, width, 2 * chans), jnp.bfloat16),
         input_output_aliases=aliases,
         compiler_params=pltpu.CompilerParams(vmem_limit_bytes=VMEM_LIMIT),
         cost_estimate=pl.CostEstimate(
-            flops=8 * per * rows * depth * chans,
-            bytes_accessed=8 * per * rows * chans,
+            flops=8 * per * width * depth * chans,
+            bytes_accessed=8 * per * width * chans,
             transcendentals=0,
         ),
         name="products",
@@ -255,9 +237,8 @@
     def partner(z, a, b):
         return z, 1 - a, b
 
-    home = (c == t // 2).astype(jnp.int32)
-    holder = (r == t % 2).astype(jnp.int32)
-    spots = jnp.stack([r, (1 - home) * 2 + 1 - holder]).astype(jnp.int32)
+    source = jnp.where(c == t // 2, jnp.where(r == t % 2, 0, 1), jnp.where(r == t % 2, 2, 3))
+    spots = jnp.stack([r, source]).astype(jnp.int32)
 
     inner = (t == 1) | (t == 2)
 
@@ -283,7 +264,7 @@
         theirs = lax.ppermute(whole, axes, moves(partner))
         if late is not None:
             result = products(*late, F, result, scale)
-        late = (spots, whole, theirs, near, far, start)
+        late = [spots, whole, theirs, near, far, start]
         start += size
     return products(*late, F, result, scale)
 

time: 66.4 us -> 64.6 us (0.973)
  Pallas kernels: 22.6 us -> 20.7 us
    pallas_call x2, Pallas kernels: 18 us -> 16 us  [products(): pl.pallas_call(functools.partial(products_kernel, scale, start), in_specs...]
  transfers between devices with their start and end apart: 14 -> 14, of which waited for: 5 -> 5; matrix products, arithmetic and copies ran while one was open for 3% -> 3% of each run, Pallas kernels for 14% -> 12%
where the time goes in v4:
time: 64.6 us; the launch traced here: 64.4 us
  waiting for transfers between devices  23.6 us (37%)
  Pallas kernels  20.7 us (32%)
  starting transfers between devices  16.2 us (25%)
  local copies, waits for them, and re-layouts  3.44 us (5%)
    pallas_call x2, Pallas kernels, products(): pl.pallas_call(functools.partial(products_kernel, scale, start), in_specs...  16 us
    ppermute x2, waiting for transfers between devices, share(): second = lax.ppermute(block, axes, move(2))  12.9 us
    ppermute x1, waiting for transfers between devices, share(): return (first, second, lax.ppermute(block, axes, move(3)))  4.99 us
    pallas_call x1, Pallas kernels, spectra(): pl.pallas_call(spectra_kernel, in_specs=[pl.BlockSpec(memory_space=pltpu....  4.68 us
    ppermute x2, waiting for transfers between devices, square_body(): near = lax.ppermute(whole[r], axes, moves(across))  4.53 us
    ppermute x1, starting transfers between devices, square_body(): here_all = lax.ppermute(every, axes, turned(0))  4.51 us
    ppermute x1, starting transfers between devices, share(): return (first, second, lax.ppermute(block, axes, move(3)))  3.13 us
    ppermute x2, starting transfers between devices, share(): first = lax.ppermute(block, axes, move(1))  2.96 us
  transfers between devices with their start and end apart: 14, of which 5 were waited for; matrix products, arithmetic and copies ran while one was open for 3% of the time, Pallas kernels for 12%

profile of v4, /device:TPU:1, one launch (start us, length us, event | category | flops | bytes accessed | tf_op | source)
XLA Modules:
  0.0 64.4 jit_solution(6572081179148329106)
XLA Ops:
  0.0 4.7 %spectra.1 = (bf16[2,2,32,640]{3,2,1,0:T(8,128)(2,1)}, bf16[2,4,32,640]{3,2,1,0:T(8,128)(2,1)}) custom-call(s32[1,16]{1,0:T(1,128)} %bitcast.12, f32[16,256]{1,0:T(8,128)} %constant.44.clone.table_in, s32[1,128]{1,0:T(1,128)} %bitcast.13, bf16[16,144,1280]{2,1,0:T(8,128)(2,1)} %raw_in.1), custom_call_target="tpu_custom_call" | custom-call | flops 94371840 | bytes 5898240 | tf_op jit(solution)/shard_map/spectra/pallas_call | solution.py:95
  4.7 4.5 %collective-permute-start = (bf16[2,4,32,640]{3,2,1,0:T(8,128)(2,1)}, bf16[2,4,32,640]{3,2,1,0:T(8,128)(2,1)S(1)}, u32[]{:S(2)}, u32[]{:S(2)}) collective-permute-start(bf16[2,4,32,640]{3,2,1,0:T(8,128)(2,1)} %get-tuple-element.7), channel_id=1, source_target_pairs={{0,0},{1,2},{2,1},{3,3},{4,4},{5,6},{6,5},{7,7},{8,8},{9,10},{10,9... | collective-permute-start | bytes 983048 | tf_op jit(solution)/shard_map/ppermute | solution.py:256
  9.2 2.1 %collective-permute-start.8 = (bf16[2,2,32,640]{3,2,1,0:T(8,128)(2,1)}, bf16[2,2,32,640]{3,2,1,0:T(8,128)(2,1)S(1)}, u32[]{:S(2)}, u32[]{:S(2)}) collective-permute-start(bf16[2,2,32,640]{3,2,1,0:T(8,128)(2,1)} %get-tuple-element.8), channel_id=1, source_target_pairs={{0,8},{1,10},{2,9},{3,11},{4,12},{5,14},{6,13},{7,15},{8,0},{9,2},... | collective-permute-start | bytes 491528 | tf_op jit(solution)/shard_map/ppermute | solution.py:247
  11.3 0.0 collective-permute-start.9
  11.3 2.7 %collective-permute-start.7 = (bf16[2,2,32,640]{3,2,1,0:T(8,128)(2,1)}, bf16[2,2,32,640]{3,2,1,0:T(8,128)(2,1)S(1)}, u32[]{:S(2)}, u32[]{:S(2)}) collective-permute-start(bf16[2,2,32,640]{3,2,1,0:T(8,128)(2,1)} %get-tuple-element.8), channel_id=1, source_target_pairs={{0,4},{1,6},{2,5},{3,7},{4,0},{5,2},{6,1},{7,3},{8,12},{9,14},{10,... | collective-permute-start | bytes 491528 | tf_op jit(solution)/shard_map/ppermute | solution.py:248
  14.1 5.7 %collective-permute-done.8 = bf16[2,2,32,640]{3,2,1,0:T(8,128)(2,1)S(1)} collective-permute-done((bf16[2,2,32,640]{3,2,1,0:T(8,128)(2,1)}, bf16[2,2,32,640]{3,2,1,0:T(8,128)(2,1)S(1)}, u32[]{:S(2)}, u32[]{:S(2)}) %collective-permute-start.8) | collective-permute-done | bytes 163872 | tf_op jit(solution)/shard_map/ppermute | solution.py:247
  19.8 0.0 collective-permute-start.10
  19.8 0.0 collective-permute-done
  19.8 3.1 %collective-permute-start.3 = (bf16[2,2,32,640]{3,2,1,0:T(8,128)(2,1)S(1)}, bf16[2,2,32,640]{3,2,1,0:T(8,128)(2,1)S(1)}, u32[]{:S(2)}, u32[]{:S(2)}) collective-permute-start(bf16[2,2,32,640]{3,2,1,0:T(8,128)(2,1)S(1)} %get-tuple-element.14), channel_id=1, source_target_pairs={{0,12},{1,13},{2,14},{3,15},{4,8},{5,9},{6,10},{7,11},{8,4},{9,5},... | collective-permute-start | bytes 491528 | tf_op jit(solution)/shard_map/ppermute | solution.py:250
  23.0 0.4 collective-permute-start.2
  23.3 0.0 collective-permute-done.9
  23.3 0.2 collective-permute-start.1
  23.6 1.1 %collective-permute-done.10 = bf16[2,2,32,640]{3,2,1,0:T(8,128)(2,1)S(1)} collective-permute-done((bf16[2,2,32,640]{3,2,1,0:T(8,128)(2,1)S(1)}, bf16[2,2,32,640]{3,2,1,0:T(8,128)(2,1)S(1)}, u32[]{:S(2)}, u32[]{:S(2)}) %collective-permute-start.10) | collective-permute-done | bytes 163872 | tf_op jit(solution)/shard_map/ppermute | solution.py:252
  24.7 0.0 collective-permute-done.7
  24.7 0.1 pad_maximum_fusion.1.whole
  24.7 0.2 collective-permute-start.11
  25.0 0.8 %dynamic-slice_bitcast_fusion = (bf16[2,128,640]{2,1,0:T(8,128)(2,1)S(1)}, bf16[2,128,640]{2,1,0:T(8,128)(2,1)}) fusion(bf16[2,2,128,640]{3,2,1,0:T(8,128)(2,1)S(1)} %pad_maximum_fusion.1.whole, s32[]{:T(128)S(6)} %select_n.46, s32[]{:T(128)S(6)} %select_n.45), kind=kLoop, calls=%fused_computation.2 | loop fusion | bytes 1310728 | tf_op jit(solution)/shard_map/squeeze | solution.py:263
  25.7 0.4 collective-permute-start.13
  26.1 5.0 %collective-permute-done.3 = bf16[2,2,32,640]{3,2,1,0:T(8,128)(2,1)S(1)} collective-permute-done((bf16[2,2,32,640]{3,2,1,0:T(8,128)(2,1)S(1)}, bf16[2,2,32,640]{3,2,1,0:T(8,128)(2,1)S(1)}, u32[]{:S(2)}, u32[]{:S(2)}) %collective-permute-start.3) | collective-permute-done | bytes 163872 | tf_op jit(solution)/shard_map/ppermute | solution.py:250
  31.1 7.2 %collective-permute-done.2 = bf16[2,2,32,640]{3,2,1,0:T(8,128)(2,1)S(1)} collective-permute-done((bf16[2,2,32,640]{3,2,1,0:T(8,128)(2,1)S(1)}, bf16[2,2,32,640]{3,2,1,0:T(8,128)(2,1)S(1)}, u32[]{:S(2)}, u32[]{:S(2)}) %collective-permute-start.2) | collective-permute-done | bytes 163872 | tf_op jit(solution)/shard_map/ppermute | solution.py:247
  38.3 0.0 collective-permute-done.1
  38.3 0.1 pad_maximum_fusion.whole
  38.3 0.7 %collective-permute-start.4 = (bf16[2,2,128,640]{3,2,1,0:T(8,128)(2,1)S(1)}, bf16[2,2,128,640]{3,2,1,0:T(8,128)(2,1)S(1)}, u32[]{:S(2)}, u32[]{:S(2)}) collective-permute-start(bf16[2,2,128,640]{3,2,1,0:T(8,128)(2,1)S(1)} %pad_maximum_fusion.whole), channel_id=1, source_target_pairs={{0,2},{1,3},{2,0},{3,1},{4,6},{5,7},{6,4},{7,5},{8,10},{9,11},{10,... | collective-permute-start | bytes 1966088 | tf_op jit(solution)/shard_map/ppermute | solution.py:264
  39.1 0.1 collective-permute-start.12
  39.2 0.9 %dynamic-slice_bitcast_fusion.2 = (bf16[2,128,640]{2,1,0:T(8,128)(2,1)}, bf16[2,128,640]{2,1,0:T(8,128)(2,1)}) fusion(bf16[2,2,128,640]{3,2,1,0:T(8,128)(2,1)S(1)} %pad_maximum_fusion.whole, s32[]{:T(128)S(6)} %select_n.46, s32[]{:T(128)S(6)} %select_n.45), kind=kLoop, calls=%fused_computation.4 | loop fusion | bytes 1310728 | tf_op jit(solution)/shard_map/squeeze | solution.py:263
  40.1 0.0 collective-permute-start.6
  40.1 0.0 collective-permute-done.13.far
  40.1 0.0 copy-start
  40.1 0.7 %copy-done = bf16[2,128,640]{2,1,0:T(8,128)(2,1)} copy-done((bf16[2,128,640]{2,1,0:T(8,128)(2,1)}, bf16[2,128,640]{2,1,0:T(8,128)(2,1)S(1)}, u32[]{:S(2)}) %copy-start) | copy-done | bytes 327704
  40.8 1.8 %collective-permute-start.5 = (bf16[2,128,640]{2,1,0:T(8,128)(2,1)}, bf16[2,128,640]{2,1,0:T(8,128)(2,1)S(1)}, u32[]{:S(2)}, u32[]{:S(2)}) collective-permute-start(bf16[2,128,640]{2,1,0:T(8,128)(2,1)} %get-tuple-element.12), channel_id=1, source_target_pairs={{0,1},{1,3},{2,0},{3,2},{4,6},{5,4},{6,7},{7,5},{8,10},{9,8},{10,1... | collective-permute-start | bytes 983048 | tf_op jit(solution)/shard_map/ppermute | solution.py:262
  42.6 0.1 pad_add_fusion.spots
  42.7 4.5 %collective-permute-done.12.near = bf16[2,128,640]{2,1,0:T(8,128)(2,1)} collective-permute-done((bf16[2,128,640]{2,1,0:T(8,128)(2,1)}, bf16[2,128,640]{2,1,0:T(8,128)(2,1)}, u32[]{:S(2)}, u32[]{:S(2)}) %collective-permute-start.12) | collective-permute-done | bytes 327712 | tf_op jit(solution)/shard_map/ppermute | solution.py:262
  47.2 0.0 collective-permute-done.11.theirs
  47.2 0.0 copy-start.1
  47.2 1.0 %copy-done.1 = bf16[2,128,640]{2,1,0:T(8,128)(2,1)S(1)} copy-done((bf16[2,128,640]{2,1,0:T(8,128)(2,1)S(1)}, bf16[2,128,640]{2,1,0:T(8,128)(2,1)}, u32[]{:S(2)}) %copy-start.1) | copy-done | bytes 327704
  48.2 7.9 %products.2.rest_0_ = bf16[2,4,640,2560]{3,2,1,0:T(8,128)(2,1)} custom-call(s32[2]{0:T(128)S(1)} %pad_add_fusion.spots, bf16[2,2,128,640]{3,2,1,0:T(8,128)(2,1)S(1)} %pad_maximum_fusion.1.whole, bf16[2,2,128,640]{3,2,1,0:T(8,128)(2,1)S(1)} %collective-permute-done.11.theirs, bf16[2,128,640]{2,1,0:T(8,128)(2,1)} %collective-permute-done.12.near, ...), custom_call_target="tpu_custom_call" | custom-call | flops 1677721600 | bytes 13107200 | tf_op jit(solution)/shard_map/products/pallas_call | solution.py:183
  56.1 0.0 collective-permute-done.6.far
  56.1 0.0 collective-permute-done.5.near
  56.1 0.0 collective-permute-done.4.theirs
  56.1 8.1 %products.3 = bf16[2,4,640,2560]{3,2,1,0:T(8,128)(2,1)} custom-call(s32[2]{0:T(128)S(1)} %pad_add_fusion.spots, bf16[2,2,128,640]{3,2,1,0:T(8,128)(2,1)S(1)} %pad_maximum_fusion.whole, bf16[2,2,128,640]{3,2,1,0:T(8,128)(2,1)S(1)} %collective-permute-done.4.theirs, ...), custom_call_target="tpu_custom_call", output_to_operand_aliasing={{}: (5, {})} | custom-call | flops 1677721600 | bytes 13107200 | tf_op jit(solution)/shard_map/products/pallas_call | solution.py:183
  (2 shorter events, 0.1 us)
Async XLA Ops:
  4.7 15.1 %collective-permute-start = (bf16[2,4,32,640]{3,2,1,0:T(8,128)(2,1)}, bf16[2,4,32,640]{3,2,1,0:T(8,128)(2,1)S(1)}, u32[]{:S(2)}, u32[]{:S(2)}) collective-permute-start(bf16[2,4,32,640]{3,2,1,0:T(8,128)(2,1)} %get-tuple-element.7), channel_id=1, source_target_pairs={{0,0},{1,2},{2,1},{3,3},{4,4},{5,6},{6,5},{7,7},{8,8},{9,10},{10,9... | collective-permute-start | bytes 983048 | tf_op jit(solution)/shard_map/ppermute | solution.py:256
  9.2 10.6 %collective-permute-start.8 = (bf16[2,2,32,640]{3,2,1,0:T(8,128)(2,1)}, bf16[2,2,32,640]{3,2,1,0:T(8,128)(2,1)S(1)}, u32[]{:S(2)}, u32[]{:S(2)}) collective-permute-start(bf16[2,2,32,640]{3,2,1,0:T(8,128)(2,1)} %get-tuple-element.8), channel_id=1, source_target_pairs={{0,8},{1,10},{2,9},{3,11},{4,12},{5,14},{6,13},{7,15},{8,0},{9,2},... | collective-permute-start | bytes 491528 | tf_op jit(solution)/shard_map/ppermute | solution.py:247
  11.3 12.0 %collective-permute-start.9 = (bf16[2,2,32,640]{3,2,1,0:T(8,128)(2,1)}, bf16[2,2,32,640]{3,2,1,0:T(8,128)(2,1)S(1)}, u32[]{:S(2)}, u32[]{:S(2)}) collective-permute-start(bf16[2,2,32,640]{3,2,1,0:T(8,128)(2,1)} %get-tuple-element.8), channel_id=1, source_target_pairs={{0,2},{1,3},{2,0},{3,1},{4,8},{5,10},{6,9},{7,11},{8,4},{9,6},{10,... | collective-permute-start | bytes 491528 | tf_op jit(solution)/shard_map/ppermute | solution.py:251
  11.3 13.4 %collective-permute-start.7 = (bf16[2,2,32,640]{3,2,1,0:T(8,128)(2,1)}, bf16[2,2,32,640]{3,2,1,0:T(8,128)(2,1)S(1)}, u32[]{:S(2)}, u32[]{:S(2)}) collective-permute-start(bf16[2,2,32,640]{3,2,1,0:T(8,128)(2,1)} %get-tuple-element.8), channel_id=1, source_target_pairs={{0,4},{1,6},{2,5},{3,7},{4,0},{5,2},{6,1},{7,3},{8,12},{9,14},{10,... | collective-permute-start | bytes 491528 | tf_op jit(solution)/shard_map/ppermute | solution.py:248
  19.8 4.8 %collective-permute-start.10 = (bf16[2,2,32,640]{3,2,1,0:T(8,128)(2,1)S(1)}, bf16[2,2,32,640]{3,2,1,0:T(8,128)(2,1)S(1)}, u32[]{:S(2)}, u32[]{:S(2)}) collective-permute-start(bf16[2,2,32,640]{3,2,1,0:T(8,128)(2,1)S(1)} %collective-permute-done.8), channel_id=1, source_target_pairs={{0,4},{1,5},{2,6},{3,7},{4,0},{5,1},{6,2},{7,3},{8,12},{9,13},{10,... | collective-permute-start | bytes 491528 | tf_op jit(solution)/shard_map/ppermute | solution.py:252
  19.8 11.3 %collective-permute-start.3 = (bf16[2,2,32,640]{3,2,1,0:T(8,128)(2,1)S(1)}, bf16[2,2,32,640]{3,2,1,0:T(8,128)(2,1)S(1)}, u32[]{:S(2)}, u32[]{:S(2)}) collective-permute-start(bf16[2,2,32,640]{3,2,1,0:T(8,128)(2,1)S(1)} %get-tuple-element.14), channel_id=1, source_target_pairs={{0,12},{1,13},{2,14},{3,15},{4,8},{5,9},{6,10},{7,11},{8,4},{9,5},... | collective-permute-start | bytes 491528 | tf_op jit(solution)/shard_map/ppermute | solution.py:250
  23.0 15.3 %collective-permute-start.2 = (bf16[2,2,32,640]{3,2,1,0:T(8,128)(2,1)S(1)}, bf16[2,2,32,640]{3,2,1,0:T(8,128)(2,1)S(1)}, u32[]{:S(2)}, u32[]{:S(2)}) collective-permute-start(bf16[2,2,32,640]{3,2,1,0:T(8,128)(2,1)S(1)} %get-tuple-element.14), channel_id=1, source_target_pairs={{0,8},{1,9},{2,10},{3,11},{4,12},{5,13},{6,14},{7,15},{8,0},{9,1},... | collective-permute-start | bytes 491528 | tf_op jit(solution)/shard_map/ppermute | solution.py:247
  23.3 14.9 %collective-permute-start.1 = (bf16[2,2,32,640]{3,2,1,0:T(8,128)(2,1)S(1)}, bf16[2,2,32,640]{3,2,1,0:T(8,128)(2,1)S(1)}, u32[]{:S(2)}, u32[]{:S(2)}) collective-permute-start(bf16[2,2,32,640]{3,2,1,0:T(8,128)(2,1)S(1)} %get-tuple-element.14), channel_id=1, source_target_pairs={{0,4},{1,5},{2,6},{3,7},{4,0},{5,1},{6,2},{7,3},{8,12},{9,13},{10,... | collective-permute-start | bytes 491528 | tf_op jit(solution)/shard_map/ppermute | solution.py:248
  24.7 22.5 %collective-permute-start.11 = (bf16[2,2,128,640]{3,2,1,0:T(8,128)(2,1)S(1)}, bf16[2,2,128,640]{3,2,1,0:T(8,128)(2,1)S(1)}, u32[]{:S(2)}, u32[]{:S(2)}) collective-permute-start(bf16[2,2,128,640]{3,2,1,0:T(8,128)(2,1)S(1)} %pad_maximum_fusion.1.whole), channel_id=1, source_target_pairs={{0,2},{1,3},{2,0},{3,1},{4,6},{5,7},{6,4},{7,5},{8,10},{9,11},{10,... | collective-permute-start | bytes 1966088 | tf_op jit(solution)/shard_map/ppermute | solution.py:264
  25.7 14.4 %collective-permute-start.13 = (bf16[2,128,640]{2,1,0:T(8,128)(2,1)S(1)}, bf16[2,128,640]{2,1,0:T(8,128)(2,1)S(1)}, u32[]{:S(2)}, u32[]{:S(2)}) collective-permute-start(bf16[2,128,640]{2,1,0:T(8,128)(2,1)S(1)} %get-tuple-element.9), channel_id=1, source_target_pairs={{0,3},{1,2},{2,0},{3,1},{4,6},{5,7},{6,5},{7,4},{8,11},{9,10},{10,... | collective-permute-start | bytes 983048 | tf_op jit(solution)/shard_map/ppermute | solution.py:263
  38.3 17.8 %collective-permute-start.4 = (bf16[2,2,128,640]{3,2,1,0:T(8,128)(2,1)S(1)}, bf16[2,2,128,640]{3,2,1,0:T(8,128)(2,1)S(1)}, u32[]{:S(2)}, u32[]{:S(2)}) collective-permute-start(bf16[2,2,128,640]{3,2,1,0:T(8,128)(2,1)S(1)} %pad_maximum_fusion.whole), channel_id=1, source_target_pairs={{0,2},{1,3},{2,0},{3,1},{4,6},{5,7},{6,4},{7,5},{8,10},{9,11},{10,... | collective-permute-start | bytes 1966088 | tf_op jit(solution)/shard_map/ppermute | solution.py:264
  39.1 8.1 %collective-permute-start.12 = (bf16[2,128,640]{2,1,0:T(8,128)(2,1)}, bf16[2,128,640]{2,1,0:T(8,128)(2,1)}, u32[]{:S(2)}, u32[]{:S(2)}) collective-permute-start(bf16[2,128,640]{2,1,0:T(8,128)(2,1)} %get-tuple-element.10), channel_id=1, source_target_pairs={{0,1},{1,3},{2,0},{3,2},{4,6},{5,4},{6,7},{7,5},{8,10},{9,8},{10,1... | collective-permute-start | bytes 983048 | tf_op jit(solution)/shard_map/ppermute | solution.py:262
  40.1 16.0 %collective-permute-start.6 = (bf16[2,128,640]{2,1,0:T(8,128)(2,1)}, bf16[2,128,640]{2,1,0:T(8,128)(2,1)S(1)}, u32[]{:S(2)}, u32[]{:S(2)}) collective-permute-start(bf16[2,128,640]{2,1,0:T(8,128)(2,1)} %get-tuple-element.11), channel_id=1, source_target_pairs={{0,3},{1,2},{2,0},{3,1},{4,6},{5,7},{6,5},{7,4},{8,11},{9,10},{10,... | collective-permute-start | bytes 983048 | tf_op jit(solution)/shard_map/ppermute | solution.py:263
  40.1 0.7 %copy-start = (bf16[2,128,640]{2,1,0:T(8,128)(2,1)}, bf16[2,128,640]{2,1,0:T(8,128)(2,1)S(1)}, u32[]{:S(2)}) copy-start(bf16[2,128,640]{2,1,0:T(8,128)(2,1)S(1)} %collective-permute-done.13.far) | copy-start | bytes 983044
  40.8 15.3 %collective-permute-start.5 = (bf16[2,128,640]{2,1,0:T(8,128)(2,1)}, bf16[2,128,640]{2,1,0:T(8,128)(2,1)S(1)}, u32[]{:S(2)}, u32[]{:S(2)}) collective-permute-start(bf16[2,128,640]{2,1,0:T(8,128)(2,1)} %get-tuple-element.12), channel_id=1, source_target_pairs={{0,1},{1,3},{2,0},{3,2},{4,6},{5,4},{6,7},{7,5},{8,10},{9,8},{10,1... | collective-permute-start | bytes 983048 | tf_op jit(solution)/shard_map/ppermute | solution.py:262
  47.2 1.0 %copy-start.1 = (bf16[2,128,640]{2,1,0:T(8,128)(2,1)S(1)}, bf16[2,128,640]{2,1,0:T(8,128)(2,1)}, u32[]{:S(2)}) copy-start(bf16[2,128,640]{2,1,0:T(8,128)(2,1)} %copy-done) | copy-start | bytes 983044

commit v5 on v4

--- a/solution.py
+++ b/solution.py
@@ -195,8 +195,8 @@
         input_output_aliases=aliases,
         compiler_params=pltpu.CompilerParams(vmem_limit_bytes=VMEM_LIMIT),
         cost_estimate=pl.CostEstimate(
-            flops=8 * per * width * depth * chans,
-            bytes_accessed=8 * per * width * chans,
+            flops=80 * per * width * depth * chans,
+            bytes_accessed=40 * per * width * chans,
             transcendentals=0,
         ),
         name="products",
@@ -253,7 +253,8 @@
         return first, second, jnp.where(inner, middle, passed)
 
     leading, every = spectra(raw_traces, window_offsets, dead_channels, SIZES[0], 2)
-    here_all = lax.ppermute(every, axes, turned(0))
+    opposite = lax.ppermute(every, axes, moves(lambda z, a, b: (z, 1 - a, 1 - b)))
+    here_all = jnp.where(r == c, every, opposite)
     result, late, start = None, None, 0
     for size, forward in zip(SIZES, FORWARD):
         here = here_all[:, start : start + size]

time: 64.6 us -> 62.2 us (0.963)
  the two profiles are of different devices: /device:TPU:1 before, /device:TPU:0 now
where the time goes in v5:
time: 62.2 us; the launch traced here: 61.3 us
  waiting for transfers between devices  25.1 us (40%)
  Pallas kernels  20.7 us (33%)
  starting transfers between devices  13.8 us (22%)
  other arithmetic  1.23 us (2%)
    pallas_call x2, Pallas kernels, products(): pl.pallas_call(functools.partial(products_kernel, scale, start), in_specs...  16.1 us
    ppermute x2, waiting for transfers between devices, share(): second = lax.ppermute(block, axes, move(2))  15.3 us
    ppermute x1, waiting for transfers between devices, share(): passed = lax.ppermute(second, axes, apart(1))  5.35 us
    pallas_call x1, Pallas kernels, spectra(): pl.pallas_call(spectra_kernel, in_specs=[pl.BlockSpec(memory_space=pltpu....  4.68 us
    ppermute x1, waiting for transfers between devices, share(): return (first, second, lax.ppermute(block, axes, move(3)))  4.43 us
    ppermute x2, starting transfers between devices, share(): first = lax.ppermute(block, axes, move(1))  3.31 us
    ppermute x2, starting transfers between devices, share(): second = lax.ppermute(block, axes, move(2))  2.59 us
    ppermute x1, starting transfers between devices, share(): return (first, second, lax.ppermute(block, axes, move(3)))  2.53 us
  transfers between devices with their start and end apart: 14, of which 4 were waited for; matrix products, arithmetic and copies ran while one was open for 2% of the time, Pallas kernels for 13%

profile of v5, /device:TPU:0, one launch (start us, length us, event | category | flops | bytes accessed | tf_op | source)
XLA Modules:
  0.0 61.3 jit_solution(10617222629393672927)
XLA Ops:
  0.0 4.7 %spectra.1 = (bf16[2,2,32,640]{3,2,1,0:T(8,128)(2,1)}, bf16[2,4,32,640]{3,2,1,0:T(8,128)(2,1)}) custom-call(s32[1,16]{1,0:T(1,128)} %bitcast.12, f32[16,256]{1,0:T(8,128)} %constant.44.clone.table_in, s32[1,128]{1,0:T(1,128)} %bitcast.13, bf16[16,144,1280]{2,1,0:T(8,128)(2,1)} %raw_in.1), custom_call_target="tpu_custom_call" | custom-call | flops 94371840 | bytes 5898240 | tf_op jit(solution)/shard_map/spectra/pallas_call | solution.py:95
  4.7 2.4 %collective-permute-start = (bf16[2,4,32,640]{3,2,1,0:T(8,128)(2,1)}, bf16[2,4,32,640]{3,2,1,0:T(8,128)(2,1)S(1)}, u32[]{:S(2)}, u32[]{:S(2)}) collective-permute-start(bf16[2,4,32,640]{3,2,1,0:T(8,128)(2,1)} %get-tuple-element.7), channel_id=1, source_target_pairs={{0,3},{1,2},{2,1},{3,0},{4,7},{5,6},{6,5},{7,4},{8,11},{9,10},{10,... | collective-permute-start | bytes 983048 | tf_op jit(solution)/shard_map/ppermute | solution.py:256
  7.1 2.6 %collective-permute-start.8 = (bf16[2,2,32,640]{3,2,1,0:T(8,128)(2,1)}, bf16[2,2,32,640]{3,2,1,0:T(8,128)(2,1)S(1)}, u32[]{:S(2)}, u32[]{:S(2)}) collective-permute-start(bf16[2,2,32,640]{3,2,1,0:T(8,128)(2,1)} %get-tuple-element.8), channel_id=1, source_target_pairs={{0,8},{1,10},{2,9},{3,11},{4,12},{5,14},{6,13},{7,15},{8,0},{9,2},... | collective-permute-start | bytes 491528 | tf_op jit(solution)/shard_map/ppermute | solution.py:247
  9.7 0.2 collective-permute-start.9
  9.9 1.4 %collective-permute-start.7 = (bf16[2,2,32,640]{3,2,1,0:T(8,128)(2,1)}, bf16[2,2,32,640]{3,2,1,0:T(8,128)(2,1)S(1)}, u32[]{:S(2)}, u32[]{:S(2)}) collective-permute-start(bf16[2,2,32,640]{3,2,1,0:T(8,128)(2,1)} %get-tuple-element.8), channel_id=1, source_target_pairs={{0,4},{1,6},{2,5},{3,7},{4,0},{5,2},{6,1},{7,3},{8,12},{9,14},{10,... | collective-permute-start | bytes 491528 | tf_op jit(solution)/shard_map/ppermute | solution.py:248
  11.3 7.5 %collective-permute-done.8 = bf16[2,2,32,640]{3,2,1,0:T(8,128)(2,1)S(1)} collective-permute-done((bf16[2,2,32,640]{3,2,1,0:T(8,128)(2,1)}, bf16[2,2,32,640]{3,2,1,0:T(8,128)(2,1)S(1)}, u32[]{:S(2)}, u32[]{:S(2)}) %collective-permute-start.8) | collective-permute-done | bytes 163872 | tf_op jit(solution)/shard_map/ppermute | solution.py:247
  18.8 0.4 collective-permute-start.10
  19.2 0.0 collective-permute-done
  19.2 1.0 %broadcast_select_fusion = bf16[2,4,32,640]{3,2,1,0:T(8,128)(2,1)S(1)} fusion(bf16[2,4,32,640]{3,2,1,0:T(8,128)(2,1)} %get-tuple-element.7, bf16[2,4,32,640]{3,2,1,0:T(8,128)(2,1)S(1)} %collective-permute-done, pred[]{:T(512)S(6)} %eq.21), kind=kLoop, calls=%fused_computation.6 | loop fusion | flops 163840 | bytes 983041 | tf_op jit(solution)/shard_map/jit(_where)/select_n | solution.py:257
  20.3 0.0 collective-permute-done.9
  20.3 5.4 %collective-permute-done.10 = bf16[2,2,32,640]{3,2,1,0:T(8,128)(2,1)S(1)} collective-permute-done((bf16[2,2,32,640]{3,2,1,0:T(8,128)(2,1)S(1)}, bf16[2,2,32,640]{3,2,1,0:T(8,128)(2,1)S(1)}, u32[]{:S(2)}, u32[]{:S(2)}) %collective-permute-start.10) | collective-permute-done | bytes 163872 | tf_op jit(solution)/shard_map/ppermute | solution.py:252
  25.6 0.0 collective-permute-done.7
  25.7 0.1 pad_maximum_fusion.1.whole
  25.7 0.1 collective-permute-start.11
  25.8 2.5 %collective-permute-start.3 = (bf16[2,2,32,640]{3,2,1,0:T(8,128)(2,1)S(1)}, bf16[2,2,32,640]{3,2,1,0:T(8,128)(2,1)S(1)}, u32[]{:S(2)}, u32[]{:S(2)}) collective-permute-start(bf16[2,2,32,640]{3,2,1,0:T(8,128)(2,1)S(1)} %get-tuple-element.14), channel_id=1, source_target_pairs={{0,12},{1,13},{2,14},{3,15},{4,8},{5,9},{6,10},{7,11},{8,4},{9,5},... | collective-permute-start | bytes 491528 | tf_op jit(solution)/shard_map/ppermute | solution.py:250
  28.3 0.0 collective-permute-start.2
  28.3 1.9 %collective-permute-start.1 = (bf16[2,2,32,640]{3,2,1,0:T(8,128)(2,1)S(1)}, bf16[2,2,32,640]{3,2,1,0:T(8,128)(2,1)S(1)}, u32[]{:S(2)}, u32[]{:S(2)}) collective-permute-start(bf16[2,2,32,640]{3,2,1,0:T(8,128)(2,1)S(1)} %get-tuple-element.14), channel_id=1, source_target_pairs={{0,4},{1,5},{2,6},{3,7},{4,0},{5,1},{6,2},{7,3},{8,12},{9,13},{10,... | collective-permute-start | bytes 491528 | tf_op jit(solution)/shard_map/ppermute | solution.py:248
  30.3 0.1 dynamic-slice_bitcast_fusion
  30.3 0.1 collective-permute-start.13
  30.4 4.4 %collective-permute-done.3 = bf16[2,2,32,640]{3,2,1,0:T(8,128)(2,1)S(1)} collective-permute-done((bf16[2,2,32,640]{3,2,1,0:T(8,128)(2,1)S(1)}, bf16[2,2,32,640]{3,2,1,0:T(8,128)(2,1)S(1)}, u32[]{:S(2)}, u32[]{:S(2)}) %collective-permute-start.3) | collective-permute-done | bytes 163872 | tf_op jit(solution)/shard_map/ppermute | solution.py:250
  34.8 0.0 collective-permute-start.12
  34.8 0.1 pad_add_fusion.spots
  34.9 7.8 %collective-permute-done.2 = bf16[2,2,32,640]{3,2,1,0:T(8,128)(2,1)S(1)} collective-permute-done((bf16[2,2,32,640]{3,2,1,0:T(8,128)(2,1)S(1)}, bf16[2,2,32,640]{3,2,1,0:T(8,128)(2,1)S(1)}, u32[]{:S(2)}, u32[]{:S(2)}) %collective-permute-start.2) | collective-permute-done | bytes 163872 | tf_op jit(solution)/shard_map/ppermute | solution.py:247
  42.7 0.0 collective-permute-done.1
  42.7 0.1 pad_maximum_fusion.whole
  42.7 0.1 collective-permute-start.4
  42.8 0.1 dynamic-slice_bitcast_fusion.2
  42.9 0.6 collective-permute-start.6
  43.5 0.0 collective-permute-done.13.far
  43.5 1.6 %collective-permute-start.5 = (bf16[2,128,640]{2,1,0:T(8,128)(2,1)S(1)}, bf16[2,128,640]{2,1,0:T(8,128)(2,1)S(1)}, u32[]{:S(2)}, u32[]{:S(2)}) collective-permute-start(bf16[2,128,640]{2,1,0:T(8,128)(2,1)S(1)} %get-tuple-element.12), channel_id=1, source_target_pairs={{0,1},{1,3},{2,0},{3,2},{4,6},{5,4},{6,7},{7,5},{8,10},{9,8},{10,1... | collective-permute-start | bytes 983048 | tf_op jit(solution)/shard_map/ppermute | solution.py:263
  45.1 0.0 collective-permute-done.12.near
  45.1 0.0 collective-permute-done.11.theirs
  45.1 7.9 %products.2.rest_0_ = bf16[2,4,640,2560]{3,2,1,0:T(8,128)(2,1)} custom-call(s32[2]{0:T(128)S(1)} %pad_add_fusion.spots, bf16[2,2,128,640]{3,2,1,0:T(8,128)(2,1)S(1)} %pad_maximum_fusion.1.whole, bf16[2,2,128,640]{3,2,1,0:T(8,128)(2,1)S(1)} %collective-permute-done.11.theirs, bf16[2,128,640]{2,1,0:T(8,128)(2,1)S(1)} %collective-permute-done.12.near, ...), custom_call_target="tpu_custom_call" | custom-call | flops 16777216000 | bytes 65536000 | tf_op jit(solution)/shard_map/products/pallas_call | solution.py:183
  53.0 0.0 collective-permute-done.6.far
  53.0 0.0 collective-permute-done.5.near
  53.0 0.0 collective-permute-done.4.theirs
  53.0 8.1 %products.3 = bf16[2,4,640,2560]{3,2,1,0:T(8,128)(2,1)} custom-call(s32[2]{0:T(128)S(1)} %pad_add_fusion.spots, bf16[2,2,128,640]{3,2,1,0:T(8,128)(2,1)S(1)} %pad_maximum_fusion.whole, bf16[2,2,128,640]{3,2,1,0:T(8,128)(2,1)S(1)} %collective-permute-done.4.theirs, ...), custom_call_target="tpu_custom_call", output_to_operand_aliasing={{}: (5, {})} | custom-call | flops 16777216000 | bytes 65536000 | tf_op jit(solution)/shard_map/products/pallas_call | solution.py:183
  (2 shorter events, 0.1 us)
Async XLA Ops:
  4.7 14.5 %collective-permute-start = (bf16[2,4,32,640]{3,2,1,0:T(8,128)(2,1)}, bf16[2,4,32,640]{3,2,1,0:T(8,128)(2,1)S(1)}, u32[]{:S(2)}, u32[]{:S(2)}) collective-permute-start(bf16[2,4,32,640]{3,2,1,0:T(8,128)(2,1)} %get-tuple-element.7), channel_id=1, source_target_pairs={{0,3},{1,2},{2,1},{3,0},{4,7},{5,6},{6,5},{7,4},{8,11},{9,10},{10,... | collective-permute-start | bytes 983048 | tf_op jit(solution)/shard_map/ppermute | solution.py:256
  7.1 11.6 %collective-permute-start.8 = (bf16[2,2,32,640]{3,2,1,0:T(8,128)(2,1)}, bf16[2,2,32,640]{3,2,1,0:T(8,128)(2,1)S(1)}, u32[]{:S(2)}, u32[]{:S(2)}) collective-permute-start(bf16[2,2,32,640]{3,2,1,0:T(8,128)(2,1)} %get-tuple-element.8), channel_id=1, source_target_pairs={{0,8},{1,10},{2,9},{3,11},{4,12},{5,14},{6,13},{7,15},{8,0},{9,2},... | collective-permute-start | bytes 491528 | tf_op jit(solution)/shard_map/ppermute | solution.py:247
  9.7 10.5 %collective-permute-start.9 = (bf16[2,2,32,640]{3,2,1,0:T(8,128)(2,1)}, bf16[2,2,32,640]{3,2,1,0:T(8,128)(2,1)S(1)}, u32[]{:S(2)}, u32[]{:S(2)}) collective-permute-start(bf16[2,2,32,640]{3,2,1,0:T(8,128)(2,1)} %get-tuple-element.8), channel_id=1, source_target_pairs={{0,2},{1,3},{2,0},{3,1},{4,8},{5,10},{6,9},{7,11},{8,4},{9,6},{10,... | collective-permute-start | bytes 491528 | tf_op jit(solution)/shard_map/ppermute | solution.py:251
  9.9 15.7 %collective-permute-start.7 = (bf16[2,2,32,640]{3,2,1,0:T(8,128)(2,1)}, bf16[2,2,32,640]{3,2,1,0:T(8,128)(2,1)S(1)}, u32[]{:S(2)}, u32[]{:S(2)}) collective-permute-start(bf16[2,2,32,640]{3,2,1,0:T(8,128)(2,1)} %get-tuple-element.8), channel_id=1, source_target_pairs={{0,4},{1,6},{2,5},{3,7},{4,0},{5,2},{6,1},{7,3},{8,12},{9,14},{10,... | collective-permute-start | bytes 491528 | tf_op jit(solution)/shard_map/ppermute | solution.py:248
  18.8 6.8 %collective-permute-start.10 = (bf16[2,2,32,640]{3,2,1,0:T(8,128)(2,1)S(1)}, bf16[2,2,32,640]{3,2,1,0:T(8,128)(2,1)S(1)}, u32[]{:S(2)}, u32[]{:S(2)}) collective-permute-start(bf16[2,2,32,640]{3,2,1,0:T(8,128)(2,1)S(1)} %collective-permute-done.8), channel_id=1, source_target_pairs={{0,4},{1,5},{2,6},{3,7},{4,0},{5,1},{6,2},{7,3},{8,12},{9,13},{10,... | collective-permute-start | bytes 491528 | tf_op jit(solution)/shard_map/ppermute | solution.py:252
  25.7 19.3 %collective-permute-start.11 = (bf16[2,2,128,640]{3,2,1,0:T(8,128)(2,1)S(1)}, bf16[2,2,128,640]{3,2,1,0:T(8,128)(2,1)S(1)}, u32[]{:S(2)}, u32[]{:S(2)}) collective-permute-start(bf16[2,2,128,640]{3,2,1,0:T(8,128)(2,1)S(1)} %pad_maximum_fusion.1.whole), channel_id=1, source_target_pairs={{0,2},{1,3},{2,0},{3,1},{4,6},{5,7},{6,4},{7,5},{8,10},{9,11},{10,... | collective-permute-start | bytes 1966088 | tf_op jit(solution)/shard_map/ppermute | solution.py:265
  25.8 9.0 %collective-permute-start.3 = (bf16[2,2,32,640]{3,2,1,0:T(8,128)(2,1)S(1)}, bf16[2,2,32,640]{3,2,1,0:T(8,128)(2,1)S(1)}, u32[]{:S(2)}, u32[]{:S(2)}) collective-permute-start(bf16[2,2,32,640]{3,2,1,0:T(8,128)(2,1)S(1)} %get-tuple-element.14), channel_id=1, source_target_pairs={{0,12},{1,13},{2,14},{3,15},{4,8},{5,9},{6,10},{7,11},{8,4},{9,5},... | collective-permute-start | bytes 491528 | tf_op jit(solution)/shard_map/ppermute | solution.py:250
  28.3 14.3 %collective-permute-start.2 = (bf16[2,2,32,640]{3,2,1,0:T(8,128)(2,1)S(1)}, bf16[2,2,32,640]{3,2,1,0:T(8,128)(2,1)S(1)}, u32[]{:S(2)}, u32[]{:S(2)}) collective-permute-start(bf16[2,2,32,640]{3,2,1,0:T(8,128)(2,1)S(1)} %get-tuple-element.14), channel_id=1, source_target_pairs={{0,8},{1,9},{2,10},{3,11},{4,12},{5,13},{6,14},{7,15},{8,0},{9,1},... | collective-permute-start | bytes 491528 | tf_op jit(solution)/shard_map/ppermute | solution.py:247
  28.3 14.3 %collective-permute-start.1 = (bf16[2,2,32,640]{3,2,1,0:T(8,128)(2,1)S(1)}, bf16[2,2,32,640]{3,2,1,0:T(8,128)(2,1)S(1)}, u32[]{:S(2)}, u32[]{:S(2)}) collective-permute-start(bf16[2,2,32,640]{3,2,1,0:T(8,128)(2,1)S(1)} %get-tuple-element.14), channel_id=1, source_target_pairs={{0,4},{1,5},{2,6},{3,7},{4,0},{5,1},{6,2},{7,3},{8,12},{9,13},{10,... | collective-permute-start | bytes 491528 | tf_op jit(solution)/shard_map/ppermute | solution.py:248
  30.3 13.2 %collective-permute-start.13 = (bf16[2,128,640]{2,1,0:T(8,128)(2,1)S(1)}, bf16[2,128,640]{2,1,0:T(8,128)(2,1)S(1)}, u32[]{:S(2)}, u32[]{:S(2)}) collective-permute-start(bf16[2,128,640]{2,1,0:T(8,128)(2,1)S(1)} %get-tuple-element.9), channel_id=1, source_target_pairs={{0,3},{1,2},{2,0},{3,1},{4,6},{5,7},{6,5},{7,4},{8,11},{9,10},{10,... | collective-permute-start | bytes 983048 | tf_op jit(solution)/shard_map/ppermute | solution.py:264
  34.8 10.3 %collective-permute-start.12 = (bf16[2,128,640]{2,1,0:T(8,128)(2,1)S(1)}, bf16[2,128,640]{2,1,0:T(8,128)(2,1)S(1)}, u32[]{:S(2)}, u32[]{:S(2)}) collective-permute-start(bf16[2,128,640]{2,1,0:T(8,128)(2,1)S(1)} %get-tuple-element.10), channel_id=1, source_target_pairs={{0,1},{1,3},{2,0},{3,2},{4,6},{5,4},{6,7},{7,5},{8,10},{9,8},{10,1... | collective-permute-start | bytes 983048 | tf_op jit(solution)/shard_map/ppermute | solution.py:263
  42.7 10.3 %collective-permute-start.4 = (bf16[2,2,128,640]{3,2,1,0:T(8,128)(2,1)S(1)}, bf16[2,2,128,640]{3,2,1,0:T(8,128)(2,1)S(1)}, u32[]{:S(2)}, u32[]{:S(2)}) collective-permute-start(bf16[2,2,128,640]{3,2,1,0:T(8,128)(2,1)S(1)} %pad_maximum_fusion.whole), channel_id=1, source_target_pairs={{0,2},{1,3},{2,0},{3,1},{4,6},{5,7},{6,4},{7,5},{8,10},{9,11},{10,... | collective-permute-start | bytes 1966088 | tf_op jit(solution)/shard_map/ppermute | solution.py:265
  42.9 10.1 %collective-permute-start.6 = (bf16[2,128,640]{2,1,0:T(8,128)(2,1)S(1)}, bf16[2,128,640]{2,1,0:T(8,128)(2,1)S(1)}, u32[]{:S(2)}, u32[]{:S(2)}) collective-permute-start(bf16[2,128,640]{2,1,0:T(8,128)(2,1)S(1)} %get-tuple-element.11), channel_id=1, source_target_pairs={{0,3},{1,2},{2,0},{3,1},{4,6},{5,7},{6,5},{7,4},{8,11},{9,10},{10,... | collective-permute-start | bytes 983048 | tf_op jit(solution)/shard_map/ppermute | solution.py:264
  43.5 9.5 %collective-permute-start.5 = (bf16[2,128,640]{2,1,0:T(8,128)(2,1)S(1)}, bf16[2,128,640]{2,1,0:T(8,128)(2,1)S(1)}, u32[]{:S(2)}, u32[]{:S(2)}) collective-permute-start(bf16[2,128,640]{2,1,0:T(8,128)(2,1)S(1)} %get-tuple-element.12), channel_id=1, source_target_pairs={{0,1},{1,3},{2,0},{3,2},{4,6},{5,4},{6,7},{7,5},{8,10},{9,8},{10,1... | collective-permute-start | bytes 983048 | tf_op jit(solution)/shard_map/ppermute | solution.py:263

commit v6 on v5

--- a/solution.py
+++ b/solution.py
@@ -173,7 +173,7 @@
     slots = per * 2 * splits
     in_specs = [pl.BlockSpec(memory_space=pltpu.SMEM)]
     in_specs += [pl.BlockSpec(memory_space=pltpu.VMEM)] * 2
-    in_specs += [pl.BlockSpec(memory_space=pl.ANY)] * 2
+    in_specs += [pl.BlockSpec(memory_space=pltpu.HBM)] * 2
     args = [spots, whole, theirs, near, far]
     aliases = {}
     if target is not None:

time: 62.2 us -> 62.2 us (level)
  no operation moved by 1% of the time
where the time goes in v6:
time: 62.2 us; the launch traced here: 61.3 us
  waiting for transfers between devices  25.1 us (40%)
  Pallas kernels  20.7 us (33%)
  starting transfers between devices  13.8 us (22%)
  other arithmetic  1.23 us (2%)
    pallas_call x2, Pallas kernels, products(): pl.pallas_call(functools.partial(products_kernel, scale, start), in_specs...  16.1 us
    ppermute x2, waiting for transfers between devices, share(): second = lax.ppermute(block, axes, move(2))  15.3 us
    ppermute x1, waiting for transfers between devices, share(): passed = lax.ppermute(second, axes, apart(1))  5.35 us
    pallas_call x1, Pallas kernels, spectra(): pl.pallas_call(spectra_kernel, in_specs=[pl.BlockSpec(memory_space=pltpu....  4.68 us
    ppermute x1, waiting for transfers between devices, share(): return (first, second, lax.ppermute(block, axes, move(3)))  4.43 us
    ppermute x2, starting transfers between devices, share(): first = lax.ppermute(block, axes, move(1))  3.31 us
    ppermute x2, starting transfers between devices, share(): second = lax.ppermute(block, axes, move(2))  2.59 us
    ppermute x1, starting transfers between devices, share(): return (first, second, lax.ppermute(block, axes, move(3)))  2.53 us
  transfers between devices with their start and end apart: 14, of which 4 were waited for; matrix products, arithmetic and copies ran while one was open for 2% of the time, Pallas kernels for 13%

profile of v6, /device:TPU:0, one launch (start us, length us, event | category | flops | bytes accessed | tf_op | source)
XLA Modules:
  0.0 61.3 jit_solution(10617222629393672927)
XLA Ops:
  0.0 4.7 %spectra.1 = (bf16[2,2,32,640]{3,2,1,0:T(8,128)(2,1)}, bf16[2,4,32,640]{3,2,1,0:T(8,128)(2,1)}) custom-call(s32[1,16]{1,0:T(1,128)} %bitcast.12, f32[16,256]{1,0:T(8,128)} %constant.44.clone.table_in, s32[1,128]{1,0:T(1,128)} %bitcast.13, bf16[16,144,1280]{2,1,0:T(8,128)(2,1)} %raw_in.1), custom_call_target="tpu_custom_call" | custom-call | flops 94371840 | bytes 5898240 | tf_op jit(solution)/shard_map/spectra/pallas_call | solution.py:95
  4.7 2.4 %collective-permute-start = (bf16[2,4,32,640]{3,2,1,0:T(8,128)(2,1)}, bf16[2,4,32,640]{3,2,1,0:T(8,128)(2,1)S(1)}, u32[]{:S(2)}, u32[]{:S(2)}) collective-permute-start(bf16[2,4,32,640]{3,2,1,0:T(8,128)(2,1)} %get-tuple-element.7), channel_id=1, source_target_pairs={{0,3},{1,2},{2,1},{3,0},{4,7},{5,6},{6,5},{7,4},{8,11},{9,10},{10,... | collective-permute-start | bytes 983048 | tf_op jit(solution)/shard_map/ppermute | solution.py:256
  7.1 2.6 %collective-permute-start.8 = (bf16[2,2,32,640]{3,2,1,0:T(8,128)(2,1)}, bf16[2,2,32,640]{3,2,1,0:T(8,128)(2,1)S(1)}, u32[]{:S(2)}, u32[]{:S(2)}) collective-permute-start(bf16[2,2,32,640]{3,2,1,0:T(8,128)(2,1)} %get-tuple-element.8), channel_id=1, source_target_pairs={{0,8},{1,10},{2,9},{3,11},{4,12},{5,14},{6,13},{7,15},{8,0},{9,2},... | collective-permute-start | bytes 491528 | tf_op jit(solution)/shard_map/ppermute | solution.py:247
  9.7 0.2 collective-permute-start.9
  9.9 1.4 %collective-permute-start.7 = (bf16[2,2,32,640]{3,2,1,0:T(8,128)(2,1)}, bf16[2,2,32,640]{3,2,1,0:T(8,128)(2,1)S(1)}, u32[]{:S(2)}, u32[]{:S(2)}) collective-permute-start(bf16[2,2,32,640]{3,2,1,0:T(8,128)(2,1)} %get-tuple-element.8), channel_id=1, source_target_pairs={{0,4},{1,6},{2,5},{3,7},{4,0},{5,2},{6,1},{7,3},{8,12},{9,14},{10,... | collective-permute-start | bytes 491528 | tf_op jit(solution)/shard_map/ppermute | solution.py:248
  11.3 7.5 %collective-permute-done.8 = bf16[2,2,32,640]{3,2,1,0:T(8,128)(2,1)S(1)} collective-permute-done((bf16[2,2,32,640]{3,2,1,0:T(8,128)(2,1)}, bf16[2,2,32,640]{3,2,1,0:T(8,128)(2,1)S(1)}, u32[]{:S(2)}, u32[]{:S(2)}) %collective-permute-start.8) | collective-permute-done | bytes 163872 | tf_op jit(solution)/shard_map/ppermute | solution.py:247
  18.8 0.4 collective-permute-start.10
  19.2 0.0 collective-permute-done
  19.2 1.0 %broadcast_select_fusion = bf16[2,4,32,640]{3,2,1,0:T(8,128)(2,1)S(1)} fusion(bf16[2,4,32,640]{3,2,1,0:T(8,128)(2,1)} %get-tuple-element.7, bf16[2,4,32,640]{3,2,1,0:T(8,128)(2,1)S(1)} %collective-permute-done, pred[]{:T(512)S(6)} %eq.21), kind=kLoop, calls=%fused_computation.6 | loop fusion | flops 163840 | bytes 983041 | tf_op jit(solution)/shard_map/jit(_where)/select_n | solution.py:257
  20.3 0.0 collective-permute-done.9
  20.3 5.4 %collective-permute-done.10 = bf16[2,2,32,640]{3,2,1,0:T(8,128)(2,1)S(1)} collective-permute-done((bf16[2,2,32,640]{3,2,1,0:T(8,128)(2,1)S(1)}, bf16[2,2,32,640]{3,2,1,0:T(8,128)(2,1)S(1)}, u32[]{:S(2)}, u32[]{:S(2)}) %collective-permute-start.10) | collective-permute-done | bytes 163872 | tf_op jit(solution)/shard_map/ppermute | solution.py:252
  25.6 0.0 collective-permute-done.7
  25.7 0.1 pad_maximum_fusion.1.whole
  25.7 0.1 collective-permute-start.11
  25.8 2.5 %collective-permute-start.3 = (bf16[2,2,32,640]{3,2,1,0:T(8,128)(2,1)S(1)}, bf16[2,2,32,640]{3,2,1,0:T(8,128)(2,1)S(1)}, u32[]{:S(2)}, u32[]{:S(2)}) collective-permute-start(bf16[2,2,32,640]{3,2,1,0:T(8,128)(2,1)S(1)} %get-tuple-element.14), channel_id=1, source_target_pairs={{0,12},{1,13},{2,14},{3,15},{4,8},{5,9},{6,10},{7,11},{8,4},{9,5},... | collective-permute-start | bytes 491528 | tf_op jit(solution)/shard_map/ppermute | solution.py:250
  28.3 0.0 collective-permute-start.2
  28.3 1.9 %collective-permute-start.1 = (bf16[2,2,32,640]{3,2,1,0:T(8,128)(2,1)S(1)}, bf16[2,2,32,640]{3,2,1,0:T(8,128)(2,1)S(1)}, u32[]{:S(2)}, u32[]{:S(2)}) collective-permute-start(bf16[2,2,32,640]{3,2,1,0:T(8,128)(2,1)S(1)} %get-tuple-element.14), channel_id=1, source_target_pairs={{0,4},{1,5},{2,6},{3,7},{4,0},{5,1},{6,2},{7,3},{8,12},{9,13},{10,... | collective-permute-start | bytes 491528 | tf_op jit(solution)/shard_map/ppermute | solution.py:248
  30.3 0.1 dynamic-slice_bitcast_fusion
  30.3 0.1 collective-permute-start.13
  30.4 4.4 %collective-permute-done.3 = bf16[2,2,32,640]{3,2,1,0:T(8,128)(2,1)S(1)} collective-permute-done((bf16[2,2,32,640]{3,2,1,0:T(8,128)(2,1)S(1)}, bf16[2,2,32,640]{3,2,1,0:T(8,128)(2,1)S(1)}, u32[]{:S(2)}, u32[]{:S(2)}) %collective-permute-start.3) | collective-permute-done | bytes 163872 | tf_op jit(solution)/shard_map/ppermute | solution.py:250
  34.8 0.0 collective-permute-start.12
  34.8 0.1 pad_add_fusion.spots
  34.9 7.8 %collective-permute-done.2 = bf16[2,2,32,640]{3,2,1,0:T(8,128)(2,1)S(1)} collective-permute-done((bf16[2,2,32,640]{3,2,1,0:T(8,128)(2,1)S(1)}, bf16[2,2,32,640]{3,2,1,0:T(8,128)(2,1)S(1)}, u32[]{:S(2)}, u32[]{:S(2)}) %collective-permute-start.2) | collective-permute-done | bytes 163872 | tf_op jit(solution)/shard_map/ppermute | solution.py:247
  42.7 0.0 collective-permute-done.1
  42.7 0.1 pad_maximum_fusion.whole
  42.7 0.1 collective-permute-start.4
  42.8 0.1 dynamic-slice_bitcast_fusion.2
  42.9 0.6 collective-permute-start.6
  43.5 0.0 collective-permute-done.13.far
  43.5 1.6 %collective-permute-start.5 = (bf16[2,128,640]{2,1,0:T(8,128)(2,1)S(1)}, bf16[2,128,640]{2,1,0:T(8,128)(2,1)S(1)}, u32[]{:S(2)}, u32[]{:S(2)}) collective-permute-start(bf16[2,128,640]{2,1,0:T(8,128)(2,1)S(1)} %get-tuple-element.12), channel_id=1, source_target_pairs={{0,1},{1,3},{2,0},{3,2},{4,6},{5,4},{6,7},{7,5},{8,10},{9,8},{10,1... | collective-permute-start | bytes 983048 | tf_op jit(solution)/shard_map/ppermute | solution.py:263
  45.1 0.0 collective-permute-done.12.near
  45.1 0.0 collective-permute-done.11.theirs
  45.1 7.9 %products.2.rest_0_ = bf16[2,4,640,2560]{3,2,1,0:T(8,128)(2,1)} custom-call(s32[2]{0:T(128)S(1)} %pad_add_fusion.spots, bf16[2,2,128,640]{3,2,1,0:T(8,128)(2,1)S(1)} %pad_maximum_fusion.1.whole, bf16[2,2,128,640]{3,2,1,0:T(8,128)(2,1)S(1)} %collective-permute-done.11.theirs, bf16[2,128,640]{2,1,0:T(8,128)(2,1)S(1)} %collective-permute-done.12.near, ...), custom_call_target="tpu_custom_call" | custom-call | flops 16777216000 | bytes 65536000 | tf_op jit(solution)/shard_map/products/pallas_call | solution.py:183
  53.0 0.0 collective-permute-done.6.far
  53.0 0.0 collective-permute-done.5.near
  53.0 0.0 collective-permute-done.4.theirs
  53.0 8.1 %products.3 = bf16[2,4,640,2560]{3,2,1,0:T(8,128)(2,1)} custom-call(s32[2]{0:T(128)S(1)} %pad_add_fusion.spots, bf16[2,2,128,640]{3,2,1,0:T(8,128)(2,1)S(1)} %pad_maximum_fusion.whole, bf16[2,2,128,640]{3,2,1,0:T(8,128)(2,1)S(1)} %collective-permute-done.4.theirs, ...), custom_call_target="tpu_custom_call", output_to_operand_aliasing={{}: (5, {})} | custom-call | flops 16777216000 | bytes 65536000 | tf_op jit(solution)/shard_map/products/pallas_call | solution.py:183
  (2 shorter events, 0.1 us)
Async XLA Ops:
  4.7 14.5 %collective-permute-start = (bf16[2,4,32,640]{3,2,1,0:T(8,128)(2,1)}, bf16[2,4,32,640]{3,2,1,0:T(8,128)(2,1)S(1)}, u32[]{:S(2)}, u32[]{:S(2)}) collective-permute-start(bf16[2,4,32,640]{3,2,1,0:T(8,128)(2,1)} %get-tuple-element.7), channel_id=1, source_target_pairs={{0,3},{1,2},{2,1},{3,0},{4,7},{5,6},{6,5},{7,4},{8,11},{9,10},{10,... | collective-permute-start | bytes 983048 | tf_op jit(solution)/shard_map/ppermute | solution.py:256
  7.1 11.6 %collective-permute-start.8 = (bf16[2,2,32,640]{3,2,1,0:T(8,128)(2,1)}, bf16[2,2,32,640]{3,2,1,0:T(8,128)(2,1)S(1)}, u32[]{:S(2)}, u32[]{:S(2)}) collective-permute-start(bf16[2,2,32,640]{3,2,1,0:T(8,128)(2,1)} %get-tuple-element.8), channel_id=1, source_target_pairs={{0,8},{1,10},{2,9},{3,11},{4,12},{5,14},{6,13},{7,15},{8,0},{9,2},... | collective-permute-start | bytes 491528 | tf_op jit(solution)/shard_map/ppermute | solution.py:247
  9.7 10.5 %collective-permute-start.9 = (bf16[2,2,32,640]{3,2,1,0:T(8,128)(2,1)}, bf16[2,2,32,640]{3,2,1,0:T(8,128)(2,1)S(1)}, u32[]{:S(2)}, u32[]{:S(2)}) collective-permute-start(bf16[2,2,32,640]{3,2,1,0:T(8,128)(2,1)} %get-tuple-element.8), channel_id=1, source_target_pairs={{0,2},{1,3},{2,0},{3,1},{4,8},{5,10},{6,9},{7,11},{8,4},{9,6},{10,... | collective-permute-start | bytes 491528 | tf_op jit(solution)/shard_map/ppermute | solution.py:251
  9.9 15.7 %collective-permute-start.7 = (bf16[2,2,32,640]{3,2,1,0:T(8,128)(2,1)}, bf16[2,2,32,640]{3,2,1,0:T(8,128)(2,1)S(1)}, u32[]{:S(2)}, u32[]{:S(2)}) collective-permute-start(bf16[2,2,32,640]{3,2,1,0:T(8,128)(2,1)} %get-tuple-element.8), channel_id=1, source_target_pairs={{0,4},{1,6},{2,5},{3,7},{4,0},{5,2},{6,1},{7,3},{8,12},{9,14},{10,... | collective-permute-start | bytes 491528 | tf_op jit(solution)/shard_map/ppermute | solution.py:248
  18.8 6.8 %collective-permute-start.10 = (bf16[2,2,32,640]{3,2,1,0:T(8,128)(2,1)S(1)}, bf16[2,2,32,640]{3,2,1,0:T(8,128)(2,1)S(1)}, u32[]{:S(2)}, u32[]{:S(2)}) collective-permute-start(bf16[2,2,32,640]{3,2,1,0:T(8,128)(2,1)S(1)} %collective-permute-done.8), channel_id=1, source_target_pairs={{0,4},{1,5},{2,6},{3,7},{4,0},{5,1},{6,2},{7,3},{8,12},{9,13},{10,... | collective-permute-start | bytes 491528 | tf_op jit(solution)/shard_map/ppermute | solution.py:252
  25.7 19.3 %collective-permute-start.11 = (bf16[2,2,128,640]{3,2,1,0:T(8,128)(2,1)S(1)}, bf16[2,2,128,640]{3,2,1,0:T(8,128)(2,1)S(1)}, u32[]{:S(2)}, u32[]{:S(2)}) collective-permute-start(bf16[2,2,128,640]{3,2,1,0:T(8,128)(2,1)S(1)} %pad_maximum_fusion.1.whole), channel_id=1, source_target_pairs={{0,2},{1,3},{2,0},{3,1},{4,6},{5,7},{6,4},{7,5},{8,10},{9,11},{10,... | collective-permute-start | bytes 1966088 | tf_op jit(solution)/shard_map/ppermute | solution.py:265
  25.8 9.0 %collective-permute-start.3 = (bf16[2,2,32,640]{3,2,1,0:T(8,128)(2,1)S(1)}, bf16[2,2,32,640]{3,2,1,0:T(8,128)(2,1)S(1)}, u32[]{:S(2)}, u32[]{:S(2)}) collective-permute-start(bf16[2,2,32,640]{3,2,1,0:T(8,128)(2,1)S(1)} %get-tuple-element.14), channel_id=1, source_target_pairs={{0,12},{1,13},{2,14},{3,15},{4,8},{5,9},{6,10},{7,11},{8,4},{9,5},... | collective-permute-start | bytes 491528 | tf_op jit(solution)/shard_map/ppermute | solution.py:250
  28.3 14.3 %collective-permute-start.2 = (bf16[2,2,32,640]{3,2,1,0:T(8,128)(2,1)S(1)}, bf16[2,2,32,640]{3,2,1,0:T(8,128)(2,1)S(1)}, u32[]{:S(2)}, u32[]{:S(2)}) collective-permute-start(bf16[2,2,32,640]{3,2,1,0:T(8,128)(2,1)S(1)} %get-tuple-element.14), channel_id=1, source_target_pairs={{0,8},{1,9},{2,10},{3,11},{4,12},{5,13},{6,14},{7,15},{8,0},{9,1},... | collective-permute-start | bytes 491528 | tf_op jit(solution)/shard_map/ppermute | solution.py:247
  28.3 14.3 %collective-permute-start.1 = (bf16[2,2,32,640]{3,2,1,0:T(8,128)(2,1)S(1)}, bf16[2,2,32,640]{3,2,1,0:T(8,128)(2,1)S(1)}, u32[]{:S(2)}, u32[]{:S(2)}) collective-permute-start(bf16[2,2,32,640]{3,2,1,0:T(8,128)(2,1)S(1)} %get-tuple-element.14), channel_id=1, source_target_pairs={{0,4},{1,5},{2,6},{3,7},{4,0},{5,1},{6,2},{7,3},{8,12},{9,13},{10,... | collective-permute-start | bytes 491528 | tf_op jit(solution)/shard_map/ppermute | solution.py:248
  30.3 13.2 %collective-permute-start.13 = (bf16[2,128,640]{2,1,0:T(8,128)(2,1)S(1)}, bf16[2,128,640]{2,1,0:T(8,128)(2,1)S(1)}, u32[]{:S(2)}, u32[]{:S(2)}) collective-permute-start(bf16[2,128,640]{2,1,0:T(8,128)(2,1)S(1)} %get-tuple-element.9), channel_id=1, source_target_pairs={{0,3},{1,2},{2,0},{3,1},{4,6},{5,7},{6,5},{7,4},{8,11},{9,10},{10,... | collective-permute-start | bytes 983048 | tf_op jit(solution)/shard_map/ppermute | solution.py:264
  34.8 10.3 %collective-permute-start.12 = (bf16[2,128,640]{2,1,0:T(8,128)(2,1)S(1)}, bf16[2,128,640]{2,1,0:T(8,128)(2,1)S(1)}, u32[]{:S(2)}, u32[]{:S(2)}) collective-permute-start(bf16[2,128,640]{2,1,0:T(8,128)(2,1)S(1)} %get-tuple-element.10), channel_id=1, source_target_pairs={{0,1},{1,3},{2,0},{3,2},{4,6},{5,4},{6,7},{7,5},{8,10},{9,8},{10,1... | collective-permute-start | bytes 983048 | tf_op jit(solution)/shard_map/ppermute | solution.py:263
  42.7 10.3 %collective-permute-start.4 = (bf16[2,2,128,640]{3,2,1,0:T(8,128)(2,1)S(1)}, bf16[2,2,128,640]{3,2,1,0:T(8,128)(2,1)S(1)}, u32[]{:S(2)}, u32[]{:S(2)}) collective-permute-start(bf16[2,2,128,640]{3,2,1,0:T(8,128)(2,1)S(1)} %pad_maximum_fusion.whole), channel_id=1, source_target_pairs={{0,2},{1,3},{2,0},{3,1},{4,6},{5,7},{6,4},{7,5},{8,10},{9,11},{10,... | collective-permute-start | bytes 1966088 | tf_op jit(solution)/shard_map/ppermute | solution.py:265
  42.9 10.1 %collective-permute-start.6 = (bf16[2,128,640]{2,1,0:T(8,128)(2,1)S(1)}, bf16[2,128,640]{2,1,0:T(8,128)(2,1)S(1)}, u32[]{:S(2)}, u32[]{:S(2)}) collective-permute-start(bf16[2,128,640]{2,1,0:T(8,128)(2,1)S(1)} %get-tuple-element.11), channel_id=1, source_target_pairs={{0,3},{1,2},{2,0},{3,1},{4,6},{5,7},{6,5},{7,4},{8,11},{9,10},{10,... | collective-permute-start | bytes 983048 | tf_op jit(solution)/shard_map/ppermute | solution.py:264
  43.5 9.5 %collective-permute-start.5 = (bf16[2,128,640]{2,1,0:T(8,128)(2,1)S(1)}, bf16[2,128,640]{2,1,0:T(8,128)(2,1)S(1)}, u32[]{:S(2)}, u32[]{:S(2)}) collective-permute-start(bf16[2,128,640]{2,1,0:T(8,128)(2,1)S(1)} %get-tuple-element.12), channel_id=1, source_target_pairs={{0,1},{1,3},{2,0},{3,2},{4,6},{5,4},{6,7},{7,5},{8,10},{9,8},{10,1... | collective-permute-start | bytes 983048 | tf_op jit(solution)/shard_map/ppermute | solution.py:263
